TPU v7x, 32 devices: a whole 2x2x4 slice. The times are simulated.
32 devices in a mesh: lon: 8 (over y, x, core), lat: 4 (over z).
Axes of the slice: x: 2, y: 2, z: 4, core: 2. Of those that a mesh axis runs over, the one named last changes fastest.
Arguments:
- depth_init: float32 [1024, 1024], P('lat', 'lon'), may hold values from 0.5 to 2.5
- ground: float32 [1024, 1024], P('lat', 'lon'), may hold values from -4 to 4
- roughness: float32 [1024, 1024], P('lat', 'lon'), may hold values from 0.02 to 0.12
- river_init: float32 [1024, 1024], P('lat', 'lon'), may hold values from 0.5 to 4.5
- reach_mask: int32 [1024, 8], P('lat', 'lon'), may hold values from 0 to 1, as said below
- width_class: int32 [1024, 1024], P('lat', 'lon'), may hold values from 0 to 7
- bank_class: int32 [1024, 1024], P('lat', 'lon'), may hold values from 0 to 7
Outputs:
- flood_depth: float32 [1024, 1024], P('lat', 'lon')
- river_depth: float32 [1024, 1024], P('lat', 'lon')
- flow_east: float32 [1024, 1024], P('lat', 'lon')
- flow_north: float32 [1024, 1024], P('lat', 'lon')
Inputs may be any that keep to these rules, and one draw needn't show every extreme that they name: Call the 256 rows of one lat index and one lon index of reach_mask a tile. A tile has at most 64 channelled reaches, and some tile exactly 64. A tile with more than 32 has 34 or more, and lies four or more lon indices (around the cycle) from any other such tile of the same lat index; every other tile has at most 16, and some tile beside a full one exactly that many.
All inputs are finite; a program needn't handle non-finite values.
Results may differ from a plain program's by a relative error of at most 0.00002.
Values sent between devices are 32-bit elements; how exact they have to be, the bound alone decides.
No kernel may reach another device: no remote copies, remote signals or barrier semaphores. Data moves between devices by JAX's collectives and lax.ppermute only.
A program may use at most 64 MiB of HBM per device.

v0:
```python
import jax
import jax.numpy as jnp
from jax import lax
from jax.sharding import PartitionSpec as P

SUB = 8
STEPS = 4


GRAVITY = 9.81
CELL_SIZE = 90.0
TIME_STEP = 10.0
SHALLOW = 0.1
EXCHANGE = 0.01
CHANNEL_MANNING = 0.035


def padded(block, sides, width, periodic):
    for axis, dim in sides:
        count = lax.axis_size(axis)
        forward = [(i, i + 1) for i in range(count - 1)]
        if periodic:
            forward.append((count - 1, 0))
        backward = [(target, source) for source, target in forward]
        low = lax.ppermute(
            lax.slice_in_dim(block, block.shape[dim] - width, None, axis=dim), axis, forward
        )
        high = lax.ppermute(lax.slice_in_dim(block, 0, width, axis=dim), axis, backward)
        block = jnp.concatenate([low, block, high], axis=dim)
    return block


def face_flow(
    current, surface_from, surface_to, ground_from, ground_to, friction, breadth, duration
):
    height = jnp.maximum(surface_from, surface_to) - jnp.maximum(ground_from, ground_to)
    driven = (
        current - GRAVITY * duration * breadth * height * (surface_to - surface_from) / CELL_SIZE
    )
    resisted = 1.0 + GRAVITY * duration * friction * jnp.abs(current) / (
        height * height + SHALLOW * SHALLOW
    ) ** (7.0 / 6.0)
    return driven / resisted


def reach_update(river_bed, channel_width, safe_width, river_depth, discharge, surface):
    duration = TIME_STEP / SUB
    breadth = 0.5 * (channel_width[:, :-1] + channel_width[:, 1:])
    safe_breadth = 0.5 * (safe_width[:, :-1] + safe_width[:, 1:])
    friction = CHANNEL_MANNING * CHANNEL_MANNING / safe_breadth
    closed = jnp.zeros_like(river_depth[:, :1])
    gathered = jnp.zeros_like(river_depth)
    for substep in range(SUB):
        water_level = river_bed + river_depth
        interior = face_flow(
            discharge[:, :-1],
            water_level[:, :-1],
            water_level[:, 1:],
            river_bed[:, :-1],
            river_bed[:, 1:],
            friction,
            breadth,
            duration,
        )
        discharge = jnp.concatenate([interior, closed], axis=1)
        inflow = jnp.concatenate([closed, interior], axis=1)
        transfer = EXCHANGE * (water_level - surface)
        river_depth = river_depth + duration * (
            (inflow - discharge) / (safe_width * CELL_SIZE) - transfer
        )
        gathered = gathered + duration * transfer
    return (river_depth, discharge, gathered)


def channel_slots(slot_state):
    safe_width = jnp.where(slot_state[1] > 0.0, slot_state[1], 1.0)
    new_river, new_discharge, gathered = reach_update(
        slot_state[0], slot_state[1], safe_width, slot_state[2], slot_state[3], slot_state[4]
    )
    return jnp.stack([new_river, new_discharge, gathered])


def rims(fields):
    across = padded(fields, (("lon", 2),), 1, True)
    along_lat = padded(fields, (("lat", 1),), 1, False)
    return (across, along_lat)


def body(depth_init, ground, roughness, river_init, reach_mask, width_class, bank_class):
    row_count, col_count = ground.shape
    most_slots = row_count // 4
    channel_width = 8.0 + 9.0 * width_class.astype(jnp.float32)
    river_bed = ground - (1.0 + 0.5 * bank_class.astype(jnp.float32))
    lat_number = lax.axis_index("lat")
    lat_total = lax.axis_size("lat")
    row_numbers = jnp.arange(row_count)
    open_north = ((row_numbers < row_count - 1) | (lat_number < lat_total - 1))[:, None]
    open_south = lat_number > 0
    static_across, static_along = rims(jnp.stack([ground, roughness]))
    ground_east = static_across[0, :, 2:]
    rough_east = static_across[1, :, 2:]
    ground_west = static_across[0, :, 0]
    rough_west = static_across[1, :, 0]
    ground_north = static_along[0, 2:, :]
    rough_north = static_along[1, 2:, :]
    ground_south = static_along[0, 0, :]
    rough_south = static_along[1, 0, :]
    channelled = reach_mask[:, 0] > 0
    channel_count = jnp.sum(channelled.astype(jnp.int32))
    listed = jnp.nonzero(channelled, size=most_slots, fill_value=0)[0].astype(jnp.int32)
    positions = jnp.arange(most_slots)
    occupied = positions < channel_count
    chosen_rows = listed[jnp.clip(positions, 0, most_slots - 1)]
    target = jnp.where(occupied, chosen_rows, row_count).astype(jnp.int32)

    def select_rows(field):
        return jnp.where(occupied[:, None], field[chosen_rows], 0.0)

    slot_bed = select_rows(river_bed)
    slot_width = select_rows(channel_width)
    flood = depth_init
    river_depth = river_init
    discharge = jnp.zeros((row_count, col_count), jnp.float32)
    flow_east = jnp.zeros((row_count, col_count), jnp.float32)
    flow_north = jnp.zeros((row_count, col_count), jnp.float32)
    flow_west = jnp.zeros((row_count,), jnp.float32)
    flow_south = jnp.zeros((col_count,), jnp.float32)
    for repeat in range(STEPS):
        depth_across, depth_along = rims(flood[None])
        surface = ground + flood
        surface_east = ground_east + depth_across[0, :, 2:]
        surface_west = ground_west + depth_across[0, :, 0]
        surface_north = ground_north + depth_along[0, 2:, :]
        surface_south = ground_south + depth_along[0, 0, :]
        flow_east = face_flow(
            flow_east,
            surface,
            surface_east,
            ground,
            ground_east,
            roughness * rough_east,
            1.0,
            TIME_STEP,
        )
        flow_west = face_flow(
            flow_west,
            surface_west,
            surface[:, 0],
            ground_west,
            ground[:, 0],
            rough_west * roughness[:, 0],
            1.0,
            TIME_STEP,
        )
        north_flux = face_flow(
            flow_north,
            surface,
            surface_north,
            ground,
            ground_north,
            roughness * rough_north,
            1.0,
            TIME_STEP,
        )
        flow_north = jnp.where(open_north, north_flux, 0.0)
        south_flux = face_flow(
            flow_south,
            surface_south,
            surface[0],
            ground_south,
            ground[0],
            rough_south * roughness[0],
            1.0,
            TIME_STEP,
        )
        flow_south = jnp.where(open_south, south_flux, 0.0)
        from_west = jnp.concatenate([flow_west[:, None], flow_east[:, :-1]], axis=1)
        from_south = jnp.concatenate([flow_south[None, :], flow_north[:-1]], axis=0)
        flooded = flood + TIME_STEP / CELL_SIZE * (from_west - flow_east + from_south - flow_north)
        slot_state = jnp.stack(
            [
                slot_bed,
                slot_width,
                select_rows(river_depth),
                select_rows(discharge),
                select_rows(surface),
            ]
        )
        results = channel_slots(slot_state)
        river_depth = river_depth.at[target].set(results[0], mode="drop")
        discharge = discharge.at[target].set(results[1], mode="drop")
        gathered = jnp.zeros_like(flood).at[target].set(results[2], mode="drop")
        flood = flooded + jnp.where(channelled[:, None], gathered * channel_width / CELL_SIZE, 0.0)
    return (flood, river_depth, flow_east, flow_north)


def solution(mesh):
    return jax.shard_map(
        body,
        mesh=mesh,
        in_specs=(
            P("lat", "lon"),
            P("lat", "lon"),
            P("lat", "lon"),
            P("lat", "lon"),
            P("lat", "lon"),
            P("lat", "lon"),
            P("lat", "lon"),
        ),
        out_specs=(P("lat", "lon"), P("lat", "lon"), P("lat", "lon"), P("lat", "lon")),
        check_vma=False,
    )
```

profile of v0, /device:TPU:11, one launch (start us, length us, event | category | flops | bytes accessed | tf_op | source)
XLA Modules:
  0.0 83.6 jit_solution(5315973568915750591)
XLA Ops:
  0.6 0.9 %copy.196 = f32[256,128]{1,0:T(8,128)S(1)} copy(f32[256,128]{1,0:T(8,128)} %param.10) | data formatting | bytes 262144
  3.6 2.1 %collective-permute-start.7 = (f32[1,1,128]{1,2,0:T(8,128)S(1)}, f32[1,1,128]{1,2,0:T(8,128)S(1)}, u32[]{:S(2)}, u32[]{:S(2)}) collective-permute-start(f32[1,1,128]{1,2,0:T(8,128)S(1)} %get-tuple-element.91), channel_id=1, source_target_pairs={{1,0},{2,1},{3,2},{5,4},{6,5},{7,6},{9,8},{10,9},{11,10},{13,12},{... | collective-permute-start | bytes 1544 | tf_op jit(solution)/shard_map/ppermute | solution.py:28
  5.7 1.9 %collective-permute-start.6 = (f32[2,1,128]{1,2,0:T(8,128)S(1)}, f32[2,1,128]{1,2,0:T(8,128)S(1)}, u32[]{:S(2)}, u32[]{:S(2)}) collective-permute-start(f32[2,1,128]{1,2,0:T(8,128)S(1)} %get-tuple-element.74), channel_id=1, source_target_pairs={{1,0},{2,1},{3,2},{5,4},{6,5},{7,6},{9,8},{10,9},{11,10},{13,12},{... | collective-permute-start | bytes 3080 | tf_op jit(solution)/shard_map/ppermute | solution.py:28
  7.7 2.3 %collective-permute-start.1 = (f32[1,256,1]{1,2,0:T(1,128)S(1)}, f32[1,256,1]{1,2,0:T(1,128)S(1)}, u32[]{:S(2)}, u32[]{:S(2)}) collective-permute-start(f32[1,256,1]{1,2,0:T(1,128)S(1)} %get-tuple-element.92), channel_id=1, source_target_pairs={{0,4},{4,8},{8,12},{12,16},{16,20},{20,24},{24,28},{28,0},{1,5},{5... | collective-permute-start | bytes 3080 | tf_op jit(solution)/shard_map/ppermute | solution.py:25
  11.3 2.3 %scatter_custom_fusion = s32[64]{0:T(128)S(1)} fusion(s32[256]{0:T(256)S(1)} %bitcast.195, s32[256]{0:T(256)S(1)} %broadcast.723, s32[]{:T(128)} %constant.236.clone.1), kind=kCustom, calls=%fused_computation.353 | custom fusion | flops 256 | bytes 260 | tf_op jit(solution)/shard_map/scatter-add | solution.py:110
  21.7 3.6 %collective-permute-start.5 = (f32[1,1,128]{1,2,0:T(8,128)S(1)}, f32[1,1,128]{1,2,0:T(8,128)S(1)}, u32[]{:S(2)}, u32[]{:S(2)}) collective-permute-start(f32[1,1,128]{1,2,0:T(8,128)S(1)} %get-tuple-element.90), channel_id=1, source_target_pairs={{0,1},{1,2},{2,3},{4,5},{5,6},{6,7},{8,9},{9,10},{10,11},{12,13},{... | collective-permute-start | bytes 1544 | tf_op jit(solution)/shard_map/ppermute | solution.py:25
  25.6 3.2 %collective-permute-start.4 = (f32[2,1,128]{1,2,0:T(8,128)S(1)}, f32[2,1,128]{1,2,0:T(8,128)S(1)}, u32[]{:S(2)}, u32[]{:S(2)}) collective-permute-start(f32[2,1,128]{1,2,0:T(8,128)S(1)} %get-tuple-element.73), channel_id=1, source_target_pairs={{0,1},{1,2},{2,3},{4,5},{5,6},{6,7},{8,9},{9,10},{10,11},{12,13},{... | collective-permute-start | bytes 3080 | tf_op jit(solution)/shard_map/ppermute | solution.py:25
  32.1 0.9 %scatter_custom_fusion.1 = f32[256,128]{1,0:T(8,128)S(1)} fusion(s32[64]{0:T(128)S(1)} %get-tuple-element.99, f32[]{:T(128)} %constant.229.clone.1, f32[]{:T(128)} %constant.245.clone.1, f32[64,128]{1,0:T(8,128)S(1)} %get-tuple-element.96, f32[64,128]{1,0:T(8,128)S(1)} %gather_fusion.3, pred[64]{0:T(512)(128)(4,1)S(1)} %iota_compare_fusion, ...), kind=kCustom, calls=%fused_computation.111 | custom fusion | flops 139264 | bytes 428032 | tf_op jit(solution)/shard_map/scatter | solution.py:192
  34.1 2.1 %collective-permute-start.11 = (f32[1,1,128]{1,2,0:T(8,128)S(1)}, f32[1,1,128]{1,2,0:T(8,128)S(1)}, u32[]{:S(2)}, u32[]{:S(2)}) collective-permute-start(f32[1,1,128]{1,2,0:T(8,128)S(1)} %get-tuple-element.86), channel_id=1, source_target_pairs={{1,0},{2,1},{3,2},{5,4},{6,5},{7,6},{9,8},{10,9},{11,10},{13,12},{... | collective-permute-start | bytes 1544 | tf_op jit(solution)/shard_map/ppermute | solution.py:28
  36.1 2.5 %collective-permute-start.8 = (f32[1,256,1]{1,2,0:T(1,128)S(1)}, f32[1,256,1]{1,2,0:T(1,128)S(1)}, u32[]{:S(2)}, u32[]{:S(2)}) collective-permute-start(f32[1,256,1]{1,2,0:T(1,128)S(1)} %get-tuple-element.87), channel_id=1, source_target_pairs={{0,4},{4,8},{8,12},{12,16},{16,20},{20,24},{24,28},{28,0},{1,5},{5... | collective-permute-start | bytes 3080 | tf_op jit(solution)/shard_map/ppermute | solution.py:25
  38.7 3.2 %collective-permute-start.10 = (f32[1,1,128]{1,2,0:T(8,128)S(1)}, f32[1,1,128]{1,2,0:T(8,128)S(1)}, u32[]{:S(2)}, u32[]{:S(2)}) collective-permute-start(f32[1,1,128]{1,2,0:T(8,128)S(1)} %get-tuple-element.85), channel_id=1, source_target_pairs={{0,1},{1,2},{2,3},{4,5},{5,6},{6,7},{8,9},{9,10},{10,11},{12,13},{... | collective-permute-start | bytes 1544 | tf_op jit(solution)/shard_map/ppermute | solution.py:25
  42.7 0.9 %scatter_custom_fusion.2 = f32[256,128]{1,0:T(8,128)S(1)} fusion(f32[256,128]{1,0:T(8,128)S(1)} %copy.196, s32[64]{0:T(128)S(1)} %get-tuple-element.99, f32[64,128]{1,0:T(8,128)S(1)} %get-tuple-element.43, f32[64,127]{1,0:T(8,128)S(1)} %add_divide_fusion.28, f32[]{:T(128)} %constant.229.clone.1, f32[]{:T(128)} %constant.252.clone.1, ...), kind=kCustom, calls=%fused_computation.235 | custom fusion | flops 90112 | bytes 297472 | tf_op jit(solution)/shard_map/scatter | solution.py:190
  47.4 0.9 %scatter_custom_fusion.4 = f32[256,128]{1,0:T(8,128)S(1)} fusion(s32[64]{0:T(128)S(1)} %get-tuple-element.99, f32[]{:T(128)} %constant.229.clone.1, f32[]{:T(128)} %constant.245.clone.1, f32[64,128]{1,0:T(8,128)S(1)} %select_add_fusion.2, f32[64,128]{1,0:T(8,128)S(1)} %gather_fusion.7, pred[64]{0:T(512)(128)(4,1)S(1)} %iota_compare_fusion, ...), kind=kCustom, calls=%fused_computation.109 | custom fusion | flops 139264 | bytes 428032 | tf_op jit(solution)/shard_map/scatter | solution.py:192
  49.0 2.1 %collective-permute-start.15 = (f32[1,1,128]{1,2,0:T(8,128)S(1)}, f32[1,1,128]{1,2,0:T(8,128)S(1)}, u32[]{:S(2)}, u32[]{:S(2)}) collective-permute-start(f32[1,1,128]{1,2,0:T(8,128)S(1)} %get-tuple-element.82), channel_id=1, source_target_pairs={{1,0},{2,1},{3,2},{5,4},{6,5},{7,6},{9,8},{10,9},{11,10},{13,12},{... | collective-permute-start | bytes 1544 | tf_op jit(solution)/shard_map/ppermute | solution.py:28
  51.1 3.0 %collective-permute-start.12 = (f32[1,256,1]{1,2,0:T(1,128)S(1)}, f32[1,256,1]{1,2,0:T(1,128)S(1)}, u32[]{:S(2)}, u32[]{:S(2)}) collective-permute-start(f32[1,256,1]{1,2,0:T(1,128)S(1)} %get-tuple-element.83), channel_id=1, source_target_pairs={{0,4},{4,8},{8,12},{12,16},{16,20},{20,24},{24,28},{28,0},{1,5},{5... | collective-permute-start | bytes 3080 | tf_op jit(solution)/shard_map/ppermute | solution.py:25
  54.1 3.2 %collective-permute-start.14 = (f32[1,1,128]{1,2,0:T(8,128)S(1)}, f32[1,1,128]{1,2,0:T(8,128)S(1)}, u32[]{:S(2)}, u32[]{:S(2)}) collective-permute-start(f32[1,1,128]{1,2,0:T(8,128)S(1)} %get-tuple-element.81), channel_id=1, source_target_pairs={{0,1},{1,2},{2,3},{4,5},{5,6},{6,7},{8,9},{9,10},{10,11},{12,13},{... | collective-permute-start | bytes 1544 | tf_op jit(solution)/shard_map/ppermute | solution.py:25
  58.1 0.9 %scatter_custom_fusion.5 = f32[256,128]{1,0:T(8,128)S(1)} fusion(f32[256,128]{1,0:T(8,128)S(1)} %scatter_custom_fusion.2, s32[64]{0:T(128)S(1)} %get-tuple-element.99, f32[64,128]{1,0:T(8,128)S(1)} %get-tuple-element.33, f32[64,127]{1,0:T(8,128)S(1)} %add_divide_fusion.20, f32[]{:T(128)} %constant.229.clone.1, f32[]{:T(128)} %constant.252.clone.1, ...), kind=kCustom, calls=%fused_computation.212 | custom fusion | flops 90112 | bytes 297472 | tf_op jit(solution)/shard_map/scatter | solution.py:190
  63.0 0.9 %scatter_custom_fusion.7 = f32[256,128]{1,0:T(8,128)S(1)} fusion(s32[64]{0:T(128)S(1)} %get-tuple-element.99, f32[]{:T(128)} %constant.229.clone.1, f32[]{:T(128)} %constant.245.clone.1, f32[64,128]{1,0:T(8,128)S(1)} %select_add_fusion.1, f32[64,128]{1,0:T(8,128)S(1)} %gather_fusion.10, pred[64]{0:T(512)(128)(4,1)S(1)} %iota_compare_fusion, ...), kind=kCustom, calls=%fused_computation.105 | custom fusion | flops 139264 | bytes 428032 | tf_op jit(solution)/shard_map/scatter | solution.py:192
  64.5 2.1 %collective-permute-start.19 = (f32[1,1,128]{1,2,0:T(8,128)S(1)}, f32[1,1,128]{1,2,0:T(8,128)S(1)}, u32[]{:S(2)}, u32[]{:S(2)}) collective-permute-start(f32[1,1,128]{1,2,0:T(8,128)S(1)} %get-tuple-element.78), channel_id=1, source_target_pairs={{1,0},{2,1},{3,2},{5,4},{6,5},{7,6},{9,8},{10,9},{11,10},{13,12},{... | collective-permute-start | bytes 1544 | tf_op jit(solution)/shard_map/ppermute | solution.py:28
  66.6 3.0 %collective-permute-start.16 = (f32[1,256,1]{1,2,0:T(1,128)S(1)}, f32[1,256,1]{1,2,0:T(1,128)S(1)}, u32[]{:S(2)}, u32[]{:S(2)}) collective-permute-start(f32[1,256,1]{1,2,0:T(1,128)S(1)} %get-tuple-element.79), channel_id=1, source_target_pairs={{0,4},{4,8},{8,12},{12,16},{16,20},{20,24},{24,28},{28,0},{1,5},{5... | collective-permute-start | bytes 3080 | tf_op jit(solution)/shard_map/ppermute | solution.py:25
  69.5 3.2 %collective-permute-start.18 = (f32[1,1,128]{1,2,0:T(8,128)S(1)}, f32[1,1,128]{1,2,0:T(8,128)S(1)}, u32[]{:S(2)}, u32[]{:S(2)}) collective-permute-start(f32[1,1,128]{1,2,0:T(8,128)S(1)} %get-tuple-element.77), channel_id=1, source_target_pairs={{0,1},{1,2},{2,3},{4,5},{5,6},{6,7},{8,9},{9,10},{10,11},{12,13},{... | collective-permute-start | bytes 1544 | tf_op jit(solution)/shard_map/ppermute | solution.py:25
  73.6 0.9 %scatter_custom_fusion.8 = f32[256,128]{1,0:T(8,128)S(1)} fusion(f32[256,128]{1,0:T(8,128)S(1)} %scatter_custom_fusion.5, s32[64]{0:T(128)S(1)} %get-tuple-element.99, f32[64,128]{1,0:T(8,128)S(1)} %get-tuple-element.23, f32[64,127]{1,0:T(8,128)S(1)} %add_divide_fusion.12, f32[]{:T(128)} %constant.229.clone.1, f32[]{:T(128)} %constant.252.clone.1, ...), kind=kCustom, calls=%fused_computation.189 | custom fusion | flops 90112 | bytes 297472 | tf_op jit(solution)/shard_map/scatter | solution.py:190
  78.6 0.9 %scatter_custom_fusion.10 = f32[256,128]{1,0:T(8,128)S(1)} fusion(s32[64]{0:T(128)S(1)} %get-tuple-element.99, f32[]{:T(128)} %constant.229.clone.1, f32[]{:T(128)} %constant.245.clone.1, f32[64,128]{1,0:T(8,128)S(1)} %select_add_fusion, f32[64,128]{1,0:T(8,128)S(1)} %gather_fusion.13, pred[64]{0:T(512)(128)(4,1)S(1)} %iota_compare_fusion, ...), kind=kCustom, calls=%fused_computation.103 | custom fusion | flops 139264 | bytes 428032 | tf_op jit(solution)/shard_map/scatter | solution.py:192
  82.0 0.9 %scatter_custom_fusion.11 = f32[256,128]{1,0:T(8,128)S(1)} fusion(f32[256,128]{1,0:T(8,128)S(1)} %scatter_custom_fusion.8, s32[64]{0:T(128)S(1)} %get-tuple-element.99, f32[64,128]{1,0:T(8,128)S(1)} %get-tuple-element.13, f32[64,127]{1,0:T(8,128)S(1)} %add_divide_fusion.4, f32[]{:T(128)} %constant.229.clone.1, f32[]{:T(128)} %constant.252.clone.1, ...), kind=kCustom, calls=%fused_computation.165 | custom fusion | flops 90112 | bytes 297472 | tf_op jit(solution)/shard_map/scatter | solution.py:190
  (197 shorter events, 34.1 us)
Async XLA Ops:
  0.6 1.0 %copy-start.1 = (f32[256,128]{1,0:T(8,128)S(1)}, f32[256,128]{1,0:T(8,128)}, u32[]{:S(2)}) copy-start(f32[256,128]{1,0:T(8,128)} %param.7) | copy-start | bytes 393220
  1.7 0.9 %copy-start.4 = (f32[256,128]{1,0:T(8,128)S(1)}, f32[256,128]{1,0:T(8,128)}, u32[]{:S(2)}) copy-start(f32[256,128]{1,0:T(8,128)} %param.9) | copy-start | bytes 393220
  1.7 19.3 %collective-permute-start.3 = (f32[1,256,1]{1,2,0:T(1,128)S(1)}, f32[1,256,1]{1,2,0:T(1,128)S(1)}, u32[]{:S(2)}, u32[]{:S(2)}) collective-permute-start(f32[1,256,1]{1,2,0:T(1,128)S(1)} %get-tuple-element.93), channel_id=1, source_target_pairs={{4,0},{8,4},{12,8},{16,12},{20,16},{24,20},{28,24},{0,28},{5,1},{9... | collective-permute-start | bytes 3080 | tf_op jit(solution)/shard_map/ppermute | solution.py:28
  2.8 19.0 %collective-permute-start.2 = (f32[2,256,1]{1,2,0:T(1,128)S(1)}, f32[2,256,1]{1,2,0:T(1,128)S(1)}, u32[]{:S(2)}, u32[]{:S(2)}) collective-permute-start(f32[2,256,1]{1,2,0:T(1,128)S(1)} %get-tuple-element.76), channel_id=1, source_target_pairs={{4,0},{8,4},{12,8},{16,12},{20,16},{24,20},{28,24},{0,28},{5,1},{9... | collective-permute-start | bytes 6152 | tf_op jit(solution)/shard_map/ppermute | solution.py:28
  3.6 22.1 %collective-permute-start.7 = (f32[1,1,128]{1,2,0:T(8,128)S(1)}, f32[1,1,128]{1,2,0:T(8,128)S(1)}, u32[]{:S(2)}, u32[]{:S(2)}) collective-permute-start(f32[1,1,128]{1,2,0:T(8,128)S(1)} %get-tuple-element.91), channel_id=1, source_target_pairs={{1,0},{2,1},{3,2},{5,4},{6,5},{7,6},{9,8},{10,9},{11,10},{13,12},{... | collective-permute-start | bytes 1544 | tf_op jit(solution)/shard_map/ppermute | solution.py:28
  5.7 23.1 %collective-permute-start.6 = (f32[2,1,128]{1,2,0:T(8,128)S(1)}, f32[2,1,128]{1,2,0:T(8,128)S(1)}, u32[]{:S(2)}, u32[]{:S(2)}) collective-permute-start(f32[2,1,128]{1,2,0:T(8,128)S(1)} %get-tuple-element.74), channel_id=1, source_target_pairs={{1,0},{2,1},{3,2},{5,4},{6,5},{7,6},{9,8},{10,9},{11,10},{13,12},{... | collective-permute-start | bytes 3080 | tf_op jit(solution)/shard_map/ppermute | solution.py:28
  7.7 2.3 %copy-start.6 = (s32[256,1]{0,1:T(1,128)S(1)}, s32[256,1]{0,1:T(1,128)}, u32[]{:S(2)}) copy-start(s32[256,1]{0,1:T(1,128)} %param.11) | copy-start | bytes 3076
  7.7 24.4 %collective-permute-start.1 = (f32[1,256,1]{1,2,0:T(1,128)S(1)}, f32[1,256,1]{1,2,0:T(1,128)S(1)}, u32[]{:S(2)}, u32[]{:S(2)}) collective-permute-start(f32[1,256,1]{1,2,0:T(1,128)S(1)} %get-tuple-element.92), channel_id=1, source_target_pairs={{0,4},{4,8},{8,12},{12,16},{16,20},{20,24},{24,28},{28,0},{1,5},{5... | collective-permute-start | bytes 3080 | tf_op jit(solution)/shard_map/ppermute | solution.py:25
  15.2 1.5 %copy-start.2 = (s32[256,128]{1,0:T(8,128)S(1)}, s32[256,128]{1,0:T(8,128)}, u32[]{:S(2)}) copy-start(s32[256,128]{1,0:T(8,128)} %param.12) | copy-start | bytes 393220
  21.0 11.1 %collective-permute-start = (f32[2,256,1]{1,2,0:T(1,128)S(1)}, f32[2,256,1]{1,2,0:T(1,128)S(1)}, u32[]{:S(2)}, u32[]{:S(2)}) collective-permute-start(f32[2,256,1]{1,2,0:T(1,128)S(1)} %get-tuple-element.75), channel_id=1, source_target_pairs={{0,4},{4,8},{8,12},{12,16},{16,20},{20,24},{24,28},{28,0},{1,5},{5... | collective-permute-start | bytes 6152 | tf_op jit(solution)/shard_map/ppermute | solution.py:25
  21.7 11.4 %collective-permute-start.5 = (f32[1,1,128]{1,2,0:T(8,128)S(1)}, f32[1,1,128]{1,2,0:T(8,128)S(1)}, u32[]{:S(2)}, u32[]{:S(2)}) collective-permute-start(f32[1,1,128]{1,2,0:T(8,128)S(1)} %get-tuple-element.90), channel_id=1, source_target_pairs={{0,1},{1,2},{2,3},{4,5},{5,6},{6,7},{8,9},{9,10},{10,11},{12,13},{... | collective-permute-start | bytes 1544 | tf_op jit(solution)/shard_map/ppermute | solution.py:25
  25.6 7.5 %collective-permute-start.4 = (f32[2,1,128]{1,2,0:T(8,128)S(1)}, f32[2,1,128]{1,2,0:T(8,128)S(1)}, u32[]{:S(2)}, u32[]{:S(2)}) collective-permute-start(f32[2,1,128]{1,2,0:T(8,128)S(1)} %get-tuple-element.73), channel_id=1, source_target_pairs={{0,1},{1,2},{2,3},{4,5},{5,6},{6,7},{8,9},{9,10},{10,11},{12,13},{... | collective-permute-start | bytes 3080 | tf_op jit(solution)/shard_map/ppermute | solution.py:25
  33.6 11.4 %collective-permute-start.9 = (f32[1,256,1]{1,2,0:T(1,128)S(1)}, f32[1,256,1]{1,2,0:T(1,128)S(1)}, u32[]{:S(2)}, u32[]{:S(2)}) collective-permute-start(f32[1,256,1]{1,2,0:T(1,128)S(1)} %get-tuple-element.88), channel_id=1, source_target_pairs={{4,0},{8,4},{12,8},{16,12},{20,16},{24,20},{28,24},{0,28},{5,1},{9... | collective-permute-start | bytes 3080 | tf_op jit(solution)/shard_map/ppermute | solution.py:28
  34.1 14.3 %collective-permute-start.11 = (f32[1,1,128]{1,2,0:T(8,128)S(1)}, f32[1,1,128]{1,2,0:T(8,128)S(1)}, u32[]{:S(2)}, u32[]{:S(2)}) collective-permute-start(f32[1,1,128]{1,2,0:T(8,128)S(1)} %get-tuple-element.86), channel_id=1, source_target_pairs={{1,0},{2,1},{3,2},{5,4},{6,5},{7,6},{9,8},{10,9},{11,10},{13,12},{... | collective-permute-start | bytes 1544 | tf_op jit(solution)/shard_map/ppermute | solution.py:28
  36.1 11.2 %collective-permute-start.8 = (f32[1,256,1]{1,2,0:T(1,128)S(1)}, f32[1,256,1]{1,2,0:T(1,128)S(1)}, u32[]{:S(2)}, u32[]{:S(2)}) collective-permute-start(f32[1,256,1]{1,2,0:T(1,128)S(1)} %get-tuple-element.87), channel_id=1, source_target_pairs={{0,4},{4,8},{8,12},{12,16},{16,20},{20,24},{24,28},{28,0},{1,5},{5... | collective-permute-start | bytes 3080 | tf_op jit(solution)/shard_map/ppermute | solution.py:25
  38.7 8.5 %collective-permute-start.10 = (f32[1,1,128]{1,2,0:T(8,128)S(1)}, f32[1,1,128]{1,2,0:T(8,128)S(1)}, u32[]{:S(2)}, u32[]{:S(2)}) collective-permute-start(f32[1,1,128]{1,2,0:T(8,128)S(1)} %get-tuple-element.85), channel_id=1, source_target_pairs={{0,1},{1,2},{2,3},{4,5},{5,6},{6,7},{8,9},{9,10},{10,11},{12,13},{... | collective-permute-start | bytes 1544 | tf_op jit(solution)/shard_map/ppermute | solution.py:25
  49.0 11.4 %collective-permute-start.13 = (f32[1,256,1]{1,2,0:T(1,128)S(1)}, f32[1,256,1]{1,2,0:T(1,128)S(1)}, u32[]{:S(2)}, u32[]{:S(2)}) collective-permute-start(f32[1,256,1]{1,2,0:T(1,128)S(1)} %get-tuple-element.84), channel_id=1, source_target_pairs={{4,0},{8,4},{12,8},{16,12},{20,16},{24,20},{28,24},{0,28},{5,1},{9... | collective-permute-start | bytes 3080 | tf_op jit(solution)/shard_map/ppermute | solution.py:28
  49.0 13.6 %collective-permute-start.15 = (f32[1,1,128]{1,2,0:T(8,128)S(1)}, f32[1,1,128]{1,2,0:T(8,128)S(1)}, u32[]{:S(2)}, u32[]{:S(2)}) collective-permute-start(f32[1,1,128]{1,2,0:T(8,128)S(1)} %get-tuple-element.82), channel_id=1, source_target_pairs={{1,0},{2,1},{3,2},{5,4},{6,5},{7,6},{9,8},{10,9},{11,10},{13,12},{... | collective-permute-start | bytes 1544 | tf_op jit(solution)/shard_map/ppermute | solution.py:28
  51.1 11.9 %collective-permute-start.12 = (f32[1,256,1]{1,2,0:T(1,128)S(1)}, f32[1,256,1]{1,2,0:T(1,128)S(1)}, u32[]{:S(2)}, u32[]{:S(2)}) collective-permute-start(f32[1,256,1]{1,2,0:T(1,128)S(1)} %get-tuple-element.83), channel_id=1, source_target_pairs={{0,4},{4,8},{8,12},{12,16},{16,20},{20,24},{24,28},{28,0},{1,5},{5... | collective-permute-start | bytes 3080 | tf_op jit(solution)/shard_map/ppermute | solution.py:25
  54.1 9.9 %collective-permute-start.14 = (f32[1,1,128]{1,2,0:T(8,128)S(1)}, f32[1,1,128]{1,2,0:T(8,128)S(1)}, u32[]{:S(2)}, u32[]{:S(2)}) collective-permute-start(f32[1,1,128]{1,2,0:T(8,128)S(1)} %get-tuple-element.81), channel_id=1, source_target_pairs={{0,1},{1,2},{2,3},{4,5},{5,6},{6,7},{8,9},{9,10},{10,11},{12,13},{... | collective-permute-start | bytes 1544 | tf_op jit(solution)/shard_map/ppermute | solution.py:25
  64.4 11.4 %collective-permute-start.17 = (f32[1,256,1]{1,2,0:T(1,128)S(1)}, f32[1,256,1]{1,2,0:T(1,128)S(1)}, u32[]{:S(2)}, u32[]{:S(2)}) collective-permute-start(f32[1,256,1]{1,2,0:T(1,128)S(1)} %get-tuple-element.80), channel_id=1, source_target_pairs={{4,0},{8,4},{12,8},{16,12},{20,16},{24,20},{28,24},{0,28},{5,1},{9... | collective-permute-start | bytes 3080 | tf_op jit(solution)/shard_map/ppermute | solution.py:28
  64.5 13.7 %collective-permute-start.19 = (f32[1,1,128]{1,2,0:T(8,128)S(1)}, f32[1,1,128]{1,2,0:T(8,128)S(1)}, u32[]{:S(2)}, u32[]{:S(2)}) collective-permute-start(f32[1,1,128]{1,2,0:T(8,128)S(1)} %get-tuple-element.78), channel_id=1, source_target_pairs={{1,0},{2,1},{3,2},{5,4},{6,5},{7,6},{9,8},{10,9},{11,10},{13,12},{... | collective-permute-start | bytes 1544 | tf_op jit(solution)/shard_map/ppermute | solution.py:28
  66.6 12.0 %collective-permute-start.16 = (f32[1,256,1]{1,2,0:T(1,128)S(1)}, f32[1,256,1]{1,2,0:T(1,128)S(1)}, u32[]{:S(2)}, u32[]{:S(2)}) collective-permute-start(f32[1,256,1]{1,2,0:T(1,128)S(1)} %get-tuple-element.79), channel_id=1, source_target_pairs={{0,4},{4,8},{8,12},{12,16},{16,20},{20,24},{24,28},{28,0},{1,5},{5... | collective-permute-start | bytes 3080 | tf_op jit(solution)/shard_map/ppermute | solution.py:25
  69.5 11.5 %collective-permute-start.18 = (f32[1,1,128]{1,2,0:T(8,128)S(1)}, f32[1,1,128]{1,2,0:T(8,128)S(1)}, u32[]{:S(2)}, u32[]{:S(2)}) collective-permute-start(f32[1,1,128]{1,2,0:T(8,128)S(1)} %get-tuple-element.77), channel_id=1, source_target_pairs={{0,1},{1,2},{2,3},{4,5},{5,6},{6,7},{8,9},{9,10},{10,11},{12,13},{... | collective-permute-start | bytes 1544 | tf_op jit(solution)/shard_map/ppermute | solution.py:25
  (5 other events, 3.8 us)
where the time goes:
time: 85.1 us; the launch traced here: 83.6 us
  starting transfers between devices  40.1 us (47%)
  other arithmetic  21.9 us (26%)
  local copies, waits for them, and re-layouts  19.7 us (23%)
  between operations  1.78 us (2%)
    ppermute x10, starting transfers between devices, padded(): lax.ppermute(lax.slice_in_dim(block, block.shape[dim] - width, None, axis...  27.8 us
    ppermute x10, starting transfers between devices, padded(): lax.ppermute(lax.slice_in_dim(block, 0, width, axis=dim), axis, backward)  12.3 us
    gather x14, local copies, waits for them, and re-layouts, select_rows(): return jnp.where(occupied[:, None], field[chosen_rows], 0.0)  8.39 us
    unnamed x23, local copies, waits for them, and re-layouts  5.28 us
    div x40, other arithmetic, face_flow(): return driven / resisted  4.43 us
    scatter x4, other arithmetic, body(): river_depth = river_depth.at[target].set(results[0], mode='drop')  3.62 us
    scatter x4, other arithmetic, body(): gathered = jnp.zeros_like(flood).at[target].set(results[2], mode='drop')  3.47 us
    add x31, other arithmetic, reach_update(): water_level = river_bed + river_depth  2.88 us
  transfers between devices with their start and end apart: 20, of which 0 were waited for; matrix products, arithmetic and copies ran while one was open for 42% of the time, Pallas kernels for 0%

commit v1 on v0

v1 whole, which is shorter than its diff:
```python
import jax
import jax.numpy as jnp
from jax import lax
from jax.experimental import pallas as pl
from jax.experimental.pallas import tpu as pltpu
from jax.sharding import PartitionSpec as P

SUB = 8
STEPS = 4

GRAVITY = 9.81
CELL_SIZE = 90.0
TIME_STEP = 10.0
SHALLOW = 0.1
EXCHANGE = 0.01
CHANNEL_MANNING = 0.035

RIM = 8
COLS = SUB * (STEPS - 2)
DURATION = TIME_STEP / SUB
SURFACE, GROUND, ROUGH = range(3)
FLOOD_FIELDS = 3
LEVEL, FLUX, BED, WIDTH, GAIN, LIVE = range(6)
SLOT_FIELDS = 6


def lanes(shape):
    return lax.broadcasted_iota(jnp.int32, shape, 1)


def sublanes(shape):
    return lax.broadcasted_iota(jnp.int32, shape, 0)


def east_of(field):
    return pltpu.roll(field, field.shape[1] - 1, 1)


def power(field, exponent):
    return jnp.exp(jnp.log(field) * exponent)


def face(flow, here, there, top, drive, friction):
    height = jnp.maximum(here, there) - top
    driven = flow - drive * height * (there - here)
    spread = power(height * height + SHALLOW * SHALLOW, -7.0 / 6.0)
    resisted = 1.0 + friction * jnp.abs(flow) * spread
    return driven * pl.reciprocal(resisted, approx=True)


def first_face(here, there, top, drive):
    height = jnp.maximum(here, there) - top
    return -(drive * height * (there - here))


def reach_constants(bed, width):
    top = jnp.maximum(bed, east_of(bed))
    breadth = 0.5 * (width + east_of(width))
    inner = lanes(bed.shape) < bed.shape[1] - 1
    drive = jnp.where(inner, (GRAVITY * DURATION / CELL_SIZE) * breadth, 0.0)
    friction = jnp.where(
        inner, (GRAVITY * DURATION * CHANNEL_MANNING * CHANNEL_MANNING) / breadth, 0.0
    )
    feed = (DURATION / CELL_SIZE) / width
    return top, drive, friction, feed


def reach_substeps(level, flux, surface, constants, starting):
    top, drive, friction, feed = constants
    gathered = None
    for substep in range(SUB):
        there = east_of(level)
        if starting and substep == 0:
            flux = first_face(level, there, top, drive)
        else:
            flux = face(flux, level, there, top, drive, friction)
        transfer = (EXCHANGE * DURATION) * (level - surface)
        level = level + ((pltpu.roll(flux, 1, 1) - flux) * feed - transfer)
        gathered = transfer if gathered is None else gathered + transfer
    return level, flux, gathered


def odd_position(axis):
    return lax.rem(lax.axis_index(axis), 2)


def rows_kernel(mask_hbm, *refs):
    fields, outs, (reals, classes, mask_ref, sems) = refs[:6], refs[6:8], refs[8:]
    rows = mask_hbm.shape[0]
    northern = odd_position("lat") == 0
    copies = [pltpu.make_async_copy(mask_hbm, mask_ref, sems.at[0])]
    for k, field in enumerate(fields):
        for side, start in enumerate((0, rows - RIM)):
            to = reals.at[side, k] if k < 4 else classes.at[side, k - 4]
            copies.append(
                pltpu.make_async_copy(field.at[pl.ds(start, RIM)], to, sems.at[1 + 2 * k + side])
            )
    for copy in copies:
        copy.start()
    for copy in copies:
        copy.wait()
    shape = reals.shape[2:]
    row = sublanes(shape)

    def rims(side, start):
        depth, ground, rough, river = [reals[side, k] for k in range(4)]
        width, bank = classes[side, 0], classes[side, 1]
        live = jnp.zeros(shape, jnp.float32)
        for j in range(RIM):
            live = jnp.where(row == j, mask_ref[start + j].astype(jnp.float32), live)
        bed = ground - (1.0 + 0.5 * bank.astype(jnp.float32))
        wide = 8.0 + 9.0 * width.astype(jnp.float32)
        return [ground + depth, ground, rough, bed + river, bed, wide, live]

    for k, (low, high) in enumerate(zip(rims(0, 0), rims(1, rows - RIM))):
        outs[0][RIM * k : RIM * (k + 1), :] = jnp.where(northern, high, low)
        outs[1][RIM * k : RIM * (k + 1), :] = jnp.where(northern, low, high)


def fill_list(mask_ref, rows_ref):
    rows, room = mask_ref.shape[0], rows_ref.shape[0]
    for i in range(room):
        rows_ref[i] = rows + 2 * RIM
    count = jnp.int32(0)
    batch = 16
    for r in range(0, rows, batch):
        bits = [mask_ref[r + j] for j in range(batch)]
        places = []
        for j in range(batch):
            places.append(count)
            count = count + bits[j]
        for j in range(batch):
            rows_ref[places[j]] = r + j + RIM
    rows_ref[count] = rows + 2 * RIM


def first_reaches(slot_ref, t):
    at = slice(t, t + RIM)
    width = slot_ref[WIDTH, at, :]
    constants = reach_constants(slot_ref[BED, at, :], width)
    level, flux, gathered = reach_substeps(
        slot_ref[LEVEL, at, :], None, slot_ref[GAIN, at, :], constants, True
    )
    slot_ref[LEVEL, at, :] = level
    slot_ref[FLUX, at, :] = flux
    live = slot_ref[LIVE, at, :] > 0.0
    slot_ref[GAIN, at, :] = jnp.where(live, gathered * (width / CELL_SIZE), 0.0)


def own_kernel(
    mask_ref, depth_ref, ground_ref, river_ref, width_ref, bank_ref,
    rows_ref, slot_ref, surface_ref, gain_ref, level_ref, listed_ref,
    bed_ref, wide_ref,
):
    rows, cols = depth_ref.shape
    slots = rows // 4
    tail = rows + RIM
    fill_list(mask_ref, rows_ref)
    ground = ground_ref[...]
    bed = ground - (1.0 + 0.5 * bank_ref[...].astype(jnp.float32))
    surface_ref[RIM:tail, :] = ground + depth_ref[...]
    surface_ref[tail + RIM : tail + 2 * RIM, :] = jnp.zeros((RIM, cols), jnp.float32)
    level_ref[0:rows, :] = bed + river_ref[...]
    bed_ref[0:rows, :] = bed
    wide_ref[0:rows, :] = 8.0 + 9.0 * width_ref[...].astype(jnp.float32)
    level_ref[rows : rows + RIM, :] = jnp.zeros((RIM, cols), jnp.float32)
    bed_ref[rows : rows + RIM, :] = jnp.zeros((RIM, cols), jnp.float32)
    wide_ref[rows : rows + RIM, :] = jnp.ones((RIM, cols), jnp.float32)
    gain_ref[...] = jnp.zeros(gain_ref.shape, jnp.float32)
    lane = lanes((RIM, cols))
    listed = jnp.zeros((RIM, cols), jnp.float32)

    for i in range(slots):
        e = rows_ref[i]
        own = jnp.where(e < tail, e - RIM, rows)
        to, of, surf = pl.ds(i, 1), pl.ds(own, 1), pl.ds(e, 1)
        slot_ref[LEVEL, to, :] = level_ref[of, :]
        slot_ref[BED, to, :] = bed_ref[of, :]
        slot_ref[WIDTH, to, :] = wide_ref[of, :]
        slot_ref[GAIN, to, :] = surface_ref[surf, :]
        occupied = jnp.where(e < tail, 1.0, 0.0)
        slot_ref[LIVE, to, :] = jnp.full((1, cols), occupied, jnp.float32)
        listed = jnp.where(lane == cols - slots + i, e.astype(jnp.float32), listed)
    listed_ref[...] = listed
    for t in range(0, slots, RIM):
        first_reaches(slot_ref, t)
    for i in range(slots):
        gain_ref[pl.ds(rows_ref[i], 1), :] = slot_ref[GAIN, pl.ds(i, 1), :]


def pack_kernel(
    ground_ref, rough_ref, own_slot, surface_ref, own_gain, listed_ref, p_ref, q_ref,
    a_ref, b_ref, flood_ref, slot_ref, gain_ref,
):
    rows, cols = ground_ref.shape
    slots = rows // 4
    tail = rows + RIM
    half = RIM // 2
    northern = odd_position("lat") == 0
    p, q = p_ref[...], q_ref[...]
    north = jnp.where(northern, p, q)
    south = jnp.where(northern, q, p)

    def rim(block, k):
        return block[RIM * k : RIM * (k + 1)]

    def ends(k):
        return jnp.concatenate([rim(south, k)[half:], rim(north, k)[:half]], axis=0)

    last = slice(slots, slots + RIM)
    slot_ref[GAIN, last, :] = ends(0)
    slot_ref[LEVEL, last, :] = ends(3)
    slot_ref[BED, last, :] = ends(4)
    slot_ref[WIDTH, last, :] = ends(5)
    slot_ref[LIVE, last, :] = ends(6)
    first_reaches(slot_ref, slots)
    slot_ref[:, 0:slots, :] = own_slot[:, 0:slots, :]
    flood_ref[SURFACE, RIM:tail, :] = surface_ref[RIM:tail, :]
    flood_ref[GROUND, RIM:tail, :] = ground_ref[...]
    flood_ref[ROUGH, RIM:tail, :] = rough_ref[...]
    for k in range(FLOOD_FIELDS):
        flood_ref[k, 0:RIM, :] = rim(south, k)
        flood_ref[k, tail : tail + RIM, :] = rim(north, k)
        flood_ref[k, tail + RIM : tail + 2 * RIM, :] = jnp.zeros((RIM, cols), jnp.float32)
    gain_ref[...] = own_gain[...]
    gain_ref[half:RIM, :] = slot_ref[GAIN, slots : slots + half, :]
    gain_ref[tail : tail + half, :] = slot_ref[GAIN, slots + half : slots + RIM, :]

    groups = cols // COLS
    group = lanes((RIM, cols)) // COLS
    eastern = odd_position("lon") == 0
    from_a = jnp.where(eastern, cols - COLS, 0)
    from_b = jnp.where(eastern, 0, cols - COLS)
    tiles = []
    for k in range(FLOOD_FIELDS):
        for t in range(0, rows + 2 * RIM, RIM):
            tiles.append((flood_ref, k, t))
    for k in range(SLOT_FIELDS):
        for t in range(0, slots + RIM, RIM):
            tiles.append((slot_ref, k, t))
    listed = listed_ref[...]
    for out_ref, start in ((a_ref, from_a), (b_ref, from_b)):
        for m in range(0, len(tiles), groups):
            block = listed
            for g, (ref, k, t) in enumerate(tiles[m : m + groups]):
                source = ref[k, t : t + RIM, :]
                moved = pltpu.roll(source, lax.rem(cols + COLS * g - start, cols), 1)
                block = jnp.where(group == g, moved, block)
            out_ref[m // groups * RIM : (m // groups + 1) * RIM, :] = block


def step_kernel(
    rows_ref, flood_ref, slot_ref, gain_ref, level_ref, bank_ref, a_ref, b_ref,
    depth_out, river_out, east_out, north_out,
    own_ref, side_ref, side_slot, surf_ref, side_gain, own_gain,
    flow_ref, fixed_ref, river_ref, west_rows, east_rows, sems,
):
    rows, cols = depth_out.shape
    slots = rows // 4
    tail = rows + RIM
    ext = rows + 2 * RIM
    total = slots + RIM
    half = RIM // 2
    lat_number, lat_total = lax.axis_index("lat"), lax.axis_size("lat")
    eastern = odd_position("lon") == 0
    lists = a_ref.shape[0] - RIM

    def fetch(to_a, to_b):
        one = pltpu.make_async_copy(a_ref.at[lists], to_a, sems.at[0])
        two = pltpu.make_async_copy(b_ref.at[lists], to_b, sems.at[1])
        return one, two

    one, two = fetch(east_rows, west_rows)
    one.start()
    two.start()

    groups = cols // COLS
    lane = lanes((RIM, cols))
    low = lane < cols // 2
    use_a = (lane < cols // 2) == eastern
    to_a = jnp.where(eastern, 0, cols - COLS)
    to_b = jnp.where(eastern, cols - COLS, 0)
    tiles = []
    for k in range(FLOOD_FIELDS):
        for t in range(0, ext, RIM):
            tiles.append((side_ref, k, t))
    for k in range(SLOT_FIELDS):
        for t in range(0, total, RIM):
            tiles.append((side_slot, k, t))
    for n, (ref, k, t) in enumerate(tiles):
        m, g = n // groups, n % groups
        at = slice(m * RIM, (m + 1) * RIM)
        from_a = pltpu.roll(a_ref[at, :], lax.rem(cols + to_a - COLS * g, cols), 1)
        from_b = pltpu.roll(b_ref[at, :], lax.rem(cols + to_b - COLS * g, cols), 1)
        ref[k, t : t + RIM, :] = jnp.where(use_a, from_a, from_b)
    for t in range(0, ext + RIM, RIM):
        own_ref[t : t + RIM, :] = flood_ref[SURFACE, t : t + RIM, :]
        own_gain[t : t + RIM, :] = gain_ref[t : t + RIM, :]
        for k in range(2):
            side_gain[k, t : t + RIM, :] = jnp.zeros((RIM, cols), jnp.float32)
    side_ref[SURFACE, ext : ext + RIM, :] = jnp.zeros((RIM, cols), jnp.float32)
    one.wait()
    two.wait()

    first = cols - slots

    def east_row(i):
        return jnp.where(eastern, east_rows[first + i], west_rows[first + i]).astype(jnp.int32)

    def west_row(i):
        return jnp.where(eastern, west_rows[first + i], east_rows[first + i]).astype(jnp.int32)

    def spread_side():
        for i in range(slots):
            line = side_slot[GAIN, pl.ds(i, 1), :]
            side_gain[0, pl.ds(east_row(i), 1), :] = line
            side_gain[1, pl.ds(west_row(i), 1), :] = line
        for k in range(2):
            side_gain[k, half:RIM, :] = side_slot[GAIN, slots : slots + half, :]
            side_gain[k, tail : tail + half, :] = side_slot[GAIN, slots + half : total, :]

    def spread_own():
        for i in range(slots):
            own_gain[pl.ds(rows_ref[i], 1), :] = slot_ref[GAIN, pl.ds(i, 1), :]
        own_gain[half:RIM, :] = slot_ref[GAIN, slots : slots + half, :]
        own_gain[tail : tail + half, :] = slot_ref[GAIN, slots + half : total, :]

    spread_side()

    def reaches(state, surface, t):
        at = slice(t, t + RIM)
        width = state[WIDTH, at, :]
        constants = reach_constants(state[BED, at, :], width)
        level, flux, gathered = reach_substeps(
            state[LEVEL, at, :], state[FLUX, at, :], surface[at, :], constants, False
        )
        state[LEVEL, at, :] = level
        state[FLUX, at, :] = flux
        live = state[LIVE, at, :] > 0.0
        state[GAIN, at, :] = jnp.where(live, gathered * (width / CELL_SIZE), 0.0)

    last_lane = lane == cols - 1
    first_lane = lane == 0
    row = sublanes((RIM, cols))
    first_row, last_row = row == 0, row == RIM - 1
    drive = GRAVITY * TIME_STEP / CELL_SIZE
    share = TIME_STEP / CELL_SIZE

    def pair_east(own, side):
        a, b = east_of(own), east_of(side)
        return jnp.where(last_lane, b, a), jnp.where(last_lane, a, b)

    def pair_west(own, side):
        a, b = pltpu.roll(own, 1, 1), pltpu.roll(side, 1, 1)
        return jnp.where(first_lane, b, a), jnp.where(first_lane, a, b)

    def constants_of(t):
        at = slice(t, t + RIM)
        up = slice(t + 1, t + 1 + RIM)
        ground = flood_ref[GROUND, at, :], side_ref[GROUND, at, :]
        rough = flood_ref[ROUGH, at, :], side_ref[ROUGH, at, :]
        ground_east, rough_east = pair_east(*ground), pair_east(*rough)
        weight = GRAVITY * TIME_STEP
        for j, ref in enumerate((flood_ref, side_ref)):
            fixed_ref[j, 0, at, :] = jnp.maximum(ground[j], ground_east[j])
            fixed_ref[j, 1, at, :] = weight * (rough[j] * rough_east[j])
            fixed_ref[j, 2, at, :] = jnp.maximum(ground[j], ref[GROUND, up, :])
            fixed_ref[j, 3, at, :] = weight * (rough[j] * ref[ROUGH, up, :])

    def flood_step(step):
        before = [None, None]
        for t in range(0, ext, RIM):
            at = slice(t, t + RIM)
            up = slice(t + 1, t + 1 + RIM)
            final = step == STEPS - 1
            if final and t > rows:
                continue
            here = [own_ref[at, :], side_ref[SURFACE, at, :]]
            east = pair_east(*here)
            north = [own_ref[up, :], side_ref[SURFACE, up, :]]
            flows_east, flows_north = [], []
            for j in range(2):
                top_east, top_north = fixed_ref[j, 0, at, :], fixed_ref[j, 2, at, :]
                if step == 0:
                    to_east = first_face(here[j], east[j], top_east, drive)
                    to_north = first_face(here[j], north[j], top_north, drive)
                else:
                    to_east = face(
                        flow_ref[j, 0, at, :], here[j], east[j], top_east, drive, fixed_ref[j, 1, at, :]
                    )
                    to_north = None
                    if j == 0 or not final:
                        to_north = face(
                            flow_ref[j, 1, at, :], here[j], north[j], top_north, drive,
                            fixed_ref[j, 3, at, :],
                        )
                if to_north is not None and t == 0:
                    to_north = jnp.where(last_row & (lat_number == 0), 0.0, to_north)
                if to_north is not None and t == rows:
                    to_north = jnp.where(last_row & (lat_number == lat_total - 1), 0.0, to_north)
                flows_east.append(to_east)
                flows_north.append(to_north)
                if not final:
                    flow_ref[j, 0, at, :] = to_east
                    flow_ref[j, 1, at, :] = to_north
            west = pair_west(*flows_east)
            for j in range(1 if final else 2):
                turned = pltpu.roll(flows_north[j], 1, 0)
                under = turned if before[j] is None else before[j]
                south = jnp.where(first_row, under, turned)
                before[j] = turned
                moved = share * (west[j] - flows_east[j] + south - flows_north[j])
                if j == 0:
                    new = here[j] + moved + own_gain[at, :]
                    if not final:
                        own_ref[at, :] = new
                    elif t > 0:
                        out = slice(t - RIM, t)
                        depth_out[out, :] = new - flood_ref[GROUND, at, :]
                        east_out[out, :] = flows_east[0]
                        north_out[out, :] = flows_north[0]
                else:
                    gain = jnp.where(low, side_gain[0, at, :], side_gain[1, at, :])
                    side_ref[SURFACE, at, :] = here[j] + moved + gain

    for t in range(0, ext, RIM):
        constants_of(t)
    flood_step(0)
    for step in range(1, STEPS):
        for i in range(slots):
            surf_ref[0, pl.ds(i, 1), :] = own_ref[pl.ds(rows_ref[i], 1), :]
        surf_ref[0, slots : slots + half, :] = own_ref[half:RIM, :]
        surf_ref[0, slots + half : total, :] = own_ref[tail : tail + half, :]
        for t in range(0, total, RIM):
            reaches(slot_ref, surf_ref.at[0], t)
        spread_own()
        if step < STEPS - 1:
            middle = lanes((1, cols)) < cols // 2
            for i in range(slots):
                surf_ref[1, pl.ds(i, 1), :] = jnp.where(
                    middle,
                    side_ref[SURFACE, pl.ds(east_row(i), 1), :],
                    side_ref[SURFACE, pl.ds(west_row(i), 1), :],
                )
            surf_ref[1, slots : slots + half, :] = side_ref[SURFACE, half:RIM, :]
            surf_ref[1, slots + half : total, :] = side_ref[SURFACE, tail : tail + half, :]
            for t in range(0, total, RIM):
                reaches(side_slot, surf_ref.at[1], t)
            spread_side()
        flood_step(step)
    river_ref[0:rows, :] = level_ref[0:rows, :]
    for i in range(slots):
        e = rows_ref[i]
        own = jnp.where(e < tail, e - RIM, rows)
        river_ref[pl.ds(own, 1), :] = slot_ref[LEVEL, pl.ds(i, 1), :]
    bed = flood_ref[GROUND, RIM:tail, :] - (1.0 + 0.5 * bank_ref[...].astype(jnp.float32))
    river_out[...] = river_ref[0:rows, :] - bed


def swaps(count, first):
    pairs = [(i, i + 1) for i in range(first, count - 1, 2)]
    return pairs + [(b, a) for a, b in pairs]


def body(depth_init, ground, roughness, river_init, reach_mask, width_class, bank_class):
    rows, cols = ground.shape
    slots = rows // 4
    f32 = jnp.float32
    lon_total, lat_total = lax.axis_size("lon"), lax.axis_size("lat")
    mask = reach_mask.reshape(rows)
    smem = pl.BlockSpec(memory_space=pltpu.SMEM)
    vmem = pl.BlockSpec(memory_space=pltpu.VMEM)
    fields = (depth_init, ground, roughness, river_init, width_class, bank_class)
    ext = rows + 2 * RIM
    params = pltpu.CompilerParams(vmem_limit_bytes=48 * 1024 * 1024)

    hbm = pl.BlockSpec(memory_space=pltpu.HBM)
    rim_shape = jax.ShapeDtypeStruct((7 * RIM, cols), f32)
    to_p, to_q = pl.pallas_call(
        rows_kernel,
        in_specs=[hbm] * 7,
        out_specs=[vmem, vmem],
        out_shape=[rim_shape, rim_shape],
        scratch_shapes=[
            pltpu.VMEM((2, 4, RIM, cols), f32),
            pltpu.VMEM((2, 2, RIM, cols), jnp.int32),
            pltpu.SMEM((rows,), jnp.int32),
            pltpu.SemaphoreType.DMA((13,)),
        ],
        compiler_params=pltpu.CompilerParams(vmem_limit_bytes=63 * 1024 * 1024),
        name="rims",
    )(mask, *fields)
    got_p = lax.ppermute(to_p, "lat", swaps(lat_total, 0))
    got_q = lax.ppermute(to_q, "lat", swaps(lat_total, 1))
    slot_shape = jax.ShapeDtypeStruct((SLOT_FIELDS, slots + RIM, cols), f32)
    dense = jax.ShapeDtypeStruct((ext + RIM, cols), f32)
    row_list, own_slot, surface, own_gain, level, listed = pl.pallas_call(
        own_kernel,
        in_specs=[smem] + [vmem] * 5,
        out_specs=[smem] + [vmem] * 5,
        out_shape=[
            jax.ShapeDtypeStruct((2 * slots,), jnp.int32),
            slot_shape,
            dense,
            dense,
            jax.ShapeDtypeStruct((rows + RIM, cols), f32),
            jax.ShapeDtypeStruct((RIM, cols), f32),
        ],
        scratch_shapes=[pltpu.VMEM((rows + RIM, cols), f32)] * 2,
        compiler_params=params,
        name="own_reaches",
    )(mask, depth_init, ground, river_init, width_class, bank_class)

    tiles = FLOOD_FIELDS * ext // RIM + SLOT_FIELDS * (slots // RIM + 1)
    message = -(-(tiles + slots // COLS) // (cols // COLS)) * RIM
    message_shape = jax.ShapeDtypeStruct((message, cols), f32)
    to_a, to_b, flood, slot, gain = pl.pallas_call(
        pack_kernel,
        in_specs=[vmem] * 8,
        out_specs=[vmem] * 5,
        out_shape=[
            message_shape,
            message_shape,
            jax.ShapeDtypeStruct((FLOOD_FIELDS, ext + RIM, cols), f32),
            slot_shape,
            dense,
        ],
        compiler_params=params,
        name="pack",
    )(ground, roughness, own_slot, surface, own_gain, listed, got_p, got_q)
    ring = swaps(lon_total, 1) + [(lon_total - 1, 0), (0, lon_total - 1)]
    got_a = lax.ppermute(to_a, "lon", swaps(lon_total, 0))
    got_b = lax.ppermute(to_b, "lon", ring)

    tile = jax.ShapeDtypeStruct((rows, cols), f32)
    return pl.pallas_call(
        step_kernel,
        in_specs=[smem] + [vmem] * 7,
        out_specs=[vmem] * 4,
        out_shape=[tile] * 4,
        scratch_shapes=[
            pltpu.VMEM((ext + RIM, cols), f32),
            pltpu.VMEM((FLOOD_FIELDS, ext + RIM, cols), f32),
            pltpu.VMEM((SLOT_FIELDS, slots + RIM, cols), f32),
            pltpu.VMEM((2, slots + RIM, cols), f32),
            pltpu.VMEM((2, ext + RIM, cols), f32),
            pltpu.VMEM((ext + RIM, cols), f32),
            pltpu.VMEM((2, 2, ext, cols), f32),
            pltpu.VMEM((2, 4, ext, cols), f32),
            pltpu.VMEM((rows + RIM, cols), f32),
            pltpu.SMEM((cols,), f32),
            pltpu.SMEM((cols,), f32),
            pltpu.SemaphoreType.DMA((2,)),
        ],
        compiler_params=params,
        name="steps",
    )(row_list, flood, slot, gain, level, bank_class, got_a, got_b)


def solution(mesh):
    grid = P("lat", "lon")
    return jax.shard_map(
        body,
        mesh=mesh,
        in_specs=(grid,) * 7,
        out_specs=(grid,) * 4,
        check_vma=False,
    )
```

time: 85.1 us -> 27.7 us (0.33); the launches traced: 83.6 us -> 27.5 us
  starting transfers between devices: 40.1 us -> 7.14 us
  other arithmetic: 21.9 us -> 0 us
  local copies, waits for them, and re-layouts: 19.7 us -> 0.03 us
  Pallas kernels: 0 us -> 15.6 us
  waiting for transfers between devices: 0.05 us -> 3.92 us
  between operations: 1.78 us -> 0.78 us
    ppermute x20 -> x4, starting transfers between devices: 40.1 us -> 7.14 us  [the longest x1 4.45 us: body(): got_q = lax.ppermute(to_q, 'lat', swaps(lat_total, 1))]
    pallas_call x0 -> x4, Pallas kernels: none -> 15.6 us  [the longest x1 9.64 us: body(): pl.pallas_call(step_kernel, in_specs=[smem] + [vmem] * 7, out_specs=[vmem...]
    gather x15 -> x0, local copies, waits for them, and re-layouts: 9.16 us -> none  [the longest x14 8.39 us: select_rows(): return jnp.where(occupied[:, None], field[chosen_rows], 0.0)]
    scatter x8 -> x0, other arithmetic: 7.08 us -> none  [the longest x4 3.62 us: body(): river_depth = river_depth.at[target].set(results[0], mode='drop')]
    unnamed x23 -> x14, local copies, waits for them, and re-layouts: 5.28 us -> 0.03 us
    div x40 -> x0, other arithmetic: 4.43 us -> none  [face_flow(): return driven / resisted]
    ppermute x20 -> x4, waiting for transfers between devices: 0.05 us -> 3.92 us  [the longest x1 3.91 us: body(): got_b = lax.ppermute(to_b, 'lon', ring)]
    add x36 -> x0, other arithmetic: 3.35 us -> none  [the longest x31 2.88 us: reach_update(): water_level = river_bed + river_depth]
  transfers between devices with their start and end apart: 20 -> 4, of which waited for: 0 -> 1; matrix products, arithmetic and copies ran while one was open for 42% -> 0% of each run, Pallas kernels for 0% -> 11%
where the time goes in v1:
time: 27.7 us; the launch traced here: 27.5 us
  Pallas kernels  15.6 us (56%)
  starting transfers between devices  7.14 us (26%)
  waiting for transfers between devices  3.92 us (14%)
  between operations  0.78 us (3%)
    pallas_call x1, Pallas kernels, body(): pl.pallas_call(step_kernel, in_specs=[smem] + [vmem] * 7, out_specs=[vmem...  9.64 us
    ppermute x1, starting transfers between devices, body(): got_q = lax.ppermute(to_q, 'lat', swaps(lat_total, 1))  4.45 us
    ppermute x1, waiting for transfers between devices, body(): got_b = lax.ppermute(to_b, 'lon', ring)  3.91 us
    pallas_call x1, Pallas kernels, body(): pl.pallas_call(own_kernel, in_specs=[smem] + [vmem] * 5, out_specs=[smem]...  2.97 us
    pallas_call x1, Pallas kernels, body(): pl.pallas_call(rows_kernel, in_specs=[hbm] * 7, out_specs=[vmem, vmem], o...  1.62 us
    pallas_call x1, Pallas kernels, body(): pl.pallas_call(pack_kernel, in_specs=[vmem] * 8, out_specs=[vmem] * 5, ou...  1.4 us
    ppermute x1, starting transfers between devices, body(): got_a = lax.ppermute(to_a, 'lon', swaps(lon_total, 0))  1.28 us
    ppermute x1, starting transfers between devices, body(): got_b = lax.ppermute(to_b, 'lon', ring)  1.17 us
  transfers between devices with their start and end apart: 4, of which 1 were waited for; matrix products, arithmetic and copies ran while one was open for 0% of the time, Pallas kernels for 11%

profile of v1, /device:TPU:11, one launch (start us, length us, event | category | flops | bytes accessed | tf_op | source)
XLA Modules:
  0.0 27.5 jit_solution(10018101904631920377)
XLA Ops:
  0.6 0.0 copy-start
  0.6 0.0 copy-start.1
  0.7 0.0 copy-start.2
  0.7 0.0 copy-start.3
  0.7 0.0 copy-start.4
  0.7 1.6 %rims.1 = (f32[56,128]{1,0:T(8,128)}, f32[56,128]{1,0:T(8,128)}) custom-call(s32[256]{0:T(256)} %bitcast.1, f32[256,128]{1,0:T(8,128)} %refs_0_.1, f32[256,128]{1,0:T(8,128)} %ground_ref.3, f32[256,128]{1,0:T(8,128)} %rough_ref.1, f32[256,128]{1,0:T(8,128)} %refs_3_.1, s32[256,128]{1,0:T(8,128)} %refs_4_.1, s32[256,128]{1,0:T(8,128)} %bank_ref.3), custom_call_target="tpu_custom_call" | custom-call | tf_op jit(solution)/shard_map/rims/pallas_call | solution.py:479
  2.3 0.0 copy-start.6
  2.3 0.2 collective-permute-start
  2.6 4.5 %collective-permute-start.1 = (f32[56,128]{1,0:T(8,128)}, f32[56,128]{1,0:T(8,128)S(1)}, u32[]{:S(2)}, u32[]{:S(2)}) collective-permute-start(f32[56,128]{1,0:T(8,128)} %get-tuple-element.23), channel_id=1, source_target_pairs={{1,2},{2,1},{5,6},{6,5},{9,10},{10,9},{13,14},{14,13},{17,18},{18,... | collective-permute-start | bytes 86024 | tf_op jit(solution)/shard_map/ppermute | solution.py:494
  7.0 0.0 copy-done
  7.0 0.0 copy-done.1
  7.0 0.0 copy-done.2
  7.0 0.0 copy-done.3
  7.1 0.0 copy-done.4
  7.1 0.0 copy-done.6
  7.1 3.0 %own_reaches.1 = (s32[128]{0:T(128)S(1)}, f32[6,72,128]{2,1,0:T(8,128)S(1)}, f32[280,128]{1,0:T(8,128)S(1)}, f32[280,128]{1,0:T(8,128)S(1)}, f32[264,128]{1,0:T(8,128)S(1)}, /*index=5*/f32[8,128]{1,0:T(8,128)S(1)}) custom-call(s32[256]{0:T(256)S(1)} %bitcast.2, f32[256,128]{1,0:T(8,128)S(1)} %copy-done.2, f32[256,128]{1,0:T(8,128)S(1)} %copy-done, ...), custom_call_target="tpu_custom_call" | custom-call | tf_op jit(solution)/shard_map/own_reaches/pallas_call | solution.py:497
  10.1 0.0 collective-permute-done.p_ref
  10.1 0.0 collective-permute-done.1.q_ref
  10.1 1.4 %pack.1 = (f32[160,128]{1,0:T(8,128)S(1)}, f32[160,128]{1,0:T(8,128)S(1)}, f32[3,280,128]{2,1,0:T(8,128)S(1)}, f32[6,72,128]{2,1,0:T(8,128)S(1)}, f32[280,128]{1,0:T(8,128)S(1)}) custom-call(f32[256,128]{1,0:T(8,128)S(1)} %copy-done, f32[256,128]{1,0:T(8,128)S(1)} %copy-done.5, f32[6,72,128]{2,1,0:T(8,128)S(1)} %get-tuple-element.18.own_slot, ...), custom_call_target="tpu_custom_call" | custom-call | tf_op jit(solution)/shard_map/pack/pallas_call | solution.py:517
  11.5 1.3 %collective-permute-start.2 = (f32[160,128]{1,0:T(8,128)S(1)}, f32[160,128]{1,0:T(8,128)S(1)}, u32[]{:S(2)}, u32[]{:S(2)}) collective-permute-start(f32[160,128]{1,0:T(8,128)S(1)} %get-tuple-element.28), channel_id=1, source_target_pairs={{0,4},{8,12},{16,20},{24,28},{4,0},{12,8},{20,16},{28,24},{1,5},{9... | collective-permute-start | bytes 245768 | tf_op jit(solution)/shard_map/ppermute | solution.py:532
  12.8 1.2 %collective-permute-start.3 = (f32[160,128]{1,0:T(8,128)S(1)}, f32[160,128]{1,0:T(8,128)S(1)}, u32[]{:S(2)}, u32[]{:S(2)}) collective-permute-start(f32[160,128]{1,0:T(8,128)S(1)} %get-tuple-element.29), channel_id=1, source_target_pairs={{4,8},{12,16},{20,24},{8,4},{16,12},{24,20},{28,0},{0,28},{5,9},{1... | collective-permute-start | bytes 245768 | tf_op jit(solution)/shard_map/ppermute | solution.py:533
  14.0 0.0 collective-permute-done.2.a_ref
  14.0 3.9 %collective-permute-done.3.b_ref = f32[160,128]{1,0:T(8,128)S(1)} collective-permute-done((f32[160,128]{1,0:T(8,128)S(1)}, f32[160,128]{1,0:T(8,128)S(1)}, u32[]{:S(2)}, u32[]{:S(2)}) %collective-permute-start.3) | collective-permute-done | bytes 81952 | tf_op jit(solution)/shard_map/ppermute | solution.py:533
  17.9 9.6 %steps.1 = (f32[256,128]{1,0:T(8,128)}, f32[256,128]{1,0:T(8,128)}, f32[256,128]{1,0:T(8,128)}, f32[256,128]{1,0:T(8,128)}) custom-call(s32[128]{0:T(128)S(1)} %get-tuple-element.17.rows_ref, f32[3,280,128]{2,1,0:T(8,128)S(1)} %get-tuple-element.24.flood_ref, f32[6,72,128]{2,1,0:T(8,128)S(1)} %get-tuple-element.25.slot_ref, ...), custom_call_target="tpu_custom_call" | custom-call | tf_op jit(solution)/shard_map/steps/pallas_call | solution.py:536
  (2 shorter events, 0.0 us)
Async XLA Ops:
  0.6 6.4 %copy-start = (f32[256,128]{1,0:T(8,128)S(1)}, f32[256,128]{1,0:T(8,128)}, u32[]{:S(2)}) copy-start(f32[256,128]{1,0:T(8,128)} %ground_ref.3) | copy-start | bytes 393220
  0.6 6.4 %copy-start.1 = (s32[256,128]{1,0:T(8,128)S(1)}, s32[256,128]{1,0:T(8,128)}, u32[]{:S(2)}) copy-start(s32[256,128]{1,0:T(8,128)} %bank_ref.3) | copy-start | bytes 393220
  0.7 6.4 %copy-start.2 = (f32[256,128]{1,0:T(8,128)S(1)}, f32[256,128]{1,0:T(8,128)}, u32[]{:S(2)}) copy-start(f32[256,128]{1,0:T(8,128)} %refs_0_.1) | copy-start | bytes 393220
  0.7 6.4 %copy-start.3 = (f32[256,128]{1,0:T(8,128)S(1)}, f32[256,128]{1,0:T(8,128)}, u32[]{:S(2)}) copy-start(f32[256,128]{1,0:T(8,128)} %refs_3_.1) | copy-start | bytes 393220
  0.7 6.4 %copy-start.4 = (s32[256,128]{1,0:T(8,128)S(1)}, s32[256,128]{1,0:T(8,128)}, u32[]{:S(2)}) copy-start(s32[256,128]{1,0:T(8,128)} %refs_4_.1) | copy-start | bytes 393220
  2.3 4.8 %copy-start.6 = (s32[256,1]{0,1:T(1,128)S(1)}, s32[256,1]{0,1:T(1,128)}, u32[]{:S(2)}) copy-start(s32[256,1]{0,1:T(1,128)} %param.11) | copy-start | bytes 3076
  2.3 7.7 %collective-permute-start = (f32[56,128]{1,0:T(8,128)}, f32[56,128]{1,0:T(8,128)S(1)}, u32[]{:S(2)}, u32[]{:S(2)}) collective-permute-start(f32[56,128]{1,0:T(8,128)} %get-tuple-element.22), channel_id=1, source_target_pairs={{0,1},{2,3},{1,0},{3,2},{4,5},{6,7},{5,4},{7,6},{8,9},{10,11},{9,8... | collective-permute-start | bytes 86024 | tf_op jit(solution)/shard_map/ppermute | solution.py:493
  2.6 7.5 %copy-start.5 = (f32[256,128]{1,0:T(8,128)S(1)}, f32[256,128]{1,0:T(8,128)}, u32[]{:S(2)}) copy-start(f32[256,128]{1,0:T(8,128)} %rough_ref.1) | copy-start | bytes 393220
  2.6 7.5 %collective-permute-start.1 = (f32[56,128]{1,0:T(8,128)}, f32[56,128]{1,0:T(8,128)S(1)}, u32[]{:S(2)}, u32[]{:S(2)}) collective-permute-start(f32[56,128]{1,0:T(8,128)} %get-tuple-element.23), channel_id=1, source_target_pairs={{1,2},{2,1},{5,6},{6,5},{9,10},{10,9},{13,14},{14,13},{17,18},{18,... | collective-permute-start | bytes 86024 | tf_op jit(solution)/shard_map/ppermute | solution.py:494
  11.5 2.5 %collective-permute-start.2 = (f32[160,128]{1,0:T(8,128)S(1)}, f32[160,128]{1,0:T(8,128)S(1)}, u32[]{:S(2)}, u32[]{:S(2)}) collective-permute-start(f32[160,128]{1,0:T(8,128)S(1)} %get-tuple-element.28), channel_id=1, source_target_pairs={{0,4},{8,12},{16,20},{24,28},{4,0},{12,8},{20,16},{28,24},{1,5},{9... | collective-permute-start | bytes 245768 | tf_op jit(solution)/shard_map/ppermute | solution.py:532
  12.8 5.1 %collective-permute-start.3 = (f32[160,128]{1,0:T(8,128)S(1)}, f32[160,128]{1,0:T(8,128)S(1)}, u32[]{:S(2)}, u32[]{:S(2)}) collective-permute-start(f32[160,128]{1,0:T(8,128)S(1)} %get-tuple-element.29), channel_id=1, source_target_pairs={{4,8},{12,16},{20,24},{8,4},{16,12},{24,20},{28,0},{0,28},{5,9},{1... | collective-permute-start | bytes 245768 | tf_op jit(solution)/shard_map/ppermute | solution.py:533

commit v2 on v1

v2 whole, which is shorter than its diff:
```python
import jax
import jax.numpy as jnp
from jax import lax
from jax.experimental import pallas as pl
from jax.experimental.pallas import tpu as pltpu
from jax.sharding import PartitionSpec as P

SUB = 8
STEPS = 4

GRAVITY = 9.81
CELL_SIZE = 90.0
TIME_STEP = 10.0
SHALLOW = 0.1
EXCHANGE = 0.01
CHANNEL_MANNING = 0.035

RIM = 8
COLS = SUB * (STEPS - 2)
DURATION = TIME_STEP / SUB
SURFACE, GROUND, ROUGH = range(3)
FLOOD_FIELDS = 3
LEVEL, FLUX, BED, WIDTH, GAIN, LIVE = range(6)
SLOT_FIELDS = 6
TOP, DRIVE, FRICTION, FEED, WATER = range(6, 11)
BATCH = 72
ROWS_AT_ONCE = 64
TILES_AT_ONCE = 34
FLOOD_AT_ONCE = 34
UNPACK_AT_ONCE = 20
SUBS_AT_ONCE = 8
FIRST_AT_ONCE = 7


def lanes(shape):
    return lax.broadcasted_iota(jnp.int32, shape, 1)


def sublanes(shape):
    return lax.broadcasted_iota(jnp.int32, shape, 0)


def east_of(field):
    return pltpu.roll(field, field.shape[1] - 1, 1)


def face(flow, here, there, top, drive, friction):
    height = jnp.maximum(here, there) - top
    driven = flow - drive * height * (there - here)
    spread = jnp.exp(jnp.log(height * height + SHALLOW * SHALLOW) * (-7.0 / 6.0))
    resisted = 1.0 + friction * jnp.abs(flow) * spread
    return driven * pl.reciprocal(resisted, approx=True)


def first_face(here, there, top, drive):
    height = jnp.maximum(here, there) - top
    return -(drive * height * (there - here))


def reach_constants(bed, width):
    top = jnp.maximum(bed, east_of(bed))
    breadth = 0.5 * (width + east_of(width))
    inner = lanes(bed.shape) < bed.shape[1] - 1
    drive = jnp.where(inner, (GRAVITY * DURATION / CELL_SIZE) * breadth, 0.0)
    friction = jnp.where(
        inner, (GRAVITY * DURATION * CHANNEL_MANNING * CHANNEL_MANNING) / breadth, 0.0
    )
    feed = (DURATION / CELL_SIZE) / width
    return top, drive, friction, feed


def west_of(field):
    return pltpu.roll(field, 1, 1)


def advanced(level, west, flux, surface, feed):
    transfer = (EXCHANGE * DURATION) * (level - surface)
    return level + ((west - flux) * feed - transfer), transfer


def first_reaches(level, surface, constants):
    top, drive, friction, feed = constants
    west_faces = [west_of(value) for value in (top, drive, friction)]
    flux = first_face(level, east_of(level), top, drive)
    west = first_face(west_of(level), level, west_faces[0], west_faces[1])
    level, gathered = advanced(level, west, flux, surface, feed)

    def substep(_, state):
        level, west, flux, gathered = state
        west = face(west, west_of(level), level, *west_faces)
        flux = face(flux, level, east_of(level), top, drive, friction)
        level, transfer = advanced(level, west, flux, surface, feed)
        return level, west, flux, gathered + transfer

    state = repeated(SUB - 1, FIRST_AT_ONCE, substep, (level, west, flux, gathered))
    return state[0], state[2], state[3]


def odd_position(axis):
    return lax.rem(lax.axis_index(axis), 2)


def repeated(count, unroll, step, carry):
    if unroll >= count:
        for i in range(count):
            carry = step(i, carry)
        return carry

    def some(block, carry):
        for j in range(unroll):
            carry = step(block * unroll + j, carry)
        return carry

    return lax.fori_loop(0, count // unroll, some, carry)


def each_row(count, visit, unroll=ROWS_AT_ONCE):
    repeated(count, unroll, lambda i, carry: (visit(i), carry)[1], 0)


def row_of(tile):
    return tile * RIM if isinstance(tile, int) else pl.multiple_of(tile * RIM, RIM)


def each_tile(count, visit, unroll):
    repeated(count, unroll, lambda i, carry: (visit(row_of(i)), carry)[1], 0)


def rows_kernel(mask_hbm, *refs):
    fields, outs, (reals, classes, mask_ref, sems) = refs[:6], refs[6:8], refs[8:]
    rows = mask_hbm.shape[0]
    northern = odd_position("lat") == 0
    copies = [pltpu.make_async_copy(mask_hbm, mask_ref, sems.at[0])]
    for k, field in enumerate(fields):
        for side, start in enumerate((0, rows - RIM)):
            to = reals.at[side, k] if k < 4 else classes.at[side, k - 4]
            copies.append(
                pltpu.make_async_copy(field.at[pl.ds(start, RIM)], to, sems.at[1 + 2 * k + side])
            )
    for copy in copies:
        copy.start()
    for copy in copies:
        copy.wait()
    shape = reals.shape[2:]
    row = sublanes(shape)

    def rims(side, start):
        depth, ground, rough, river = [reals[side, k] for k in range(4)]
        width, bank = classes[side, 0], classes[side, 1]
        live = jnp.zeros(shape, jnp.float32)
        for j in range(RIM):
            live = jnp.where(row == j, mask_ref[start + j].astype(jnp.float32), live)
        bed = ground - (1.0 + 0.5 * bank.astype(jnp.float32))
        wide = 8.0 + 9.0 * width.astype(jnp.float32)
        return [ground + depth, ground, rough, bed + river, bed, wide, live]

    for k, (low, high) in enumerate(zip(rims(0, 0), rims(1, rows - RIM))):
        outs[0][RIM * k : RIM * (k + 1), :] = jnp.where(northern, high, low)
        outs[1][RIM * k : RIM * (k + 1), :] = jnp.where(northern, low, high)


def fill_list(mask_ref, rows_ref):
    rows, room = mask_ref.shape[0], rows_ref.shape[0]
    beyond = rows + 2 * RIM
    batch = 16

    def clear(i):
        rows_ref[i] = beyond

    each_row(room, clear, 16)

    def enter(block, count):
        first = block * batch
        bits = [mask_ref[first + j] for j in range(batch)]
        places = []
        for bit in bits:
            places.append(count)
            count = count + bit
        for j, place in enumerate(places):
            rows_ref[place] = first + (j + RIM)
        return count

    count = lax.fori_loop(0, rows // batch, enter, jnp.int32(0))
    rows_ref[count] = beyond


def own_kernel(
    mask_ref, depth_ref, ground_ref, rough_ref, river_ref, width_ref, bank_ref,
    rows_ref, flat_ref, gain_ref, level_ref, listed_ref,
    bed_ref, wide_ref,
):
    rows, cols = depth_ref.shape
    slots = rows // 4
    tail, ext, total = rows + RIM, rows + 2 * RIM, slots + RIM
    base = FLOOD_FIELDS * ext
    fill_list(mask_ref, rows_ref)

    def prepare(t):
        at = pl.ds(t, RIM)
        ground = ground_ref[at, :]
        bed = ground - (1.0 + 0.5 * bank_ref[at, :].astype(jnp.float32))
        flat_ref[pl.ds(t + (SURFACE * ext + RIM), RIM), :] = ground + depth_ref[at, :]
        flat_ref[pl.ds(t + (GROUND * ext + RIM), RIM), :] = ground
        flat_ref[pl.ds(t + (ROUGH * ext + RIM), RIM), :] = rough_ref[at, :]
        level_ref[at, :] = bed + river_ref[at, :]
        bed_ref[at, :] = bed
        wide_ref[at, :] = 8.0 + 9.0 * width_ref[at, :].astype(jnp.float32)
        gain_ref[at, :] = jnp.zeros((RIM, cols), jnp.float32)

    each_tile(rows // RIM, prepare, TILES_AT_ONCE)
    zero = jnp.zeros((RIM, cols), jnp.float32)
    for t in range(rows, ext + RIM, RIM):
        gain_ref[t : t + RIM, :] = zero
    level_ref[rows:tail, :] = zero
    bed_ref[rows:tail, :] = zero
    wide_ref[rows:tail, :] = zero + 1.0
    lane = lanes((RIM, cols))

    def gather(i):
        e = rows_ref[i]
        own = e - RIM
        listed_ref[...] = jnp.where(lane == cols - slots + i, e.astype(jnp.float32), listed_ref[...])
        to = base + i
        live = jnp.where(own < rows, 1.0, 0.0)
        own = jnp.minimum(own, rows)
        flat_ref[pl.ds(to + LEVEL * total, 1), :] = level_ref[pl.ds(own, 1), :]
        flat_ref[pl.ds(to + BED * total, 1), :] = bed_ref[pl.ds(own, 1), :]
        flat_ref[pl.ds(to + WIDTH * total, 1), :] = wide_ref[pl.ds(own, 1), :]
        flat_ref[pl.ds(to + LIVE * total, 1), :] = jnp.full((1, cols), live, jnp.float32)
        surface = jnp.minimum(own, rows - 1) + (SURFACE * ext + RIM)
        flat_ref[pl.ds(to + GAIN * total, 1), :] = flat_ref[pl.ds(surface, 1), :]

    listed_ref[...] = zero
    each_row(slots, gather)

    def part(field):
        return slice(base + field * total, base + field * total + slots)

    width = flat_ref[part(WIDTH), :]
    level, flux, gathered = first_reaches(
        flat_ref[part(LEVEL), :],
        flat_ref[part(GAIN), :],
        reach_constants(flat_ref[part(BED), :], width),
    )
    flat_ref[part(LEVEL), :] = level
    flat_ref[part(FLUX), :] = flux
    live = flat_ref[part(LIVE), :] > 0.0
    flat_ref[part(GAIN), :] = jnp.where(live, gathered * (width / CELL_SIZE), 0.0)

    def spread(i):
        gain_ref[pl.ds(rows_ref[i], 1), :] = flat_ref[pl.ds(base + GAIN * total + i, 1), :]

    each_row(slots, spread)


def pack_kernel(
    own_flat, own_gain, listed_ref, p_ref, q_ref,
    flat_ref, gain_ref, a_ref, b_ref,
):
    del own_flat, own_gain
    cols = a_ref.shape[1]
    ext = gain_ref.shape[0] - RIM
    rows = ext - 2 * RIM
    slots = rows // 4
    tail, total = rows + RIM, slots + RIM
    base = FLOOD_FIELDS * ext
    half = RIM // 2
    northern = odd_position("lat") == 0
    p, q = p_ref[...], q_ref[...]
    north = jnp.where(northern, p, q)
    south = jnp.where(northern, q, p)

    def rim(block, k):
        return block[RIM * k : RIM * (k + 1)]

    def ends(k):
        return jnp.concatenate([rim(south, k)[half:], rim(north, k)[:half]], axis=0)

    def part(field):
        start = base + field * total + slots
        return slice(start, start + RIM)

    bed, width = ends(4), ends(5)
    level, flux, gathered = first_reaches(ends(3), ends(0), reach_constants(bed, width))
    gained = jnp.where(ends(6) > 0.0, gathered * (width / CELL_SIZE), 0.0)
    for field, value in (
        (LEVEL, level), (FLUX, flux), (BED, bed), (WIDTH, width), (GAIN, gained), (LIVE, ends(6)),
    ):
        flat_ref[part(field), :] = value
    for k in range(FLOOD_FIELDS):
        flat_ref[k * ext : k * ext + RIM, :] = rim(south, k)
        flat_ref[k * ext + tail : (k + 1) * ext, :] = rim(north, k)
    gain_ref[half:RIM, :] = gained[:half]
    gain_ref[tail : tail + half, :] = gained[half:]

    groups = cols // COLS
    group = lanes((RIM, cols)) // COLS
    eastern = odd_position("lon") == 0
    tiles = (base + SLOT_FIELDS * total) // RIM
    turns = []
    for start in (jnp.where(eastern, cols - COLS, 0), jnp.where(eastern, 0, cols - COLS)):
        turns.append([lax.rem(cols + COLS * g - start, cols) for g in range(groups)])

    def pack(m, used):
        block_a = block_b = listed_ref[...]
        for g in range(used):
            source = flat_ref[pl.ds(row_of(m * groups + g), RIM), :]
            block_a = jnp.where(group == g, pltpu.roll(source, turns[0][g], 1), block_a)
            block_b = jnp.where(group == g, pltpu.roll(source, turns[1][g], 1), block_b)
        to = pl.ds(row_of(m), RIM)
        a_ref[to, :] = block_a
        b_ref[to, :] = block_b

    each_row(tiles // groups, lambda m: pack(m, groups), UNPACK_AT_ONCE)
    pack(tiles // groups, tiles % groups)


def step_kernel(
    rows_ref, flat_ref, gain_ref, level_ref, bank_ref, a_ref, b_ref,
    depth_out, river_out, east_out, north_out,
    own_ref, side_ref, state, side_gain, own_gain,
    flow_ref, fixed_ref, river_ref, list_rows, west_rows, east_rows, sems,
):
    rows, cols = depth_out.shape
    slots = rows // 4
    tail, ext, total = rows + RIM, rows + 2 * RIM, slots + RIM
    base = FLOOD_FIELDS * ext
    half = RIM // 2
    lat_number, lat_total = lax.axis_index("lat"), lax.axis_size("lat")
    eastern = odd_position("lon") == 0
    lists = a_ref.shape[0] - RIM
    zero = jnp.zeros((RIM, cols), jnp.float32)

    list_a, list_b = a_ref[lists : lists + RIM, :], b_ref[lists : lists + RIM, :]
    list_rows[0] = jnp.where(eastern, list_a, list_b).astype(jnp.int32)
    list_rows[1] = jnp.where(eastern, list_b, list_a).astype(jnp.int32)
    one = pltpu.make_async_copy(list_rows.at[0, 0], east_rows, sems.at[0])
    two = pltpu.make_async_copy(list_rows.at[1, 0], west_rows, sems.at[1])
    one.start()
    two.start()

    groups = cols // COLS
    lane = lanes((RIM, cols))
    low = lane < cols // 2
    use_a = low == eastern
    turns = []
    for to in (jnp.where(eastern, 0, cols - COLS), jnp.where(eastern, cols - COLS, 0)):
        turns.append([lax.rem(cols + to - COLS * g, cols) for g in range(groups)])

    def unpack(m):
        at = pl.ds(row_of(m), RIM)
        block_a, block_b = a_ref[at, :], b_ref[at, :]
        for g in range(groups):
            from_a = pltpu.roll(block_a, turns[0][g], 1)
            from_b = pltpu.roll(block_b, turns[1][g], 1)
            to = pl.ds(row_of(m * groups + g), RIM)
            side_ref[to, :] = jnp.where(use_a, from_a, from_b)

    each_row(a_ref.shape[0] // RIM, unpack, UNPACK_AT_ONCE)

    def copy_in(t):
        at = pl.ds(t, RIM)
        own_ref[at, :] = flat_ref[at, :]
        own_gain[at, :] = gain_ref[at, :]
        for k in range(2):
            side_gain[k, at, :] = zero

    each_tile(ext // RIM, copy_in, TILES_AT_ONCE)
    own_ref[ext : ext + RIM, :] = zero

    def copy_slots(t):
        values = []
        for field in range(SLOT_FIELDS):
            own = flat_ref[pl.ds(base + field * total + t, RIM), :]
            side = side_ref[pl.ds(base + field * total + t, RIM), :]
            state[field, pl.ds(t, RIM), :] = own
            state[field, pl.ds(total + t, RIM), :] = side
            values.append((own, side))
        for j in range(2):
            constants = reach_constants(values[BED][j], values[WIDTH][j])
            for field, value in zip((TOP, DRIVE, FRICTION, FEED), constants):
                state[field, pl.ds(j * total + t, RIM), :] = value

    each_tile(total // RIM, copy_slots, TILES_AT_ONCE)
    one.wait()
    two.wait()
    first = cols - slots

    def spread_side():
        def visit(i):
            line = state[GAIN, pl.ds(total + i, 1), :]
            side_gain[0, pl.ds(east_rows[first + i], 1), :] = line
            side_gain[1, pl.ds(west_rows[first + i], 1), :] = line

        each_row(slots, visit)
        start = total + slots
        for k in range(2):
            side_gain[k, half:RIM, :] = state[GAIN, start : start + half, :]
            side_gain[k, tail : tail + half, :] = state[GAIN, start + half : start + RIM, :]

    def spread_own():
        def visit(i):
            own_gain[pl.ds(rows_ref[i], 1), :] = state[GAIN, pl.ds(i, 1), :]

        each_row(slots, visit)
        own_gain[half:RIM, :] = state[GAIN, slots : slots + half, :]
        own_gain[tail : tail + half, :] = state[GAIN, slots + half : total, :]

    spread_side()

    def reaches(start, size):
        at = slice(start, start + size)

        faces = [state[k, at, :] for k in (TOP, DRIVE, FRICTION)]
        west_faces = [west_of(value) for value in faces]
        surface, feed = state[WATER, at, :], state[FEED, at, :]

        def substep(_, carry):
            level, west, flux, gathered = carry
            west = face(west, west_of(level), level, *west_faces)
            flux = face(flux, level, east_of(level), *faces)
            level, transfer = advanced(level, west, flux, surface, feed)
            return level, west, flux, gathered + transfer

        level, flux = state[LEVEL, at, :], state[FLUX, at, :]
        start = (level, west_of(flux), flux, jnp.zeros_like(level))
        level, _, flux, gathered = repeated(SUB, SUBS_AT_ONCE, substep, start)
        state[LEVEL, at, :] = level
        state[FLUX, at, :] = flux
        live = state[LIVE, at, :] > 0.0
        state[GAIN, at, :] = jnp.where(live, gathered * (state[WIDTH, at, :] / CELL_SIZE), 0.0)

    last_lane = lane == cols - 1
    first_lane = lane == 0
    row = sublanes((RIM, cols))
    first_row = row == 0
    drive = GRAVITY * TIME_STEP / CELL_SIZE
    share = TIME_STEP / CELL_SIZE
    edge_south = jnp.where(lat_number == 0, RIM - 1, -1)
    edge_north = jnp.where(lat_number == lat_total - 1, tail - 1, -1)

    def pair_east(own, side):
        a, b = east_of(own), east_of(side)
        return jnp.where(last_lane, b, a), jnp.where(last_lane, a, b)

    def pair_west(own, side):
        a, b = pltpu.roll(own, 1, 1), pltpu.roll(side, 1, 1)
        return jnp.where(first_lane, b, a), jnp.where(first_lane, a, b)

    def constants_of(t):
        at = pl.ds(t, RIM)

        def read(field, shift):
            where = pl.ds(t + (field * ext + shift), RIM)
            return flat_ref[where, :], side_ref[where, :]

        ground, rough = read(GROUND, 0), read(ROUGH, 0)
        ground_north, rough_north = read(GROUND, 1), read(ROUGH, 1)
        ground_east, rough_east = pair_east(*ground), pair_east(*rough)
        weight = GRAVITY * TIME_STEP
        for j in range(2):
            fixed_ref[j, 0, at, :] = jnp.maximum(ground[j], ground_east[j])
            fixed_ref[j, 1, at, :] = weight * (rough[j] * rough_east[j])
            fixed_ref[j, 2, at, :] = jnp.maximum(ground[j], ground_north[j])
            fixed_ref[j, 3, at, :] = weight * (rough[j] * rough_north[j])

    def north_flow(j, t, here, step):
        at = pl.ds(t, RIM)
        north = (own_ref, side_ref)[j][pl.ds(t + 1, RIM), :]
        top = fixed_ref[j, 2, at, :]
        if step == 0:
            flow = first_face(here, north, top, drive)
        else:
            flow = face(flow_ref[j, 1, at, :], here, north, top, drive, fixed_ref[j, 3, at, :])
        e = t + row
        return jnp.where((e == edge_south) | (e == edge_north), 0.0, flow)

    def flood_tile(t, before, step):
        at = pl.ds(t, RIM)
        final = step == STEPS - 1
        here = own_ref[at, :], side_ref[at, :]
        east = pair_east(*here)
        to_east = []
        for j in range(2):
            top = fixed_ref[j, 0, at, :]
            if step == 0:
                flow = first_face(here[j], east[j], top, drive)
            else:
                flow = face(
                    flow_ref[j, 0, at, :], here[j], east[j], top, drive, fixed_ref[j, 1, at, :]
                )
            to_east.append(flow)
        west = pair_west(*to_east)
        after = []
        for j in range(1 if final else 2):
            to_north = north_flow(j, t, here[j], step)
            turned = pltpu.roll(to_north, 1, 0)
            south = jnp.where(first_row, before[j], turned)
            after.append(turned)
            new = here[j] + share * (west[j] - to_east[j] + south - to_north)
            if final:
                out = pl.ds(t - RIM, RIM)
                new = new + own_gain[at, :]
                depth_out[out, :] = new - flat_ref[pl.ds(t + GROUND * ext, RIM), :]
                east_out[out, :] = to_east[0]
                north_out[out, :] = to_north
                continue
            flow_ref[j, 0, at, :] = to_east[j]
            flow_ref[j, 1, at, :] = to_north
            if j == 0:
                own_ref[at, :] = new + own_gain[at, :]
            else:
                side_ref[at, :] = new + jnp.where(low, side_gain[0, at, :], side_gain[1, at, :])
        return tuple(after)

    def flood_step(step, tiles):
        final = step == STEPS - 1
        begin, count = (1, rows // RIM) if final else (0, ext // RIM)
        before = (zero, zero)
        if final:
            before = (pltpu.roll(north_flow(0, 0, own_ref[0:RIM, :], step), 1, 0),)

        repeated(count, tiles, lambda i, before: flood_tile(row_of(i + begin), before, step), before)

    each_tile(ext // RIM, constants_of, TILES_AT_ONCE)
    flood_step(0, FLOOD_AT_ONCE)
    middle = lanes((1, cols)) < cols // 2
    for step in range(1, STEPS):
        sides = step < STEPS - 1

        def water(i):
            state[WATER, pl.ds(i, 1), :] = own_ref[pl.ds(rows_ref[i], 1), :]
            if sides:
                state[WATER, pl.ds(total + i, 1), :] = jnp.where(
                    middle,
                    side_ref[pl.ds(east_rows[first + i], 1), :],
                    side_ref[pl.ds(west_rows[first + i], 1), :],
                )

        each_row(slots, water)
        for j, ref in enumerate((own_ref, side_ref)[: 2 if sides else 1]):
            start = j * total + slots
            state[WATER, start : start + half, :] = ref[half:RIM, :]
            state[WATER, start + half : start + RIM, :] = ref[tail : tail + half, :]
        for start in range(0, (2 if sides else 1) * total, BATCH):
            reaches(start, BATCH)
        spread_own()
        if sides:
            spread_side()
        flood_step(step, FLOOD_AT_ONCE)

    river_ref[0:rows, :] = level_ref[0:rows, :]

    def settle(i):
        own = jnp.minimum(rows_ref[i] - RIM, rows)
        river_ref[pl.ds(own, 1), :] = state[LEVEL, pl.ds(i, 1), :]

    each_row(slots, settle)

    def finish(t):
        at = pl.ds(t, RIM)
        ground = flat_ref[pl.ds(t + (GROUND * ext + RIM), RIM), :]
        bed = ground - (1.0 + 0.5 * bank_ref[at, :].astype(jnp.float32))
        river_out[at, :] = river_ref[at, :] - bed

    each_tile(rows // RIM, finish, TILES_AT_ONCE)


def swaps(count, first):
    pairs = [(i, i + 1) for i in range(first, count - 1, 2)]
    return pairs + [(b, a) for a, b in pairs]


def body(depth_init, ground, roughness, river_init, reach_mask, width_class, bank_class):
    rows, cols = ground.shape
    slots = rows // 4
    f32 = jnp.float32
    lon_total, lat_total = lax.axis_size("lon"), lax.axis_size("lat")
    mask = reach_mask.reshape(rows)
    smem = pl.BlockSpec(memory_space=pltpu.SMEM)
    vmem = pl.BlockSpec(memory_space=pltpu.VMEM)
    fields = (depth_init, ground, roughness, river_init, width_class, bank_class)
    ext, total = rows + 2 * RIM, slots + RIM
    used = FLOOD_FIELDS * ext + SLOT_FIELDS * total
    groups = cols // COLS
    message = -(-(used // RIM + slots // COLS) // groups) * RIM
    room = message * groups
    params = pltpu.CompilerParams(vmem_limit_bytes=48 * 1024 * 1024)

    hbm = pl.BlockSpec(memory_space=pltpu.HBM)
    rim_shape = jax.ShapeDtypeStruct((7 * RIM, cols), f32)
    to_p, to_q = pl.pallas_call(
        rows_kernel,
        in_specs=[hbm] * 7,
        out_specs=[vmem, vmem],
        out_shape=[rim_shape, rim_shape],
        scratch_shapes=[
            pltpu.VMEM((2, 4, RIM, cols), f32),
            pltpu.VMEM((2, 2, RIM, cols), jnp.int32),
            pltpu.SMEM((rows,), jnp.int32),
            pltpu.SemaphoreType.DMA((13,)),
        ],
        compiler_params=pltpu.CompilerParams(vmem_limit_bytes=63 * 1024 * 1024),
        name="rims",
    )(mask, *fields)
    got_q = lax.ppermute(to_q, "lat", swaps(lat_total, 1))
    got_p = lax.ppermute(to_p, "lat", swaps(lat_total, 0))
    flat_shape = jax.ShapeDtypeStruct((room, cols), f32)
    dense = jax.ShapeDtypeStruct((ext + RIM, cols), f32)
    row_list, own_flat, own_gain, level, listed = pl.pallas_call(
        own_kernel,
        in_specs=[smem] + [vmem] * 6,
        out_specs=[smem] + [vmem] * 4,
        out_shape=[
            jax.ShapeDtypeStruct((2 * slots,), jnp.int32),
            flat_shape,
            dense,
            jax.ShapeDtypeStruct((rows + RIM, cols), f32),
            jax.ShapeDtypeStruct((RIM, cols), f32),
        ],
        scratch_shapes=[pltpu.VMEM((rows + RIM, cols), f32)] * 2,
        compiler_params=params,
        name="own_reaches",
    )(mask, *fields)

    message_shape = jax.ShapeDtypeStruct((message, cols), f32)
    flat, gain, to_a, to_b = pl.pallas_call(
        pack_kernel,
        in_specs=[vmem] * 5,
        out_specs=[vmem] * 4,
        out_shape=[flat_shape, dense, message_shape, message_shape],
        input_output_aliases={0: 0, 1: 1},
        compiler_params=params,
        name="pack",
    )(own_flat, own_gain, listed, got_p, got_q)
    ring = swaps(lon_total, 1) + [(lon_total - 1, 0), (0, lon_total - 1)]
    got_a = lax.ppermute(to_a, "lon", swaps(lon_total, 0))
    got_b = lax.ppermute(to_b, "lon", ring)

    tile = jax.ShapeDtypeStruct((rows, cols), f32)
    return pl.pallas_call(
        step_kernel,
        in_specs=[smem] + [vmem] * 6,
        out_specs=[vmem] * 4,
        out_shape=[tile] * 4,
        scratch_shapes=[
            pltpu.VMEM((ext + RIM, cols), f32),
            pltpu.VMEM((room, cols), f32),
            pltpu.VMEM((WATER + 1, 2 * total, cols), f32),
            pltpu.VMEM((2, ext + RIM, cols), f32),
            pltpu.VMEM((ext + RIM, cols), f32),
            pltpu.VMEM((2, 2, ext, cols), f32),
            pltpu.VMEM((2, 4, ext, cols), f32),
            pltpu.VMEM((rows + RIM, cols), f32),
            pltpu.VMEM((2, RIM, cols), jnp.int32),
            pltpu.SMEM((cols,), jnp.int32),
            pltpu.SMEM((cols,), jnp.int32),
            pltpu.SemaphoreType.DMA((2,)),
        ],
        compiler_params=params,
        name="steps",
    )(row_list, flat, gain, level, bank_class, got_a, got_b)


def solution(mesh):
    grid = P("lat", "lon")
    return jax.shard_map(
        body,
        mesh=mesh,
        in_specs=(grid,) * 7,
        out_specs=(grid,) * 4,
        check_vma=False,
    )
```

time: 27.7 us -> 25.2 us (0.910)
  Pallas kernels: 15.6 us -> 13.3 us
    pallas_call x3, Pallas kernels: 14 us -> 11.6 us  [the longest x1 7.71 us: body(): pl.pallas_call(step_kernel, in_specs=[smem] + [vmem] * 6, out_specs=[vmem...]
  transfers between devices with their start and end apart: 4 -> 4, of which waited for: 1 -> 1; matrix products, arithmetic and copies ran while one was open for 0% -> 0% of each run, Pallas kernels for 11% -> 12%
where the time goes in v2:
time: 25.2 us; the launch traced here: 25 us
  Pallas kernels  13.3 us (53%)
  starting transfers between devices  7.01 us (28%)
  waiting for transfers between devices  3.92 us (16%)
  between operations  0.79 us (3%)
    pallas_call x1, Pallas kernels, body(): pl.pallas_call(step_kernel, in_specs=[smem] + [vmem] * 6, out_specs=[vmem...  7.71 us
    ppermute x1, starting transfers between devices, body(): got_q = lax.ppermute(to_q, 'lat', swaps(lat_total, 1))  4.32 us
    ppermute x1, waiting for transfers between devices, body(): got_b = lax.ppermute(to_b, 'lon', ring)  3.91 us
    pallas_call x1, Pallas kernels, body(): pl.pallas_call(own_kernel, in_specs=[smem] + [vmem] * 6, out_specs=[smem]...  3 us
    pallas_call x1, Pallas kernels, body(): pl.pallas_call(rows_kernel, in_specs=[hbm] * 7, out_specs=[vmem, vmem], o...  1.62 us
    ppermute x1, starting transfers between devices, body(): got_a = lax.ppermute(to_a, 'lon', swaps(lon_total, 0))  1.28 us
    ppermute x1, starting transfers between devices, body(): got_b = lax.ppermute(to_b, 'lon', ring)  1.17 us
    pallas_call x1, Pallas kernels, body(): pl.pallas_call(pack_kernel, in_specs=[vmem] * 5, out_specs=[vmem] * 4, ou...  0.93 us
  transfers between devices with their start and end apart: 4, of which 1 were waited for; matrix products, arithmetic and copies ran while one was open for 0% of the time, Pallas kernels for 12%

profile of v2, /device:TPU:11, one launch (start us, length us, event | category | flops | bytes accessed | tf_op | source)
XLA Modules:
  0.0 25.0 jit_solution(17170729435261691102)
XLA Ops:
  0.6 0.0 copy-start
  0.6 0.0 copy-start.1
  0.7 0.0 copy-start.2
  0.7 0.0 copy-start.3
  0.7 0.0 copy-start.4
  0.7 0.0 copy-start.5
  0.7 1.6 %rims.1 = (f32[56,128]{1,0:T(8,128)}, f32[56,128]{1,0:T(8,128)}) custom-call(s32[256]{0:T(256)} %bitcast.1, f32[256,128]{1,0:T(8,128)} %refs_0_.1, f32[256,128]{1,0:T(8,128)} %refs_1_.1, f32[256,128]{1,0:T(8,128)} %refs_2_.1, f32[256,128]{1,0:T(8,128)} %refs_3_.1, s32[256,128]{1,0:T(8,128)} %refs_4_.1, s32[256,128]{1,0:T(8,128)} %bank_ref.3), custom_call_target="tpu_custom_call" | custom-call | tf_op jit(solution)/shard_map/rims/pallas_call | solution.py:592
  2.3 0.0 copy-start.6
  2.3 0.2 collective-permute-start
  2.6 4.3 %collective-permute-start.1 = (f32[56,128]{1,0:T(8,128)}, f32[56,128]{1,0:T(8,128)S(1)}, u32[]{:S(2)}, u32[]{:S(2)}) collective-permute-start(f32[56,128]{1,0:T(8,128)} %get-tuple-element.20), channel_id=1, source_target_pairs={{1,2},{2,1},{5,6},{6,5},{9,10},{10,9},{13,14},{14,13},{17,18},{18,... | collective-permute-start | bytes 86024 | tf_op jit(solution)/shard_map/ppermute | solution.py:606
  6.9 0.0 copy-done
  6.9 0.0 copy-done.1
  6.9 0.0 copy-done.2
  6.9 0.0 copy-done.3
  6.9 0.0 copy-done.4
  7.0 3.0 %own_reaches.1 = (s32[128]{0:T(128)S(1)}, f32[1280,128]{1,0:T(8,128)S(1)}, f32[280,128]{1,0:T(8,128)S(1)}, f32[264,128]{1,0:T(8,128)S(1)}, f32[8,128]{1,0:T(8,128)S(1)}) custom-call(s32[256]{0:T(256)S(1)} %bitcast.2, f32[256,128]{1,0:T(8,128)S(1)} %copy-done.1, f32[256,128]{1,0:T(8,128)S(1)} %copy-done.2, f32[256,128]{1,0:T(8,128)S(1)} %copy-done.3, ...), custom_call_target="tpu_custom_call" | custom-call | tf_op jit(solution)/shard_map/own_reaches/pallas_call | solution.py:610
  10.0 0.0 collective-permute-done.p_ref
  10.0 0.0 collective-permute-done.1.q_ref
  10.0 0.9 %pack.1 = (f32[1280,128]{1,0:T(8,128)S(1)}, f32[280,128]{1,0:T(8,128)S(1)}, f32[160,128]{1,0:T(8,128)S(1)}, f32[160,128]{1,0:T(8,128)S(1)}) custom-call(f32[1280,128]{1,0:T(8,128)S(1)} %get-tuple-element.16.own_flat, f32[280,128]{1,0:T(8,128)S(1)} %get-tuple-element.17.own_gain, ...), custom_call_target="tpu_custom_call", output_to_operand_aliasing={{0}: (0, {}), {1}: (1, {})} | custom-call | tf_op jit(solution)/shard_map/pack/pallas_call | solution.py:627
  10.9 1.3 %collective-permute-start.2 = (f32[160,128]{1,0:T(8,128)S(1)}, f32[160,128]{1,0:T(8,128)S(1)}, u32[]{:S(2)}, u32[]{:S(2)}) collective-permute-start(f32[160,128]{1,0:T(8,128)S(1)} %get-tuple-element.24), channel_id=1, source_target_pairs={{0,4},{8,12},{16,20},{24,28},{4,0},{12,8},{20,16},{28,24},{1,5},{9... | collective-permute-start | bytes 245768 | tf_op jit(solution)/shard_map/ppermute | solution.py:637
  12.2 1.2 %collective-permute-start.3 = (f32[160,128]{1,0:T(8,128)S(1)}, f32[160,128]{1,0:T(8,128)S(1)}, u32[]{:S(2)}, u32[]{:S(2)}) collective-permute-start(f32[160,128]{1,0:T(8,128)S(1)} %get-tuple-element.25), channel_id=1, source_target_pairs={{4,8},{12,16},{20,24},{8,4},{16,12},{24,20},{28,0},{0,28},{5,9},{1... | collective-permute-start | bytes 245768 | tf_op jit(solution)/shard_map/ppermute | solution.py:638
  13.4 0.0 collective-permute-done.2.a_ref
  13.4 3.9 %collective-permute-done.3.b_ref = f32[160,128]{1,0:T(8,128)S(1)} collective-permute-done((f32[160,128]{1,0:T(8,128)S(1)}, f32[160,128]{1,0:T(8,128)S(1)}, u32[]{:S(2)}, u32[]{:S(2)}) %collective-permute-start.3) | collective-permute-done | bytes 81952 | tf_op jit(solution)/shard_map/ppermute | solution.py:638
  17.3 7.7 %steps.1 = (f32[256,128]{1,0:T(8,128)}, f32[256,128]{1,0:T(8,128)}, f32[256,128]{1,0:T(8,128)}, f32[256,128]{1,0:T(8,128)}) custom-call(s32[128]{0:T(128)S(1)} %get-tuple-element.15.rows_ref, f32[1280,128]{1,0:T(8,128)S(1)} %get-tuple-element.21.flat_ref, f32[280,128]{1,0:T(8,128)S(1)} %get-tuple-element.22.gain_ref, ...), custom_call_target="tpu_custom_call" | custom-call | tf_op jit(solution)/shard_map/steps/pallas_call | solution.py:641
  (2 shorter events, 0.0 us)
Async XLA Ops:
  0.6 6.3 %copy-start = (s32[256,128]{1,0:T(8,128)S(1)}, s32[256,128]{1,0:T(8,128)}, u32[]{:S(2)}) copy-start(s32[256,128]{1,0:T(8,128)} %bank_ref.3) | copy-start | bytes 393220
  0.6 6.3 %copy-start.1 = (f32[256,128]{1,0:T(8,128)S(1)}, f32[256,128]{1,0:T(8,128)}, u32[]{:S(2)}) copy-start(f32[256,128]{1,0:T(8,128)} %refs_0_.1) | copy-start | bytes 393220
  0.7 6.3 %copy-start.2 = (f32[256,128]{1,0:T(8,128)S(1)}, f32[256,128]{1,0:T(8,128)}, u32[]{:S(2)}) copy-start(f32[256,128]{1,0:T(8,128)} %refs_1_.1) | copy-start | bytes 393220
  0.7 6.3 %copy-start.3 = (f32[256,128]{1,0:T(8,128)S(1)}, f32[256,128]{1,0:T(8,128)}, u32[]{:S(2)}) copy-start(f32[256,128]{1,0:T(8,128)} %refs_2_.1) | copy-start | bytes 393220
  0.7 6.3 %copy-start.4 = (f32[256,128]{1,0:T(8,128)S(1)}, f32[256,128]{1,0:T(8,128)}, u32[]{:S(2)}) copy-start(f32[256,128]{1,0:T(8,128)} %refs_3_.1) | copy-start | bytes 393220
  0.7 6.3 %copy-start.5 = (s32[256,128]{1,0:T(8,128)S(1)}, s32[256,128]{1,0:T(8,128)}, u32[]{:S(2)}) copy-start(s32[256,128]{1,0:T(8,128)} %refs_4_.1) | copy-start | bytes 393220
  2.3 4.6 %copy-start.6 = (s32[256,1]{0,1:T(1,128)S(1)}, s32[256,1]{0,1:T(1,128)}, u32[]{:S(2)}) copy-start(s32[256,1]{0,1:T(1,128)} %param.11) | copy-start | bytes 3076
  2.3 7.6 %collective-permute-start = (f32[56,128]{1,0:T(8,128)}, f32[56,128]{1,0:T(8,128)S(1)}, u32[]{:S(2)}, u32[]{:S(2)}) collective-permute-start(f32[56,128]{1,0:T(8,128)} %get-tuple-element.19), channel_id=1, source_target_pairs={{0,1},{2,3},{1,0},{3,2},{4,5},{6,7},{5,4},{7,6},{8,9},{10,11},{9,8... | collective-permute-start | bytes 86024 | tf_op jit(solution)/shard_map/ppermute | solution.py:607
  2.6 7.4 %collective-permute-start.1 = (f32[56,128]{1,0:T(8,128)}, f32[56,128]{1,0:T(8,128)S(1)}, u32[]{:S(2)}, u32[]{:S(2)}) collective-permute-start(f32[56,128]{1,0:T(8,128)} %get-tuple-element.20), channel_id=1, source_target_pairs={{1,2},{2,1},{5,6},{6,5},{9,10},{10,9},{13,14},{14,13},{17,18},{18,... | collective-permute-start | bytes 86024 | tf_op jit(solution)/shard_map/ppermute | solution.py:606
  10.9 2.5 %collective-permute-start.2 = (f32[160,128]{1,0:T(8,128)S(1)}, f32[160,128]{1,0:T(8,128)S(1)}, u32[]{:S(2)}, u32[]{:S(2)}) collective-permute-start(f32[160,128]{1,0:T(8,128)S(1)} %get-tuple-element.24), channel_id=1, source_target_pairs={{0,4},{8,12},{16,20},{24,28},{4,0},{12,8},{20,16},{28,24},{1,5},{9... | collective-permute-start | bytes 245768 | tf_op jit(solution)/shard_map/ppermute | solution.py:637
  12.2 5.1 %collective-permute-start.3 = (f32[160,128]{1,0:T(8,128)S(1)}, f32[160,128]{1,0:T(8,128)S(1)}, u32[]{:S(2)}, u32[]{:S(2)}) collective-permute-start(f32[160,128]{1,0:T(8,128)S(1)} %get-tuple-element.25), channel_id=1, source_target_pairs={{4,8},{12,16},{20,24},{8,4},{16,12},{24,20},{28,0},{0,28},{5,9},{1... | collective-permute-start | bytes 245768 | tf_op jit(solution)/shard_map/ppermute | solution.py:638

commit v3 on v2

--- a/solution.py
+++ b/solution.py
@@ -23,12 +23,9 @@
 LEVEL, FLUX, BED, WIDTH, GAIN, LIVE = range(6)
 SLOT_FIELDS = 6
 TOP, DRIVE, FRICTION, FEED, WATER = range(6, 11)
-BATCH = 72
 ROWS_AT_ONCE = 64
 TILES_AT_ONCE = 34
-FLOOD_AT_ONCE = 34
 UNPACK_AT_ONCE = 20
-SUBS_AT_ONCE = 8
 FIRST_AT_ONCE = 7
 
 
@@ -160,27 +157,22 @@
 
 
 def fill_list(mask_ref, rows_ref):
-    rows, room = mask_ref.shape[0], rows_ref.shape[0]
+    rows = mask_ref.shape[0]
+    room = rows // 4
     beyond = rows + 2 * RIM
     batch = 16
 
-    def clear(i):
+    for i in range(room):
         rows_ref[i] = beyond
-
-    each_row(room, clear, 16)
-
-    def enter(block, count):
-        first = block * batch
+    count = jnp.int32(0)
+    for first in range(0, rows, batch):
         bits = [mask_ref[first + j] for j in range(batch)]
         places = []
         for bit in bits:
             places.append(count)
             count = count + bit
         for j, place in enumerate(places):
-            rows_ref[place] = first + (j + RIM)
-        return count
-
-    count = lax.fori_loop(0, rows // batch, enter, jnp.int32(0))
+            rows_ref[place] = first + j + RIM
     rows_ref[count] = beyond
 
 
@@ -209,6 +201,7 @@
 
     each_tile(rows // RIM, prepare, TILES_AT_ONCE)
     zero = jnp.zeros((RIM, cols), jnp.float32)
+    flat_ref[SURFACE * ext + tail : (SURFACE + 1) * ext, :] = zero
     for t in range(rows, ext + RIM, RIM):
         gain_ref[t : t + RIM, :] = zero
     level_ref[rows:tail, :] = zero
@@ -216,22 +209,20 @@
     wide_ref[rows:tail, :] = zero + 1.0
     lane = lanes((RIM, cols))
 
-    def gather(i):
+    listed = zero
+    for i in range(slots):
         e = rows_ref[i]
-        own = e - RIM
-        listed_ref[...] = jnp.where(lane == cols - slots + i, e.astype(jnp.float32), listed_ref[...])
+        own = jnp.minimum(e - RIM, rows)
+        listed = jnp.where(lane == cols - slots + i, e.astype(jnp.float32), listed)
         to = base + i
-        live = jnp.where(own < rows, 1.0, 0.0)
-        own = jnp.minimum(own, rows)
-        flat_ref[pl.ds(to + LEVEL * total, 1), :] = level_ref[pl.ds(own, 1), :]
-        flat_ref[pl.ds(to + BED * total, 1), :] = bed_ref[pl.ds(own, 1), :]
-        flat_ref[pl.ds(to + WIDTH * total, 1), :] = wide_ref[pl.ds(own, 1), :]
+        live = jnp.where(e < tail, 1.0, 0.0)
+        of, surface = pl.ds(own, 1), pl.ds(own + (SURFACE * ext + RIM), 1)
+        flat_ref[pl.ds(to + LEVEL * total, 1), :] = level_ref[of, :]
+        flat_ref[pl.ds(to + BED * total, 1), :] = bed_ref[of, :]
+        flat_ref[pl.ds(to + WIDTH * total, 1), :] = wide_ref[of, :]
         flat_ref[pl.ds(to + LIVE * total, 1), :] = jnp.full((1, cols), live, jnp.float32)
-        surface = jnp.minimum(own, rows - 1) + (SURFACE * ext + RIM)
-        flat_ref[pl.ds(to + GAIN * total, 1), :] = flat_ref[pl.ds(surface, 1), :]
-
-    listed_ref[...] = zero
-    each_row(slots, gather)
+        flat_ref[pl.ds(to + GAIN * total, 1), :] = flat_ref[surface, :]
+    listed_ref[...] = listed
 
     def part(field):
         return slice(base + field * total, base + field * total + slots)
@@ -415,16 +406,14 @@
         west_faces = [west_of(value) for value in faces]
         surface, feed = state[WATER, at, :], state[FEED, at, :]
 
-        def substep(_, carry):
-            level, west, flux, gathered = carry
+        level, flux = state[LEVEL, at, :], state[FLUX, at, :]
+        west, gathered = west_of(flux), jnp.zeros_like(level)
+        for _ in range(SUB):
             west = face(west, west_of(level), level, *west_faces)
             flux = face(flux, level, east_of(level), *faces)
             level, transfer = advanced(level, west, flux, surface, feed)
-            return level, west, flux, gathered + transfer
-
-        level, flux = state[LEVEL, at, :], state[FLUX, at, :]
-        start = (level, west_of(flux), flux, jnp.zeros_like(level))
-        level, _, flux, gathered = repeated(SUB, SUBS_AT_ONCE, substep, start)
+            gathered = gathered + transfer
+            yield
         state[LEVEL, at, :] = level
         state[FLUX, at, :] = flux
         live = state[LIVE, at, :] > 0.0
@@ -475,12 +464,15 @@
         e = t + row
         return jnp.where((e == edge_south) | (e == edge_north), 0.0, flow)
 
-    def flood_tile(t, before, step):
+    def flows(t, step):
         at = pl.ds(t, RIM)
         final = step == STEPS - 1
         here = own_ref[at, :], side_ref[at, :]
+        for j in range(1 if final else 2):
+            flow_ref[j, 1, at, :] = north_flow(j, t, here[j], step)
+        if final and t == 0:
+            return
         east = pair_east(*here)
-        to_east = []
         for j in range(2):
             top = fixed_ref[j, 0, at, :]
             if step == 0:
@@ -489,41 +481,58 @@
                 flow = face(
                     flow_ref[j, 0, at, :], here[j], east[j], top, drive, fixed_ref[j, 1, at, :]
                 )
-            to_east.append(flow)
+            flow_ref[j, 0, at, :] = flow
+
+    def update(t, before, step):
+        at = pl.ds(t, RIM)
+        final = step == STEPS - 1
+        to_east = flow_ref[0, 0, at, :], flow_ref[1, 0, at, :]
         west = pair_west(*to_east)
         after = []
         for j in range(1 if final else 2):
-            to_north = north_flow(j, t, here[j], step)
+            to_north = flow_ref[j, 1, at, :]
             turned = pltpu.roll(to_north, 1, 0)
             south = jnp.where(first_row, before[j], turned)
             after.append(turned)
-            new = here[j] + share * (west[j] - to_east[j] + south - to_north)
+            moved = share * (west[j] - to_east[j] + south - to_north)
             if final:
                 out = pl.ds(t - RIM, RIM)
-                new = new + own_gain[at, :]
+                new = own_ref[at, :] + moved + own_gain[at, :]
                 depth_out[out, :] = new - flat_ref[pl.ds(t + GROUND * ext, RIM), :]
                 east_out[out, :] = to_east[0]
                 north_out[out, :] = to_north
-                continue
-            flow_ref[j, 0, at, :] = to_east[j]
-            flow_ref[j, 1, at, :] = to_north
-            if j == 0:
-                own_ref[at, :] = new + own_gain[at, :]
+            elif j == 0:
+                own_ref[at, :] = own_ref[at, :] + moved + own_gain[at, :]
             else:
-                side_ref[at, :] = new + jnp.where(low, side_gain[0, at, :], side_gain[1, at, :])
-        return tuple(after)
-
-    def flood_step(step, tiles):
-        final = step == STEPS - 1
-        begin, count = (1, rows // RIM) if final else (0, ext // RIM)
-        before = (zero, zero)
-        if final:
-            before = (pltpu.roll(north_flow(0, 0, own_ref[0:RIM, :], step), 1, 0),)
-
-        repeated(count, tiles, lambda i, before: flood_tile(row_of(i + begin), before, step), before)
-
-    each_tile(ext // RIM, constants_of, TILES_AT_ONCE)
-    flood_step(0, FLOOD_AT_ONCE)
+                gain = jnp.where(low, side_gain[0, at, :], side_gain[1, at, :])
+                side_ref[at, :] = side_ref[at, :] + moved + gain
+        return after
+
+    def update_all(step):
+        if step == STEPS - 1:
+            before = (pltpu.roll(flow_ref[0, 1, 0:RIM, :], 1, 0),)
+            tiles = range(RIM, tail, RIM)
+        else:
+            before = (zero, zero)
+            tiles = range(0, ext, RIM)
+        for t in tiles:
+            before = update(t, before, step)
+
+    def settle():
+        river_ref[0:rows, :] = level_ref[0:rows, :]
+        for i in range(slots):
+            own = jnp.minimum(rows_ref[i] - RIM, rows)
+            river_ref[pl.ds(own, 1), :] = state[LEVEL, pl.ds(i, 1), :]
+        for t in range(0, rows, RIM):
+            at = pl.ds(t, RIM)
+            ground = flat_ref[pl.ds(t + (GROUND * ext + RIM), RIM), :]
+            bed = ground - (1.0 + 0.5 * bank_ref[at, :].astype(jnp.float32))
+            river_out[at, :] = river_ref[at, :] - bed
+
+    for t in range(0, ext, RIM):
+        constants_of(t)
+        flows(t, 0)
+    update_all(0)
     middle = lanes((1, cols)) < cols // 2
     for step in range(1, STEPS):
         sides = step < STEPS - 1
@@ -542,28 +551,23 @@
             start = j * total + slots
             state[WATER, start : start + half, :] = ref[half:RIM, :]
             state[WATER, start + half : start + RIM, :] = ref[tail : tail + half, :]
-        for start in range(0, (2 if sides else 1) * total, BATCH):
-            reaches(start, BATCH)
+
+        running = [reaches(start, total) for start in range(0, (2 if sides else 1) * total, total)]
+        tiles = list(range(0, ext if sides else tail, RIM))
+        share_of = -(-len(tiles) // SUB)
+        for substep in range(SUB):
+            for reach in running:
+                next(reach)
+            for t in tiles[substep * share_of : (substep + 1) * share_of]:
+                flows(t, step)
+        for reach in running:
+            next(reach, None)
         spread_own()
         if sides:
             spread_side()
-        flood_step(step, FLOOD_AT_ONCE)
-
-    river_ref[0:rows, :] = level_ref[0:rows, :]
-
-    def settle(i):
-        own = jnp.minimum(rows_ref[i] - RIM, rows)
-        river_ref[pl.ds(own, 1), :] = state[LEVEL, pl.ds(i, 1), :]
-
-    each_row(slots, settle)
-
-    def finish(t):
-        at = pl.ds(t, RIM)
-        ground = flat_ref[pl.ds(t + (GROUND * ext + RIM), RIM), :]
-        bed = ground - (1.0 + 0.5 * bank_ref[at, :].astype(jnp.float32))
-        river_out[at, :] = river_ref[at, :] - bed
-
-    each_tile(rows // RIM, finish, TILES_AT_ONCE)
+        else:
+            settle()
+        update_all(step)
 
 
 def swaps(count, first):
@@ -603,8 +607,8 @@
         compiler_params=pltpu.CompilerParams(vmem_limit_bytes=63 * 1024 * 1024),
         name="rims",
     )(mask, *fields)
+    got_p = lax.ppermute(to_p, "lat", swaps(lat_total, 0))
     got_q = lax.ppermute(to_q, "lat", swaps(lat_total, 1))
-    got_p = lax.ppermute(to_p, "lat", swaps(lat_total, 0))
     flat_shape = jax.ShapeDtypeStruct((room, cols), f32)
     dense = jax.ShapeDtypeStruct((ext + RIM, cols), f32)
     row_list, own_flat, own_gain, level, listed = pl.pallas_call(

time: 25.2 us -> 24.2 us (0.960)
  Pallas kernels: 13.3 us -> 12.2 us
    pallas_call x1, Pallas kernels: 7.71 us -> 7.05 us  [body(): pl.pallas_call(step_kernel, in_specs=[smem] + [vmem] * 6, out_specs=[vmem...]
    pallas_call x1, Pallas kernels: 3 us -> 2.65 us  [body(): pl.pallas_call(own_kernel, in_specs=[smem] + [vmem] * 6, out_specs=[smem]...]
  transfers between devices with their start and end apart: 4 -> 4, of which waited for: 1 -> 1; matrix products, arithmetic and copies ran while one was open for 0% -> 0% of each run, Pallas kernels for 12% -> 11%
where the time goes in v3:
time: 24.2 us; the launch traced here: 24 us
  Pallas kernels  12.2 us (50%)
  starting transfers between devices  7.01 us (29%)
  waiting for transfers between devices  3.92 us (16%)
  between operations  0.79 us (3%)
    pallas_call x1, Pallas kernels, body(): pl.pallas_call(step_kernel, in_specs=[smem] + [vmem] * 6, out_specs=[vmem...  7.05 us
    ppermute x1, starting transfers between devices, body(): got_q = lax.ppermute(to_q, 'lat', swaps(lat_total, 1))  4.32 us
    ppermute x1, waiting for transfers between devices, body(): got_b = lax.ppermute(to_b, 'lon', ring)  3.91 us
    pallas_call x1, Pallas kernels, body(): pl.pallas_call(own_kernel, in_specs=[smem] + [vmem] * 6, out_specs=[smem]...  2.65 us
    pallas_call x1, Pallas kernels, body(): pl.pallas_call(rows_kernel, in_specs=[hbm] * 7, out_specs=[vmem, vmem], o...  1.62 us
    ppermute x1, starting transfers between devices, body(): got_a = lax.ppermute(to_a, 'lon', swaps(lon_total, 0))  1.28 us
    ppermute x1, starting transfers between devices, body(): got_b = lax.ppermute(to_b, 'lon', ring)  1.17 us
    pallas_call x1, Pallas kernels, body(): pl.pallas_call(pack_kernel, in_specs=[vmem] * 5, out_specs=[vmem] * 4, ou...  0.93 us
  transfers between devices with their start and end apart: 4, of which 1 were waited for; matrix products, arithmetic and copies ran while one was open for 0% of the time, Pallas kernels for 11%

profile of v3, /device:TPU:11, one launch (start us, length us, event | category | flops | bytes accessed | tf_op | source)
XLA Modules:
  0.0 24.0 jit_solution(18093948756465351240)
XLA Ops:
  0.6 0.0 copy-start
  0.6 0.0 copy-start.1
  0.7 0.0 copy-start.2
  0.7 0.0 copy-start.3
  0.7 0.0 copy-start.4
  0.7 0.0 copy-start.5
  0.7 1.6 %rims.1 = (f32[56,128]{1,0:T(8,128)}, f32[56,128]{1,0:T(8,128)}) custom-call(s32[256]{0:T(256)} %bitcast.1, f32[256,128]{1,0:T(8,128)} %refs_0_.1, f32[256,128]{1,0:T(8,128)} %refs_1_.1, f32[256,128]{1,0:T(8,128)} %refs_2_.1, f32[256,128]{1,0:T(8,128)} %refs_3_.1, s32[256,128]{1,0:T(8,128)} %refs_4_.1, s32[256,128]{1,0:T(8,128)} %bank_ref.3), custom_call_target="tpu_custom_call" | custom-call | tf_op jit(solution)/shard_map/rims/pallas_call | solution.py:596
  2.3 0.0 copy-start.6
  2.3 0.2 collective-permute-start
  2.6 4.3 %collective-permute-start.1 = (f32[56,128]{1,0:T(8,128)}, f32[56,128]{1,0:T(8,128)S(1)}, u32[]{:S(2)}, u32[]{:S(2)}) collective-permute-start(f32[56,128]{1,0:T(8,128)} %get-tuple-element.20), channel_id=1, source_target_pairs={{1,2},{2,1},{5,6},{6,5},{9,10},{10,9},{13,14},{14,13},{17,18},{18,... | collective-permute-start | bytes 86024 | tf_op jit(solution)/shard_map/ppermute | solution.py:611
  6.9 0.0 copy-done
  6.9 0.0 copy-done.1
  6.9 0.0 copy-done.2
  6.9 0.0 copy-done.3
  6.9 0.0 copy-done.4
  7.0 2.6 %own_reaches.1 = (s32[128]{0:T(128)S(1)}, f32[1280,128]{1,0:T(8,128)S(1)}, f32[280,128]{1,0:T(8,128)S(1)}, f32[264,128]{1,0:T(8,128)S(1)}, f32[8,128]{1,0:T(8,128)S(1)}) custom-call(s32[256]{0:T(256)S(1)} %bitcast.2, f32[256,128]{1,0:T(8,128)S(1)} %copy-done.1, f32[256,128]{1,0:T(8,128)S(1)} %copy-done.2, f32[256,128]{1,0:T(8,128)S(1)} %copy-done.3, ...), custom_call_target="tpu_custom_call" | custom-call | tf_op jit(solution)/shard_map/own_reaches/pallas_call | solution.py:614
  9.6 0.0 collective-permute-done.p_ref
  9.6 0.0 collective-permute-done.1.q_ref
  9.6 0.9 %pack.1 = (f32[1280,128]{1,0:T(8,128)S(1)}, f32[280,128]{1,0:T(8,128)S(1)}, f32[160,128]{1,0:T(8,128)S(1)}, f32[160,128]{1,0:T(8,128)S(1)}) custom-call(f32[1280,128]{1,0:T(8,128)S(1)} %get-tuple-element.16.own_flat, f32[280,128]{1,0:T(8,128)S(1)} %get-tuple-element.17.own_gain, ...), custom_call_target="tpu_custom_call", output_to_operand_aliasing={{0}: (0, {}), {1}: (1, {})} | custom-call | tf_op jit(solution)/shard_map/pack/pallas_call | solution.py:631
  10.6 1.3 %collective-permute-start.2 = (f32[160,128]{1,0:T(8,128)S(1)}, f32[160,128]{1,0:T(8,128)S(1)}, u32[]{:S(2)}, u32[]{:S(2)}) collective-permute-start(f32[160,128]{1,0:T(8,128)S(1)} %get-tuple-element.24), channel_id=1, source_target_pairs={{0,4},{8,12},{16,20},{24,28},{4,0},{12,8},{20,16},{28,24},{1,5},{9... | collective-permute-start | bytes 245768 | tf_op jit(solution)/shard_map/ppermute | solution.py:641
  11.9 1.2 %collective-permute-start.3 = (f32[160,128]{1,0:T(8,128)S(1)}, f32[160,128]{1,0:T(8,128)S(1)}, u32[]{:S(2)}, u32[]{:S(2)}) collective-permute-start(f32[160,128]{1,0:T(8,128)S(1)} %get-tuple-element.25), channel_id=1, source_target_pairs={{4,8},{12,16},{20,24},{8,4},{16,12},{24,20},{28,0},{0,28},{5,9},{1... | collective-permute-start | bytes 245768 | tf_op jit(solution)/shard_map/ppermute | solution.py:642
  13.0 0.0 collective-permute-done.2.a_ref
  13.0 3.9 %collective-permute-done.3.b_ref = f32[160,128]{1,0:T(8,128)S(1)} collective-permute-done((f32[160,128]{1,0:T(8,128)S(1)}, f32[160,128]{1,0:T(8,128)S(1)}, u32[]{:S(2)}, u32[]{:S(2)}) %collective-permute-start.3) | collective-permute-done | bytes 81952 | tf_op jit(solution)/shard_map/ppermute | solution.py:642
  16.9 7.0 %steps.1 = (f32[256,128]{1,0:T(8,128)}, f32[256,128]{1,0:T(8,128)}, f32[256,128]{1,0:T(8,128)}, f32[256,128]{1,0:T(8,128)}) custom-call(s32[128]{0:T(128)S(1)} %get-tuple-element.15.rows_ref, f32[1280,128]{1,0:T(8,128)S(1)} %get-tuple-element.21.flat_ref, f32[280,128]{1,0:T(8,128)S(1)} %get-tuple-element.22.gain_ref, ...), custom_call_target="tpu_custom_call" | custom-call | tf_op jit(solution)/shard_map/steps/pallas_call | solution.py:645
  (2 shorter events, 0.0 us)
Async XLA Ops:
  0.6 6.3 %copy-start = (s32[256,128]{1,0:T(8,128)S(1)}, s32[256,128]{1,0:T(8,128)}, u32[]{:S(2)}) copy-start(s32[256,128]{1,0:T(8,128)} %bank_ref.3) | copy-start | bytes 393220
  0.6 6.3 %copy-start.1 = (f32[256,128]{1,0:T(8,128)S(1)}, f32[256,128]{1,0:T(8,128)}, u32[]{:S(2)}) copy-start(f32[256,128]{1,0:T(8,128)} %refs_0_.1) | copy-start | bytes 393220
  0.7 6.3 %copy-start.2 = (f32[256,128]{1,0:T(8,128)S(1)}, f32[256,128]{1,0:T(8,128)}, u32[]{:S(2)}) copy-start(f32[256,128]{1,0:T(8,128)} %refs_1_.1) | copy-start | bytes 393220
  0.7 6.3 %copy-start.3 = (f32[256,128]{1,0:T(8,128)S(1)}, f32[256,128]{1,0:T(8,128)}, u32[]{:S(2)}) copy-start(f32[256,128]{1,0:T(8,128)} %refs_2_.1) | copy-start | bytes 393220
  0.7 6.3 %copy-start.4 = (f32[256,128]{1,0:T(8,128)S(1)}, f32[256,128]{1,0:T(8,128)}, u32[]{:S(2)}) copy-start(f32[256,128]{1,0:T(8,128)} %refs_3_.1) | copy-start | bytes 393220
  0.7 6.3 %copy-start.5 = (s32[256,128]{1,0:T(8,128)S(1)}, s32[256,128]{1,0:T(8,128)}, u32[]{:S(2)}) copy-start(s32[256,128]{1,0:T(8,128)} %refs_4_.1) | copy-start | bytes 393220
  2.3 4.6 %copy-start.6 = (s32[256,1]{0,1:T(1,128)S(1)}, s32[256,1]{0,1:T(1,128)}, u32[]{:S(2)}) copy-start(s32[256,1]{0,1:T(1,128)} %param.11) | copy-start | bytes 3076
  2.3 7.3 %collective-permute-start = (f32[56,128]{1,0:T(8,128)}, f32[56,128]{1,0:T(8,128)S(1)}, u32[]{:S(2)}, u32[]{:S(2)}) collective-permute-start(f32[56,128]{1,0:T(8,128)} %get-tuple-element.19), channel_id=1, source_target_pairs={{0,1},{2,3},{1,0},{3,2},{4,5},{6,7},{5,4},{7,6},{8,9},{10,11},{9,8... | collective-permute-start | bytes 86024 | tf_op jit(solution)/shard_map/ppermute | solution.py:610
  2.6 7.1 %collective-permute-start.1 = (f32[56,128]{1,0:T(8,128)}, f32[56,128]{1,0:T(8,128)S(1)}, u32[]{:S(2)}, u32[]{:S(2)}) collective-permute-start(f32[56,128]{1,0:T(8,128)} %get-tuple-element.20), channel_id=1, source_target_pairs={{1,2},{2,1},{5,6},{6,5},{9,10},{10,9},{13,14},{14,13},{17,18},{18,... | collective-permute-start | bytes 86024 | tf_op jit(solution)/shard_map/ppermute | solution.py:611
  10.6 2.5 %collective-permute-start.2 = (f32[160,128]{1,0:T(8,128)S(1)}, f32[160,128]{1,0:T(8,128)S(1)}, u32[]{:S(2)}, u32[]{:S(2)}) collective-permute-start(f32[160,128]{1,0:T(8,128)S(1)} %get-tuple-element.24), channel_id=1, source_target_pairs={{0,4},{8,12},{16,20},{24,28},{4,0},{12,8},{20,16},{28,24},{1,5},{9... | collective-permute-start | bytes 245768 | tf_op jit(solution)/shard_map/ppermute | solution.py:641
  11.9 5.1 %collective-permute-start.3 = (f32[160,128]{1,0:T(8,128)S(1)}, f32[160,128]{1,0:T(8,128)S(1)}, u32[]{:S(2)}, u32[]{:S(2)}) collective-permute-start(f32[160,128]{1,0:T(8,128)S(1)} %get-tuple-element.25), channel_id=1, source_target_pairs={{4,8},{12,16},{20,24},{8,4},{16,12},{24,20},{28,0},{0,28},{5,9},{1... | collective-permute-start | bytes 245768 | tf_op jit(solution)/shard_map/ppermute | solution.py:642

commit v4 on v3

--- a/solution.py
+++ b/solution.py
@@ -1,3 +1,5 @@
+import functools
+
 import jax
 import jax.numpy as jnp
 from jax import lax
@@ -20,9 +22,9 @@
 DURATION = TIME_STEP / SUB
 SURFACE, GROUND, ROUGH = range(3)
 FLOOD_FIELDS = 3
-LEVEL, FLUX, BED, WIDTH, GAIN, LIVE = range(6)
-SLOT_FIELDS = 6
-TOP, DRIVE, FRICTION, FEED, WATER = range(6, 11)
+LEVEL, FLUX, BED, WIDTH, GAIN = range(5)
+SLOT_FIELDS = 5
+TOP, DRIVE, FRICTION, FEED, WATER = range(5, 10)
 ROWS_AT_ONCE = 64
 TILES_AT_ONCE = 34
 UNPACK_AT_ONCE = 20
@@ -174,18 +176,20 @@
         for j, place in enumerate(places):
             rows_ref[place] = first + j + RIM
     rows_ref[count] = beyond
+    return count
 
 
 def own_kernel(
-    mask_ref, depth_ref, ground_ref, rough_ref, river_ref, width_ref, bank_ref,
-    rows_ref, flat_ref, gain_ref, level_ref, listed_ref,
-    bed_ref, wide_ref,
+    mask_any, depth_ref, ground_ref, rough_ref, river_ref, width_ref, bank_ref,
+    flat_ref, level_ref, listed_ref,
+    bed_ref, wide_ref, mask_ref, rows_ref, sem,
 ):
     rows, cols = depth_ref.shape
     slots = rows // 4
     tail, ext, total = rows + RIM, rows + 2 * RIM, slots + RIM
     base = FLOOD_FIELDS * ext
-    fill_list(mask_ref, rows_ref)
+    fetch = pltpu.make_async_copy(mask_any, mask_ref, sem)
+    fetch.start()
 
     def prepare(t):
         at = pl.ds(t, RIM)
@@ -197,30 +201,27 @@
         level_ref[at, :] = bed + river_ref[at, :]
         bed_ref[at, :] = bed
         wide_ref[at, :] = 8.0 + 9.0 * width_ref[at, :].astype(jnp.float32)
-        gain_ref[at, :] = jnp.zeros((RIM, cols), jnp.float32)
 
     each_tile(rows // RIM, prepare, TILES_AT_ONCE)
     zero = jnp.zeros((RIM, cols), jnp.float32)
     flat_ref[SURFACE * ext + tail : (SURFACE + 1) * ext, :] = zero
-    for t in range(rows, ext + RIM, RIM):
-        gain_ref[t : t + RIM, :] = zero
     level_ref[rows:tail, :] = zero
     bed_ref[rows:tail, :] = zero
     wide_ref[rows:tail, :] = zero + 1.0
     lane = lanes((RIM, cols))
-
-    listed = zero
+    fetch.wait()
+    count = fill_list(mask_ref, rows_ref)
+
+    listed = zero + count.astype(jnp.float32)
     for i in range(slots):
         e = rows_ref[i]
         own = jnp.minimum(e - RIM, rows)
         listed = jnp.where(lane == cols - slots + i, e.astype(jnp.float32), listed)
         to = base + i
-        live = jnp.where(e < tail, 1.0, 0.0)
         of, surface = pl.ds(own, 1), pl.ds(own + (SURFACE * ext + RIM), 1)
         flat_ref[pl.ds(to + LEVEL * total, 1), :] = level_ref[of, :]
         flat_ref[pl.ds(to + BED * total, 1), :] = bed_ref[of, :]
         flat_ref[pl.ds(to + WIDTH * total, 1), :] = wide_ref[of, :]
-        flat_ref[pl.ds(to + LIVE * total, 1), :] = jnp.full((1, cols), live, jnp.float32)
         flat_ref[pl.ds(to + GAIN * total, 1), :] = flat_ref[surface, :]
     listed_ref[...] = listed
 
@@ -235,23 +236,13 @@
     )
     flat_ref[part(LEVEL), :] = level
     flat_ref[part(FLUX), :] = flux
-    live = flat_ref[part(LIVE), :] > 0.0
-    flat_ref[part(GAIN), :] = jnp.where(live, gathered * (width / CELL_SIZE), 0.0)
-
-    def spread(i):
-        gain_ref[pl.ds(rows_ref[i], 1), :] = flat_ref[pl.ds(base + GAIN * total + i, 1), :]
-
-    each_row(slots, spread)
-
-
-def pack_kernel(
-    own_flat, own_gain, listed_ref, p_ref, q_ref,
-    flat_ref, gain_ref, a_ref, b_ref,
-):
-    del own_flat, own_gain
+    flat_ref[part(GAIN), :] = gathered * (width / CELL_SIZE)
+
+
+def pack_kernel(rows, own_flat, listed_ref, p_ref, q_ref, flat_ref, a_ref, b_ref):
+    del own_flat
     cols = a_ref.shape[1]
-    ext = gain_ref.shape[0] - RIM
-    rows = ext - 2 * RIM
+    ext = rows + 2 * RIM
     slots = rows // 4
     tail, total = rows + RIM, slots + RIM
     base = FLOOD_FIELDS * ext
@@ -275,19 +266,19 @@
     level, flux, gathered = first_reaches(ends(3), ends(0), reach_constants(bed, width))
     gained = jnp.where(ends(6) > 0.0, gathered * (width / CELL_SIZE), 0.0)
     for field, value in (
-        (LEVEL, level), (FLUX, flux), (BED, bed), (WIDTH, width), (GAIN, gained), (LIVE, ends(6)),
+        (LEVEL, level), (FLUX, flux), (BED, bed), (WIDTH, width), (GAIN, gained),
     ):
         flat_ref[part(field), :] = value
+    live = base + SLOT_FIELDS * total
+    flat_ref[live : live + RIM, :] = ends(6)
     for k in range(FLOOD_FIELDS):
         flat_ref[k * ext : k * ext + RIM, :] = rim(south, k)
         flat_ref[k * ext + tail : (k + 1) * ext, :] = rim(north, k)
-    gain_ref[half:RIM, :] = gained[:half]
-    gain_ref[tail : tail + half, :] = gained[half:]
 
     groups = cols // COLS
     group = lanes((RIM, cols)) // COLS
     eastern = odd_position("lon") == 0
-    tiles = (base + SLOT_FIELDS * total) // RIM
+    tiles = (base + SLOT_FIELDS * total) // RIM + 1
     turns = []
     for start in (jnp.where(eastern, cols - COLS, 0), jnp.where(eastern, 0, cols - COLS)):
         turns.append([lax.rem(cols + COLS * g - start, cols) for g in range(groups)])
@@ -307,10 +298,10 @@
 
 
 def step_kernel(
-    rows_ref, flat_ref, gain_ref, level_ref, bank_ref, a_ref, b_ref,
+    flat_ref, level_ref, bank_ref, listed_ref, a_ref, b_ref,
     depth_out, river_out, east_out, north_out,
-    own_ref, side_ref, state, side_gain, own_gain,
-    flow_ref, fixed_ref, river_ref, list_rows, west_rows, east_rows, sems,
+    both_ref, state, gains,
+    flow_ref, fixed_ref, river_ref, list_rows, list_smem, sems,
 ):
     rows, cols = depth_out.shape
     slots = rows // 4
@@ -322,13 +313,25 @@
     lists = a_ref.shape[0] - RIM
     zero = jnp.zeros((RIM, cols), jnp.float32)
 
+    few = slots // 4
+    apart = ext + RIM
+    own_ref = both_ref.at[pl.ds(0, apart), :]
+    side_ref = both_ref.at[pl.ds(apart, both_ref.shape[0] - apart), :]
+
+    own_list = listed_ref[...]
+    crowded = jnp.broadcast_to(own_list[:, 0:1], own_list.shape) > few + 0.5
     list_a, list_b = a_ref[lists : lists + RIM, :], b_ref[lists : lists + RIM, :]
-    list_rows[0] = jnp.where(eastern, list_a, list_b).astype(jnp.int32)
-    list_rows[1] = jnp.where(eastern, list_b, list_a).astype(jnp.int32)
-    one = pltpu.make_async_copy(list_rows.at[0, 0], east_rows, sems.at[0])
-    two = pltpu.make_async_copy(list_rows.at[1, 0], west_rows, sems.at[1])
-    one.start()
-    two.start()
+    east_list = jnp.where(eastern, list_a, list_b) + apart
+    west_list = jnp.where(eastern, list_b, list_a) + apart
+    copies = []
+    for k, rows_of in enumerate((
+        jnp.where(crowded, own_list, east_list), jnp.where(crowded, own_list, west_list),
+        jnp.where(crowded, east_list, own_list), jnp.where(crowded, west_list, own_list),
+        own_list,
+    )):
+        list_rows[k] = rows_of.astype(jnp.int32)
+        copies.append(pltpu.make_async_copy(list_rows.at[k, 0], list_smem.at[k], sems.at[k]))
+        copies[k].start()
 
     groups = cols // COLS
     lane = lanes((RIM, cols))
@@ -350,56 +353,73 @@
     each_row(a_ref.shape[0] // RIM, unpack, UNPACK_AT_ONCE)
 
     def copy_in(t):
-        at = pl.ds(t, RIM)
+        at, beside = pl.ds(t, RIM), pl.ds(apart + t, RIM)
         own_ref[at, :] = flat_ref[at, :]
-        own_gain[at, :] = gain_ref[at, :]
         for k in range(2):
-            side_gain[k, at, :] = zero
+            gains[k, at, :] = zero
+            gains[k, beside, :] = zero
 
     each_tile(ext // RIM, copy_in, TILES_AT_ONCE)
     own_ref[ext : ext + RIM, :] = zero
 
-    def copy_slots(t):
-        values = []
+    def chosen(own, side):
+        return jnp.where(crowded, own, side), jnp.where(crowded, side, own)
+
+    for t in range(0, total, RIM):
+        pairs = []
         for field in range(SLOT_FIELDS):
-            own = flat_ref[pl.ds(base + field * total + t, RIM), :]
-            side = side_ref[pl.ds(base + field * total + t, RIM), :]
-            state[field, pl.ds(t, RIM), :] = own
-            state[field, pl.ds(total + t, RIM), :] = side
-            values.append((own, side))
+            at = pl.ds(base + field * total + t, RIM)
+            pairs.append(chosen(flat_ref[at, :], side_ref[at, :]))
         for j in range(2):
-            constants = reach_constants(values[BED][j], values[WIDTH][j])
+            to = t
+            if j == 1:
+                if few <= t < slots:
+                    continue
+                to = total + min(t, few)
+            constants = reach_constants(pairs[BED][j], pairs[WIDTH][j])
+            for field, pair in enumerate(pairs):
+                state[field, to : to + RIM, :] = pair[j]
             for field, value in zip((TOP, DRIVE, FRICTION, FEED), constants):
-                state[field, pl.ds(j * total + t, RIM), :] = value
-
-    each_tile(total // RIM, copy_slots, TILES_AT_ONCE)
-    one.wait()
-    two.wait()
+                state[field, to : to + RIM, :] = value
+    at = pl.ds(base + SLOT_FIELDS * total, RIM)
+    alive = [value > 0.0 for value in chosen(flat_ref[at, :], side_ref[at, :])]
+    for copy in copies:
+        copy.wait()
     first = cols - slots
-
-    def spread_side():
-        def visit(i):
-            line = state[GAIN, pl.ds(total + i, 1), :]
-            side_gain[0, pl.ds(east_rows[first + i], 1), :] = line
-            side_gain[1, pl.ds(west_rows[first + i], 1), :] = line
-
-        each_row(slots, visit)
-        start = total + slots
-        for k in range(2):
-            side_gain[k, half:RIM, :] = state[GAIN, start : start + half, :]
-            side_gain[k, tail : tail + half, :] = state[GAIN, start + half : start + RIM, :]
-
-    def spread_own():
-        def visit(i):
-            own_gain[pl.ds(rows_ref[i], 1), :] = state[GAIN, pl.ds(i, 1), :]
-
-        each_row(slots, visit)
-        own_gain[half:RIM, :] = state[GAIN, slots : slots + half, :]
-        own_gain[tail : tail + half, :] = state[GAIN, slots + half : total, :]
-
-    spread_side()
-
-    def reaches(start, size):
+    places = [(i, list_smem.at[0], list_smem.at[1], first + i) for i in range(slots)]
+    places += [(total + i, list_smem.at[2], list_smem.at[3], first + i) for i in range(few)]
+    edge = total + few
+
+    def spread():
+        for slot, lows, highs, i in places:
+            line = state[GAIN, slot : slot + 1, :]
+            gains[0, pl.ds(lows[i], 1), :] = line
+            gains[1, pl.ds(highs[i], 1), :] = line
+        for j, lines in enumerate(
+            chosen(state[GAIN, slots:total, :], state[GAIN, edge : edge + RIM, :])
+        ):
+            for k in range(2):
+                start = j * apart
+                gains[k, start + half : start + RIM, :] = lines[:half]
+                gains[k, start + tail : start + tail + half, :] = lines[half:]
+
+    middle = lanes((1, cols)) < cols // 2
+
+    def draw():
+        for slot, lows, highs, i in places:
+            state[WATER, slot : slot + 1, :] = jnp.where(
+                middle, both_ref[pl.ds(lows[i], 1), :], both_ref[pl.ds(highs[i], 1), :]
+            )
+        ends = [
+            jnp.concatenate([ref[half:RIM, :], ref[tail : tail + half, :]], axis=0)
+            for ref in (own_ref, side_ref)
+        ]
+        for start, value in zip((slots, edge), chosen(*ends)):
+            state[WATER, start : start + RIM, :] = value
+
+    spread()
+
+    def reaches(start, size, live):
         at = slice(start, start + size)
 
         faces = [state[k, at, :] for k in (TOP, DRIVE, FRICTION)]
@@ -416,8 +436,10 @@
             yield
         state[LEVEL, at, :] = level
         state[FLUX, at, :] = flux
-        live = state[LIVE, at, :] > 0.0
-        state[GAIN, at, :] = jnp.where(live, gathered * (state[WIDTH, at, :] / CELL_SIZE), 0.0)
+        gained = gathered * (state[WIDTH, at, :] / CELL_SIZE)
+        fixed = size - RIM
+        state[GAIN, start : start + fixed, :] = gained[:fixed]
+        state[GAIN, start + fixed : start + size, :] = jnp.where(live, gained[fixed:], 0.0)
 
     last_lane = lane == cols - 1
     first_lane = lane == 0
@@ -497,14 +519,15 @@
             moved = share * (west[j] - to_east[j] + south - to_north)
             if final:
                 out = pl.ds(t - RIM, RIM)
-                new = own_ref[at, :] + moved + own_gain[at, :]
+                new = own_ref[at, :] + moved + gains[0, at, :]
                 depth_out[out, :] = new - flat_ref[pl.ds(t + GROUND * ext, RIM), :]
                 east_out[out, :] = to_east[0]
                 north_out[out, :] = to_north
             elif j == 0:
-                own_ref[at, :] = own_ref[at, :] + moved + own_gain[at, :]
+                own_ref[at, :] = own_ref[at, :] + moved + gains[0, at, :]
             else:
-                gain = jnp.where(low, side_gain[0, at, :], side_gain[1, at, :])
+                beside = pl.ds(apart + t, RIM)
+                gain = jnp.where(low, gains[0, beside, :], gains[1, beside, :])
                 side_ref[at, :] = side_ref[at, :] + moved + gain
         return after
 
@@ -521,8 +544,11 @@
     def settle():
         river_ref[0:rows, :] = level_ref[0:rows, :]
         for i in range(slots):
-            own = jnp.minimum(rows_ref[i] - RIM, rows)
-            river_ref[pl.ds(own, 1), :] = state[LEVEL, pl.ds(i, 1), :]
+            own = jnp.minimum(list_smem[4, first + i] - RIM, rows)
+            other = total + min(i, few)
+            river_ref[pl.ds(own, 1), :] = jnp.where(
+                crowded[:1], state[LEVEL, i : i + 1, :], state[LEVEL, other : other + 1, :]
+            )
         for t in range(0, rows, RIM):
             at = pl.ds(t, RIM)
             ground = flat_ref[pl.ds(t + (GROUND * ext + RIM), RIM), :]
@@ -533,27 +559,12 @@
         constants_of(t)
         flows(t, 0)
     update_all(0)
-    middle = lanes((1, cols)) < cols // 2
     for step in range(1, STEPS):
-        sides = step < STEPS - 1
-
-        def water(i):
-            state[WATER, pl.ds(i, 1), :] = own_ref[pl.ds(rows_ref[i], 1), :]
-            if sides:
-                state[WATER, pl.ds(total + i, 1), :] = jnp.where(
-                    middle,
-                    side_ref[pl.ds(east_rows[first + i], 1), :],
-                    side_ref[pl.ds(west_rows[first + i], 1), :],
-                )
-
-        each_row(slots, water)
-        for j, ref in enumerate((own_ref, side_ref)[: 2 if sides else 1]):
-            start = j * total + slots
-            state[WATER, start : start + half, :] = ref[half:RIM, :]
-            state[WATER, start + half : start + RIM, :] = ref[tail : tail + half, :]
-
-        running = [reaches(start, total) for start in range(0, (2 if sides else 1) * total, total)]
-        tiles = list(range(0, ext if sides else tail, RIM))
+        final = step == STEPS - 1
+        draw()
+
+        running = [reaches(0, total, alive[0]), reaches(total, few + RIM, alive[1])]
+        tiles = list(range(0, tail if final else ext, RIM))
         share_of = -(-len(tiles) // SUB)
         for substep in range(SUB):
             for reach in running:
@@ -562,10 +573,8 @@
                 flows(t, step)
         for reach in running:
             next(reach, None)
-        spread_own()
-        if sides:
-            spread_side()
-        else:
+        spread()
+        if final:
             settle()
         update_all(step)
 
@@ -581,11 +590,10 @@
     f32 = jnp.float32
     lon_total, lat_total = lax.axis_size("lon"), lax.axis_size("lat")
     mask = reach_mask.reshape(rows)
-    smem = pl.BlockSpec(memory_space=pltpu.SMEM)
     vmem = pl.BlockSpec(memory_space=pltpu.VMEM)
     fields = (depth_init, ground, roughness, river_init, width_class, bank_class)
     ext, total = rows + 2 * RIM, slots + RIM
-    used = FLOOD_FIELDS * ext + SLOT_FIELDS * total
+    used = FLOOD_FIELDS * ext + SLOT_FIELDS * total + RIM
     groups = cols // COLS
     message = -(-(used // RIM + slots // COLS) // groups) * RIM
     room = message * groups
@@ -610,33 +618,35 @@
     got_p = lax.ppermute(to_p, "lat", swaps(lat_total, 0))
     got_q = lax.ppermute(to_q, "lat", swaps(lat_total, 1))
     flat_shape = jax.ShapeDtypeStruct((room, cols), f32)
-    dense = jax.ShapeDtypeStruct((ext + RIM, cols), f32)
-    row_list, own_flat, own_gain, level, listed = pl.pallas_call(
+    own_flat, level, listed = pl.pallas_call(
         own_kernel,
-        in_specs=[smem] + [vmem] * 6,
-        out_specs=[smem] + [vmem] * 4,
+        in_specs=[pl.BlockSpec(memory_space=pl.ANY)] + [vmem] * 6,
+        out_specs=[vmem] * 3,
         out_shape=[
-            jax.ShapeDtypeStruct((2 * slots,), jnp.int32),
             flat_shape,
-            dense,
             jax.ShapeDtypeStruct((rows + RIM, cols), f32),
             jax.ShapeDtypeStruct((RIM, cols), f32),
         ],
-        scratch_shapes=[pltpu.VMEM((rows + RIM, cols), f32)] * 2,
+        scratch_shapes=[pltpu.VMEM((rows + RIM, cols), f32)] * 2
+        + [
+            pltpu.SMEM((rows,), jnp.int32),
+            pltpu.SMEM((2 * slots,), jnp.int32),
+            pltpu.SemaphoreType.DMA,
+        ],
         compiler_params=params,
         name="own_reaches",
     )(mask, *fields)
 
     message_shape = jax.ShapeDtypeStruct((message, cols), f32)
-    flat, gain, to_a, to_b = pl.pallas_call(
-        pack_kernel,
-        in_specs=[vmem] * 5,
-        out_specs=[vmem] * 4,
-        out_shape=[flat_shape, dense, message_shape, message_shape],
-        input_output_aliases={0: 0, 1: 1},
+    flat, to_a, to_b = pl.pallas_call(
+        functools.partial(pack_kernel, rows),
+        in_specs=[vmem] * 4,
+        out_specs=[vmem] * 3,
+        out_shape=[flat_shape, message_shape, message_shape],
+        input_output_aliases={0: 0},
         compiler_params=params,
         name="pack",
-    )(own_flat, own_gain, listed, got_p, got_q)
+    )(own_flat, listed, got_p, got_q)
     ring = swaps(lon_total, 1) + [(lon_total - 1, 0), (0, lon_total - 1)]
     got_a = lax.ppermute(to_a, "lon", swaps(lon_total, 0))
     got_b = lax.ppermute(to_b, "lon", ring)
@@ -644,26 +654,23 @@
     tile = jax.ShapeDtypeStruct((rows, cols), f32)
     return pl.pallas_call(
         step_kernel,
-        in_specs=[smem] + [vmem] * 6,
+        in_specs=[vmem] * 6,
         out_specs=[vmem] * 4,
         out_shape=[tile] * 4,
         scratch_shapes=[
-            pltpu.VMEM((ext + RIM, cols), f32),
-            pltpu.VMEM((room, cols), f32),
-            pltpu.VMEM((WATER + 1, 2 * total, cols), f32),
-            pltpu.VMEM((2, ext + RIM, cols), f32),
-            pltpu.VMEM((ext + RIM, cols), f32),
+            pltpu.VMEM((ext + RIM + room, cols), f32),
+            pltpu.VMEM((WATER + 1, total + slots // 4 + RIM, cols), f32),
+            pltpu.VMEM((2, 2 * (ext + RIM), cols), f32),
             pltpu.VMEM((2, 2, ext, cols), f32),
             pltpu.VMEM((2, 4, ext, cols), f32),
             pltpu.VMEM((rows + RIM, cols), f32),
-            pltpu.VMEM((2, RIM, cols), jnp.int32),
-            pltpu.SMEM((cols,), jnp.int32),
-            pltpu.SMEM((cols,), jnp.int32),
-            pltpu.SemaphoreType.DMA((2,)),
+            pltpu.VMEM((5, RIM, cols), jnp.int32),
+            pltpu.SMEM((5, cols), jnp.int32),
+            pltpu.SemaphoreType.DMA((5,)),
         ],
         compiler_params=params,
         name="steps",
-    )(row_list, flat, gain, level, bank_class, got_a, got_b)
+    )(flat, level, bank_class, listed, got_a, got_b)
 
 
 def solution(mesh):

time: 24.2 us -> 22.9 us (0.946)
  the two profiles are of different devices: /device:TPU:11 before, /device:TPU:19 now
where the time goes in v4:
time: 22.9 us; the launch traced here: 22.7 us
  Pallas kernels  10.7 us (47%)
  starting transfers between devices  6.59 us (29%)
  waiting for transfers between devices  4.54 us (20%)
  between operations  0.78 us (3%)
    pallas_call x1, Pallas kernels, body(): pl.pallas_call(step_kernel, in_specs=[vmem] * 6, out_specs=[vmem] * 4, ou...  6.11 us
    ppermute x1, waiting for transfers between devices, body(): got_b = lax.ppermute(to_b, 'lon', ring)  3.82 us
    ppermute x1, starting transfers between devices, body(): got_a = lax.ppermute(to_a, 'lon', swaps(lon_total, 0))  2.15 us
    pallas_call x1, Pallas kernels, body(): pl.pallas_call(own_kernel, in_specs=[pl.BlockSpec(memory_space=pl.ANY)] +...  2.09 us
    ppermute x1, starting transfers between devices, body(): got_q = lax.ppermute(to_q, 'lat', swaps(lat_total, 1))  1.91 us
    pallas_call x1, Pallas kernels, body(): pl.pallas_call(rows_kernel, in_specs=[hbm] * 7, out_specs=[vmem, vmem], o...  1.62 us
    ppermute x1, starting transfers between devices, body(): got_p = lax.ppermute(to_p, 'lat', swaps(lat_total, 0))  1.36 us
    ppermute x1, starting transfers between devices, body(): got_b = lax.ppermute(to_b, 'lon', ring)  1.17 us
  transfers between devices with their start and end apart: 4, of which 2 were waited for; matrix products, arithmetic and copies ran while one was open for 0% of the time, Pallas kernels for 9%

profile of v4, /device:TPU:19, one launch (start us, length us, event | category | flops | bytes accessed | tf_op | source)
XLA Modules:
  0.0 22.7 jit_solution(1746271875153444477)
XLA Ops:
  0.6 0.0 copy-start
  0.6 0.0 copy-start.1
  0.7 0.0 copy-start.2
  0.7 0.0 copy-start.3
  0.7 0.0 copy-start.4
  0.7 0.0 copy-start.5
  0.7 1.6 %rims.1 = (f32[56,128]{1,0:T(8,128)}, f32[56,128]{1,0:T(8,128)}) custom-call(s32[256]{0:T(256)} %bitcast.1, f32[256,128]{1,0:T(8,128)} %refs_0_.1, f32[256,128]{1,0:T(8,128)} %refs_1_.1, f32[256,128]{1,0:T(8,128)} %refs_2_.1, f32[256,128]{1,0:T(8,128)} %refs_3_.1, s32[256,128]{1,0:T(8,128)} %refs_4_.1, s32[256,128]{1,0:T(8,128)} %bank_ref.3), custom_call_target="tpu_custom_call" | custom-call | tf_op jit(solution)/shard_map/rims/pallas_call | solution.py:604
  2.3 0.0 copy-start.6
  2.3 1.4 %collective-permute-start = (f32[56,128]{1,0:T(8,128)}, f32[56,128]{1,0:T(8,128)S(1)}, u32[]{:S(2)}, u32[]{:S(2)}) collective-permute-start(f32[56,128]{1,0:T(8,128)} %get-tuple-element.14), channel_id=1, source_target_pairs={{0,1},{2,3},{1,0},{3,2},{4,5},{6,7},{5,4},{7,6},{8,9},{10,11},{9,8... | collective-permute-start | bytes 86024 | tf_op jit(solution)/shard_map/ppermute | solution.py:618
  3.7 1.9 %collective-permute-start.1 = (f32[56,128]{1,0:T(8,128)}, f32[56,128]{1,0:T(8,128)S(1)}, u32[]{:S(2)}, u32[]{:S(2)}) collective-permute-start(f32[56,128]{1,0:T(8,128)} %get-tuple-element.15), channel_id=1, source_target_pairs={{1,2},{2,1},{5,6},{6,5},{9,10},{10,9},{13,14},{14,13},{17,18},{18,... | collective-permute-start | bytes 86024 | tf_op jit(solution)/shard_map/ppermute | solution.py:619
  5.6 0.0 copy-done
  5.6 0.0 copy-done.1
  5.6 0.0 copy-done.2
  5.6 0.0 copy-done.3
  5.7 0.0 copy-done.4
  5.7 2.1 %own_reaches.1 = (f32[1216,128]{1,0:T(8,128)S(1)}, f32[264,128]{1,0:T(8,128)S(1)}, f32[8,128]{1,0:T(8,128)S(1)}) custom-call(s32[256]{0:T(256)S(1)} %bitcast.2, f32[256,128]{1,0:T(8,128)S(1)} %copy-done.1, f32[256,128]{1,0:T(8,128)S(1)} %copy-done.2, f32[256,128]{1,0:T(8,128)S(1)} %copy-done.3, f32[256,128]{1,0:T(8,128)S(1)} %copy-done.4, ...), custom_call_target="tpu_custom_call" | custom-call | tf_op jit(solution)/shard_map/own_reaches/pallas_call | solution.py:621
  7.8 0.0 collective-permute-done.p_ref
  7.8 0.7 %collective-permute-done.1.q_ref = f32[56,128]{1,0:T(8,128)S(1)} collective-permute-done((f32[56,128]{1,0:T(8,128)}, f32[56,128]{1,0:T(8,128)S(1)}, u32[]{:S(2)}, u32[]{:S(2)}) %collective-permute-start.1) | collective-permute-done | bytes 28704 | tf_op jit(solution)/shard_map/ppermute | solution.py:619
  8.5 0.9 %pack.1 = (f32[1216,128]{1,0:T(8,128)S(1)}, f32[152,128]{1,0:T(8,128)S(1)}, f32[152,128]{1,0:T(8,128)S(1)}) custom-call(f32[1216,128]{1,0:T(8,128)S(1)} %get-tuple-element.12.own_flat, f32[8,128]{1,0:T(8,128)S(1)} %get-tuple-element.13.listed_ref, f32[56,128]{1,0:T(8,128)S(1)} %collective-permute-done.p_ref, ...), custom_call_target="tpu_custom_call", output_to_operand_aliasing={{0}: (0, {})} | custom-call | tf_op jit(solution)/shard_map/pack/pallas_call | solution.py:641
  9.4 2.1 %collective-permute-start.2 = (f32[152,128]{1,0:T(8,128)S(1)}, f32[152,128]{1,0:T(8,128)S(1)}, u32[]{:S(2)}, u32[]{:S(2)}) collective-permute-start(f32[152,128]{1,0:T(8,128)S(1)} %get-tuple-element.18), channel_id=1, source_target_pairs={{0,4},{8,12},{16,20},{24,28},{4,0},{12,8},{20,16},{28,24},{1,5},{9... | collective-permute-start | bytes 233480 | tf_op jit(solution)/shard_map/ppermute | solution.py:651
  11.6 1.2 %collective-permute-start.3 = (f32[152,128]{1,0:T(8,128)S(1)}, f32[152,128]{1,0:T(8,128)S(1)}, u32[]{:S(2)}, u32[]{:S(2)}) collective-permute-start(f32[152,128]{1,0:T(8,128)S(1)} %get-tuple-element.19), channel_id=1, source_target_pairs={{4,8},{12,16},{20,24},{8,4},{16,12},{24,20},{28,0},{0,28},{5,9},{1... | collective-permute-start | bytes 233480 | tf_op jit(solution)/shard_map/ppermute | solution.py:652
  12.8 0.0 collective-permute-done.2.a_ref
  12.8 3.8 %collective-permute-done.3.b_ref = f32[152,128]{1,0:T(8,128)S(1)} collective-permute-done((f32[152,128]{1,0:T(8,128)S(1)}, f32[152,128]{1,0:T(8,128)S(1)}, u32[]{:S(2)}, u32[]{:S(2)}) %collective-permute-start.3) | collective-permute-done | bytes 77856 | tf_op jit(solution)/shard_map/ppermute | solution.py:652
  16.6 6.1 %steps.1 = (f32[256,128]{1,0:T(8,128)}, f32[256,128]{1,0:T(8,128)}, f32[256,128]{1,0:T(8,128)}, f32[256,128]{1,0:T(8,128)}) custom-call(f32[1216,128]{1,0:T(8,128)S(1)} %get-tuple-element.16.flat_ref, f32[264,128]{1,0:T(8,128)S(1)} %get-tuple-element.17.level_ref, s32[256,128]{1,0:T(8,128)S(1)} %copy-done, f32[8,128]{1,0:T(8,128)S(1)} %get-tuple-element.13.listed_ref, ...), custom_call_target="tpu_custom_call" | custom-call | tf_op jit(solution)/shard_map/steps/pallas_call | solution.py:655
  (2 shorter events, 0.0 us)
Async XLA Ops:
  0.6 5.0 %copy-start = (s32[256,128]{1,0:T(8,128)S(1)}, s32[256,128]{1,0:T(8,128)}, u32[]{:S(2)}) copy-start(s32[256,128]{1,0:T(8,128)} %bank_ref.3) | copy-start | bytes 393220
  0.6 5.0 %copy-start.1 = (f32[256,128]{1,0:T(8,128)S(1)}, f32[256,128]{1,0:T(8,128)}, u32[]{:S(2)}) copy-start(f32[256,128]{1,0:T(8,128)} %refs_0_.1) | copy-start | bytes 393220
  0.7 5.0 %copy-start.2 = (f32[256,128]{1,0:T(8,128)S(1)}, f32[256,128]{1,0:T(8,128)}, u32[]{:S(2)}) copy-start(f32[256,128]{1,0:T(8,128)} %refs_1_.1) | copy-start | bytes 393220
  0.7 5.0 %copy-start.3 = (f32[256,128]{1,0:T(8,128)S(1)}, f32[256,128]{1,0:T(8,128)}, u32[]{:S(2)}) copy-start(f32[256,128]{1,0:T(8,128)} %refs_2_.1) | copy-start | bytes 393220
  0.7 5.0 %copy-start.4 = (f32[256,128]{1,0:T(8,128)S(1)}, f32[256,128]{1,0:T(8,128)}, u32[]{:S(2)}) copy-start(f32[256,128]{1,0:T(8,128)} %refs_3_.1) | copy-start | bytes 393220
  0.7 5.0 %copy-start.5 = (s32[256,128]{1,0:T(8,128)S(1)}, s32[256,128]{1,0:T(8,128)}, u32[]{:S(2)}) copy-start(s32[256,128]{1,0:T(8,128)} %refs_4_.1) | copy-start | bytes 393220
  2.3 3.4 %copy-start.6 = (s32[256,1]{0,1:T(1,128)S(1)}, s32[256,1]{0,1:T(1,128)}, u32[]{:S(2)}) copy-start(s32[256,1]{0,1:T(1,128)} %param.11) | copy-start | bytes 3076
  2.3 5.5 %collective-permute-start = (f32[56,128]{1,0:T(8,128)}, f32[56,128]{1,0:T(8,128)S(1)}, u32[]{:S(2)}, u32[]{:S(2)}) collective-permute-start(f32[56,128]{1,0:T(8,128)} %get-tuple-element.14), channel_id=1, source_target_pairs={{0,1},{2,3},{1,0},{3,2},{4,5},{6,7},{5,4},{7,6},{8,9},{10,11},{9,8... | collective-permute-start | bytes 86024 | tf_op jit(solution)/shard_map/ppermute | solution.py:618
  3.7 4.8 %collective-permute-start.1 = (f32[56,128]{1,0:T(8,128)}, f32[56,128]{1,0:T(8,128)S(1)}, u32[]{:S(2)}, u32[]{:S(2)}) collective-permute-start(f32[56,128]{1,0:T(8,128)} %get-tuple-element.15), channel_id=1, source_target_pairs={{1,2},{2,1},{5,6},{6,5},{9,10},{10,9},{13,14},{14,13},{17,18},{18,... | collective-permute-start | bytes 86024 | tf_op jit(solution)/shard_map/ppermute | solution.py:619
  9.4 3.3 %collective-permute-start.2 = (f32[152,128]{1,0:T(8,128)S(1)}, f32[152,128]{1,0:T(8,128)S(1)}, u32[]{:S(2)}, u32[]{:S(2)}) collective-permute-start(f32[152,128]{1,0:T(8,128)S(1)} %get-tuple-element.18), channel_id=1, source_target_pairs={{0,4},{8,12},{16,20},{24,28},{4,0},{12,8},{20,16},{28,24},{1,5},{9... | collective-permute-start | bytes 233480 | tf_op jit(solution)/shard_map/ppermute | solution.py:651
  11.6 5.0 %collective-permute-start.3 = (f32[152,128]{1,0:T(8,128)S(1)}, f32[152,128]{1,0:T(8,128)S(1)}, u32[]{:S(2)}, u32[]{:S(2)}) collective-permute-start(f32[152,128]{1,0:T(8,128)S(1)} %get-tuple-element.19), channel_id=1, source_target_pairs={{4,8},{12,16},{20,24},{8,4},{16,12},{24,20},{28,0},{0,28},{5,9},{1... | collective-permute-start | bytes 233480 | tf_op jit(solution)/shard_map/ppermute | solution.py:652

commit v5 on v4

--- a/solution.py
+++ b/solution.py
@@ -28,7 +28,6 @@
 ROWS_AT_ONCE = 64
 TILES_AT_ONCE = 34
 UNPACK_AT_ONCE = 20
-FIRST_AT_ONCE = 7
 
 
 def lanes(shape):
@@ -78,21 +77,36 @@
 
 
 def first_reaches(level, surface, constants):
-    top, drive, friction, feed = constants
-    west_faces = [west_of(value) for value in (top, drive, friction)]
-    flux = first_face(level, east_of(level), top, drive)
-    west = first_face(west_of(level), level, west_faces[0], west_faces[1])
-    level, gathered = advanced(level, west, flux, surface, feed)
-
-    def substep(_, state):
-        level, west, flux, gathered = state
-        west = face(west, west_of(level), level, *west_faces)
-        flux = face(flux, level, east_of(level), top, drive, friction)
-        level, transfer = advanced(level, west, flux, surface, feed)
-        return level, west, flux, gathered + transfer
-
-    state = repeated(SUB - 1, FIRST_AT_ONCE, substep, (level, west, flux, gathered))
-    return state[0], state[2], state[3]
+    feed = constants[3]
+    faces = constants[:3]
+    far_east = [east_of(value) for value in faces]
+    near_west = [west_of(value) for value in faces]
+    far_west = [west_of(value) for value in near_west]
+    feeds = west_of(feed), feed, east_of(feed)
+    waters = west_of(surface), surface, east_of(surface)
+    west = flux = gathered = None
+    for pair in range(SUB // 2):
+        levels = [west_of(level), level, east_of(level)]
+        around = [pltpu.roll(level, 2, 1)] + levels + [pltpu.roll(level, level.shape[1] - 2, 1)]
+        if pair:
+            flows = [west_of(west), west, flux, east_of(flux)]
+        else:
+            flows = [None] * 4
+        sets = [far_west, near_west, faces, far_east]
+        for k in range(4):
+            if pair:
+                flows[k] = face(flows[k], around[k], around[k + 1], *sets[k])
+            else:
+                flows[k] = first_face(around[k], around[k + 1], *sets[k][:2])
+        for k in range(3):
+            levels[k], transfer = advanced(levels[k], flows[k], flows[k + 1], waters[k], feeds[k])
+            if k == 1:
+                gathered = transfer if gathered is None else gathered + transfer
+        west = face(flows[1], levels[0], levels[1], *near_west)
+        flux = face(flows[2], levels[1], levels[2], *faces)
+        level, transfer = advanced(levels[1], west, flux, surface, feed)
+        gathered = gathered + transfer
+    return level, flux, gathered
 
 
 def odd_position(axis):
@@ -301,7 +315,7 @@
     flat_ref, level_ref, bank_ref, listed_ref, a_ref, b_ref,
     depth_out, river_out, east_out, north_out,
     both_ref, state, gains,
-    flow_ref, fixed_ref, river_ref, list_rows, list_smem, sems,
+    flow_ref, fixed_ref, river_ref, list_rows, list_smem, depth_ref, sems, out_sems,
 ):
     rows, cols = depth_out.shape
     slots = rows // 4
@@ -520,9 +534,7 @@
             if final:
                 out = pl.ds(t - RIM, RIM)
                 new = own_ref[at, :] + moved + gains[0, at, :]
-                depth_out[out, :] = new - flat_ref[pl.ds(t + GROUND * ext, RIM), :]
-                east_out[out, :] = to_east[0]
-                north_out[out, :] = to_north
+                depth_ref[out, :] = new - flat_ref[pl.ds(t + GROUND * ext, RIM), :]
             elif j == 0:
                 own_ref[at, :] = own_ref[at, :] + moved + gains[0, at, :]
             else:
@@ -530,6 +542,13 @@
                 gain = jnp.where(low, gains[0, beside, :], gains[1, beside, :])
                 side_ref[at, :] = side_ref[at, :] + moved + gain
         return after
+
+    sent = []
+
+    def send(source, target):
+        copy = pltpu.make_async_copy(source, target, out_sems.at[len(sent)])
+        copy.start()
+        sent.append(copy)
 
     def update_all(step):
         if step == STEPS - 1:
@@ -540,6 +559,9 @@
             tiles = range(0, ext, RIM)
         for t in tiles:
             before = update(t, before, step)
+            if step == STEPS - 1 and t % (rows // 2) == 0:
+                done = pl.ds(t - rows // 2, rows // 2)
+                send(depth_ref.at[done, :], depth_out.at[done, :])
 
     def settle():
         river_ref[0:rows, :] = level_ref[0:rows, :]
@@ -553,7 +575,7 @@
             at = pl.ds(t, RIM)
             ground = flat_ref[pl.ds(t + (GROUND * ext + RIM), RIM), :]
             bed = ground - (1.0 + 0.5 * bank_ref[at, :].astype(jnp.float32))
-            river_out[at, :] = river_ref[at, :] - bed
+            river_ref[at, :] = river_ref[at, :] - bed
 
     for t in range(0, ext, RIM):
         constants_of(t)
@@ -573,10 +595,17 @@
                 flows(t, step)
         for reach in running:
             next(reach, None)
+        if final:
+            own_rows = pl.ds(RIM, rows)
+            send(flow_ref.at[0, 0, own_rows, :], east_out)
+            send(flow_ref.at[0, 1, own_rows, :], north_out)
         spread()
         if final:
             settle()
+            send(river_ref.at[pl.ds(0, rows), :], river_out)
         update_all(step)
+    for copy in sent:
+        copy.wait()
 
 
 def swaps(count, first):
@@ -655,7 +684,7 @@
     return pl.pallas_call(
         step_kernel,
         in_specs=[vmem] * 6,
-        out_specs=[vmem] * 4,
+        out_specs=[pl.BlockSpec(memory_space=pl.ANY)] * 4,
         out_shape=[tile] * 4,
         scratch_shapes=[
             pltpu.VMEM((ext + RIM + room, cols), f32),
@@ -666,6 +695,8 @@
             pltpu.VMEM((rows + RIM, cols), f32),
             pltpu.VMEM((5, RIM, cols), jnp.int32),
             pltpu.SMEM((5, cols), jnp.int32),
+            pltpu.VMEM((rows, cols), f32),
+            pltpu.SemaphoreType.DMA((5,)),
             pltpu.SemaphoreType.DMA((5,)),
         ],
         compiler_params=params,

time: 22.9 us -> 22.5 us (0.983)
  Pallas kernels: 10.7 us -> 10.3 us
where the time goes in v5:
time: 22.5 us; the launch traced here: 22.3 us
  Pallas kernels  10.3 us (46%)
  starting transfers between devices  6.6 us (29%)
  waiting for transfers between devices  4.58 us (20%)
  between operations  0.78 us (3%)
    pallas_call x1, Pallas kernels, body(): pl.pallas_call(step_kernel, in_specs=[vmem] * 6, out_specs=[pl.BlockSpec(...  5.93 us
    ppermute x1, waiting for transfers between devices, body(): got_b = lax.ppermute(to_b, 'lon', ring)  3.82 us
    ppermute x1, starting transfers between devices, body(): got_a = lax.ppermute(to_a, 'lon', swaps(lon_total, 0))  2.15 us
    pallas_call x1, Pallas kernels, body(): pl.pallas_call(own_kernel, in_specs=[pl.BlockSpec(memory_space=pl.ANY)] +...  2.06 us
    ppermute x1, starting transfers between devices, body(): got_q = lax.ppermute(to_q, 'lat', swaps(lat_total, 1))  1.91 us
    pallas_call x1, Pallas kernels, body(): pl.pallas_call(rows_kernel, in_specs=[hbm] * 7, out_specs=[vmem, vmem], o...  1.62 us
    ppermute x1, starting transfers between devices, body(): got_p = lax.ppermute(to_p, 'lat', swaps(lat_total, 0))  1.36 us
    ppermute x1, starting transfers between devices, body(): got_b = lax.ppermute(to_b, 'lon', ring)  1.17 us
  transfers between devices with their start and end apart: 4, of which 2 were waited for; matrix products, arithmetic and copies ran while one was open for 0% of the time, Pallas kernels for 9%

profile of v5, /device:TPU:19, one launch (start us, length us, event | category | flops | bytes accessed | tf_op | source)
XLA Modules:
  0.0 22.3 jit_solution(10183303886730595609)
XLA Ops:
  0.6 0.0 copy-start
  0.6 0.0 copy-start.1
  0.7 0.0 copy-start.2
  0.7 0.0 copy-start.3
  0.7 0.0 copy-start.4
  0.7 0.0 copy-start.5
  0.7 1.6 %rims.1 = (f32[56,128]{1,0:T(8,128)}, f32[56,128]{1,0:T(8,128)}) custom-call(s32[256]{0:T(256)} %bitcast.1, f32[256,128]{1,0:T(8,128)} %refs_0_.1, f32[256,128]{1,0:T(8,128)} %refs_1_.1, f32[256,128]{1,0:T(8,128)} %refs_2_.1, f32[256,128]{1,0:T(8,128)} %refs_3_.1, s32[256,128]{1,0:T(8,128)} %refs_4_.1, s32[256,128]{1,0:T(8,128)} %bank_ref.3), custom_call_target="tpu_custom_call" | custom-call | tf_op jit(solution)/shard_map/rims/pallas_call | solution.py:633
  2.3 0.0 copy-start.6
  2.3 1.4 %collective-permute-start = (f32[56,128]{1,0:T(8,128)}, f32[56,128]{1,0:T(8,128)S(1)}, u32[]{:S(2)}, u32[]{:S(2)}) collective-permute-start(f32[56,128]{1,0:T(8,128)} %get-tuple-element.14), channel_id=1, source_target_pairs={{0,1},{2,3},{1,0},{3,2},{4,5},{6,7},{5,4},{7,6},{8,9},{10,11},{9,8... | collective-permute-start | bytes 86024 | tf_op jit(solution)/shard_map/ppermute | solution.py:647
  3.7 1.9 %collective-permute-start.1 = (f32[56,128]{1,0:T(8,128)}, f32[56,128]{1,0:T(8,128)S(1)}, u32[]{:S(2)}, u32[]{:S(2)}) collective-permute-start(f32[56,128]{1,0:T(8,128)} %get-tuple-element.15), channel_id=1, source_target_pairs={{1,2},{2,1},{5,6},{6,5},{9,10},{10,9},{13,14},{14,13},{17,18},{18,... | collective-permute-start | bytes 86024 | tf_op jit(solution)/shard_map/ppermute | solution.py:648
  5.6 0.0 copy-done
  5.6 0.0 copy-done.1
  5.6 0.0 copy-done.2
  5.6 0.0 copy-done.3
  5.7 0.0 copy-done.4
  5.7 2.1 %own_reaches.1 = (f32[1216,128]{1,0:T(8,128)S(1)}, f32[264,128]{1,0:T(8,128)S(1)}, f32[8,128]{1,0:T(8,128)S(1)}) custom-call(s32[256]{0:T(256)S(1)} %bitcast.2, f32[256,128]{1,0:T(8,128)S(1)} %copy-done.1, f32[256,128]{1,0:T(8,128)S(1)} %copy-done.2, f32[256,128]{1,0:T(8,128)S(1)} %copy-done.3, f32[256,128]{1,0:T(8,128)S(1)} %copy-done.4, ...), custom_call_target="tpu_custom_call" | custom-call | tf_op jit(solution)/shard_map/own_reaches/pallas_call | solution.py:650
  7.7 0.0 collective-permute-done.p_ref
  7.8 0.8 %collective-permute-done.1.q_ref = f32[56,128]{1,0:T(8,128)S(1)} collective-permute-done((f32[56,128]{1,0:T(8,128)}, f32[56,128]{1,0:T(8,128)S(1)}, u32[]{:S(2)}, u32[]{:S(2)}) %collective-permute-start.1) | collective-permute-done | bytes 28704 | tf_op jit(solution)/shard_map/ppermute | solution.py:648
  8.5 0.7 %pack.1 = (f32[1216,128]{1,0:T(8,128)S(1)}, f32[152,128]{1,0:T(8,128)S(1)}, f32[152,128]{1,0:T(8,128)S(1)}) custom-call(f32[1216,128]{1,0:T(8,128)S(1)} %get-tuple-element.12.own_flat, f32[8,128]{1,0:T(8,128)S(1)} %get-tuple-element.13.listed_ref, f32[56,128]{1,0:T(8,128)S(1)} %collective-permute-done.p_ref, ...), custom_call_target="tpu_custom_call", output_to_operand_aliasing={{0}: (0, {})} | custom-call | tf_op jit(solution)/shard_map/pack/pallas_call | solution.py:670
  9.2 2.2 %collective-permute-start.2 = (f32[152,128]{1,0:T(8,128)S(1)}, f32[152,128]{1,0:T(8,128)S(1)}, u32[]{:S(2)}, u32[]{:S(2)}) collective-permute-start(f32[152,128]{1,0:T(8,128)S(1)} %get-tuple-element.18), channel_id=1, source_target_pairs={{0,4},{8,12},{16,20},{24,28},{4,0},{12,8},{20,16},{28,24},{1,5},{9... | collective-permute-start | bytes 233480 | tf_op jit(solution)/shard_map/ppermute | solution.py:680
  11.4 1.2 %collective-permute-start.3 = (f32[152,128]{1,0:T(8,128)S(1)}, f32[152,128]{1,0:T(8,128)S(1)}, u32[]{:S(2)}, u32[]{:S(2)}) collective-permute-start(f32[152,128]{1,0:T(8,128)S(1)} %get-tuple-element.19), channel_id=1, source_target_pairs={{4,8},{12,16},{20,24},{8,4},{16,12},{24,20},{28,0},{0,28},{5,9},{1... | collective-permute-start | bytes 233480 | tf_op jit(solution)/shard_map/ppermute | solution.py:681
  12.6 0.0 collective-permute-done.2.a_ref
  12.6 3.8 %collective-permute-done.3.b_ref = f32[152,128]{1,0:T(8,128)S(1)} collective-permute-done((f32[152,128]{1,0:T(8,128)S(1)}, f32[152,128]{1,0:T(8,128)S(1)}, u32[]{:S(2)}, u32[]{:S(2)}) %collective-permute-start.3) | collective-permute-done | bytes 77856 | tf_op jit(solution)/shard_map/ppermute | solution.py:681
  16.4 5.9 %steps.1 = (f32[256,128]{1,0:T(8,128)}, f32[256,128]{1,0:T(8,128)}, f32[256,128]{1,0:T(8,128)}, f32[256,128]{1,0:T(8,128)}) custom-call(f32[1216,128]{1,0:T(8,128)S(1)} %get-tuple-element.16.flat_ref, f32[264,128]{1,0:T(8,128)S(1)} %get-tuple-element.17.level_ref, s32[256,128]{1,0:T(8,128)S(1)} %copy-done, f32[8,128]{1,0:T(8,128)S(1)} %get-tuple-element.13.listed_ref, ...), custom_call_target="tpu_custom_call" | custom-call | tf_op jit(solution)/shard_map/steps/pallas_call | solution.py:684
  (2 shorter events, 0.0 us)
Async XLA Ops:
  0.6 5.0 %copy-start = (s32[256,128]{1,0:T(8,128)S(1)}, s32[256,128]{1,0:T(8,128)}, u32[]{:S(2)}) copy-start(s32[256,128]{1,0:T(8,128)} %bank_ref.3) | copy-start | bytes 393220
  0.6 5.0 %copy-start.1 = (f32[256,128]{1,0:T(8,128)S(1)}, f32[256,128]{1,0:T(8,128)}, u32[]{:S(2)}) copy-start(f32[256,128]{1,0:T(8,128)} %refs_0_.1) | copy-start | bytes 393220
  0.7 5.0 %copy-start.2 = (f32[256,128]{1,0:T(8,128)S(1)}, f32[256,128]{1,0:T(8,128)}, u32[]{:S(2)}) copy-start(f32[256,128]{1,0:T(8,128)} %refs_1_.1) | copy-start | bytes 393220
  0.7 5.0 %copy-start.3 = (f32[256,128]{1,0:T(8,128)S(1)}, f32[256,128]{1,0:T(8,128)}, u32[]{:S(2)}) copy-start(f32[256,128]{1,0:T(8,128)} %refs_2_.1) | copy-start | bytes 393220
  0.7 5.0 %copy-start.4 = (f32[256,128]{1,0:T(8,128)S(1)}, f32[256,128]{1,0:T(8,128)}, u32[]{:S(2)}) copy-start(f32[256,128]{1,0:T(8,128)} %refs_3_.1) | copy-start | bytes 393220
  0.7 5.0 %copy-start.5 = (s32[256,128]{1,0:T(8,128)S(1)}, s32[256,128]{1,0:T(8,128)}, u32[]{:S(2)}) copy-start(s32[256,128]{1,0:T(8,128)} %refs_4_.1) | copy-start | bytes 393220
  2.3 3.4 %copy-start.6 = (s32[256,1]{0,1:T(1,128)S(1)}, s32[256,1]{0,1:T(1,128)}, u32[]{:S(2)}) copy-start(s32[256,1]{0,1:T(1,128)} %param.11) | copy-start | bytes 3076
  2.3 5.4 %collective-permute-start = (f32[56,128]{1,0:T(8,128)}, f32[56,128]{1,0:T(8,128)S(1)}, u32[]{:S(2)}, u32[]{:S(2)}) collective-permute-start(f32[56,128]{1,0:T(8,128)} %get-tuple-element.14), channel_id=1, source_target_pairs={{0,1},{2,3},{1,0},{3,2},{4,5},{6,7},{5,4},{7,6},{8,9},{10,11},{9,8... | collective-permute-start | bytes 86024 | tf_op jit(solution)/shard_map/ppermute | solution.py:647
  3.7 4.8 %collective-permute-start.1 = (f32[56,128]{1,0:T(8,128)}, f32[56,128]{1,0:T(8,128)S(1)}, u32[]{:S(2)}, u32[]{:S(2)}) collective-permute-start(f32[56,128]{1,0:T(8,128)} %get-tuple-element.15), channel_id=1, source_target_pairs={{1,2},{2,1},{5,6},{6,5},{9,10},{10,9},{13,14},{14,13},{17,18},{18,... | collective-permute-start | bytes 86024 | tf_op jit(solution)/shard_map/ppermute | solution.py:648
  9.2 3.3 %collective-permute-start.2 = (f32[152,128]{1,0:T(8,128)S(1)}, f32[152,128]{1,0:T(8,128)S(1)}, u32[]{:S(2)}, u32[]{:S(2)}) collective-permute-start(f32[152,128]{1,0:T(8,128)S(1)} %get-tuple-element.18), channel_id=1, source_target_pairs={{0,4},{8,12},{16,20},{24,28},{4,0},{12,8},{20,16},{28,24},{1,5},{9... | collective-permute-start | bytes 233480 | tf_op jit(solution)/shard_map/ppermute | solution.py:680
  11.4 5.0 %collective-permute-start.3 = (f32[152,128]{1,0:T(8,128)S(1)}, f32[152,128]{1,0:T(8,128)S(1)}, u32[]{:S(2)}, u32[]{:S(2)}) collective-permute-start(f32[152,128]{1,0:T(8,128)S(1)} %get-tuple-element.19), channel_id=1, source_target_pairs={{4,8},{12,16},{20,24},{8,4},{16,12},{24,20},{28,0},{0,28},{5,9},{1... | collective-permute-start | bytes 233480 | tf_op jit(solution)/shard_map/ppermute | solution.py:681

commit v6 on v5

--- a/solution.py
+++ b/solution.py
@@ -293,19 +293,18 @@
     group = lanes((RIM, cols)) // COLS
     eastern = odd_position("lon") == 0
     tiles = (base + SLOT_FIELDS * total) // RIM + 1
-    turns = []
-    for start in (jnp.where(eastern, cols - COLS, 0), jnp.where(eastern, 0, cols - COLS)):
-        turns.append([lax.rem(cols + COLS * g - start, cols) for g in range(groups)])
+    listed = listed_ref[...]
 
     def pack(m, used):
-        block_a = block_b = listed_ref[...]
+        block_west, block_east = listed, pltpu.roll(listed, cols - COLS, 1)
         for g in range(used):
             source = flat_ref[pl.ds(row_of(m * groups + g), RIM), :]
-            block_a = jnp.where(group == g, pltpu.roll(source, turns[0][g], 1), block_a)
-            block_b = jnp.where(group == g, pltpu.roll(source, turns[1][g], 1), block_b)
+            moved = pltpu.roll(source, COLS * g, 1) if g else source
+            block_west = jnp.where(group == g, moved, block_west)
+            block_east = jnp.where(group == (g - 1) % groups, moved, block_east)
         to = pl.ds(row_of(m), RIM)
-        a_ref[to, :] = block_a
-        b_ref[to, :] = block_b
+        a_ref[to, :] = jnp.where(eastern, block_east, block_west)
+        b_ref[to, :] = jnp.where(eastern, block_west, block_east)
 
     each_row(tiles // groups, lambda m: pack(m, groups), UNPACK_AT_ONCE)
     pack(tiles // groups, tiles % groups)
@@ -336,7 +335,7 @@
     crowded = jnp.broadcast_to(own_list[:, 0:1], own_list.shape) > few + 0.5
     list_a, list_b = a_ref[lists : lists + RIM, :], b_ref[lists : lists + RIM, :]
     east_list = jnp.where(eastern, list_a, list_b) + apart
-    west_list = jnp.where(eastern, list_b, list_a) + apart
+    west_list = pltpu.roll(jnp.where(eastern, list_b, list_a), COLS, 1) + apart
     copies = []
     for k, rows_of in enumerate((
         jnp.where(crowded, own_list, east_list), jnp.where(crowded, own_list, west_list),
@@ -350,19 +349,17 @@
     groups = cols // COLS
     lane = lanes((RIM, cols))
     low = lane < cols // 2
-    use_a = low == eastern
-    turns = []
-    for to in (jnp.where(eastern, 0, cols - COLS), jnp.where(eastern, cols - COLS, 0)):
-        turns.append([lax.rem(cols + to - COLS * g, cols) for g in range(groups)])
+    group = lane // COLS
 
     def unpack(m):
         at = pl.ds(row_of(m), RIM)
         block_a, block_b = a_ref[at, :], b_ref[at, :]
+        from_east = jnp.where(eastern, block_a, block_b)
+        from_west = jnp.where(eastern, block_b, block_a)
         for g in range(groups):
-            from_a = pltpu.roll(block_a, turns[0][g], 1)
-            from_b = pltpu.roll(block_b, turns[1][g], 1)
+            both = jnp.where(group == g, from_east, from_west)
             to = pl.ds(row_of(m * groups + g), RIM)
-            side_ref[to, :] = jnp.where(use_a, from_a, from_b)
+            side_ref[to, :] = pltpu.roll(both, cols - COLS * g, 1) if g else both
 
     each_row(a_ref.shape[0] // RIM, unpack, UNPACK_AT_ONCE)
 

time: 22.5 us -> 22.3 us (level)
  no operation moved by 1% of the time
where the time goes in v6:
time: 22.3 us; the launch traced here: 22.2 us
  Pallas kernels  10.2 us (46%)
  starting transfers between devices  6.6 us (30%)
  waiting for transfers between devices  4.58 us (21%)
  between operations  0.78 us (3%)
    pallas_call x1, Pallas kernels, body(): pl.pallas_call(step_kernel, in_specs=[vmem] * 6, out_specs=[pl.BlockSpec(...  5.75 us
    ppermute x1, waiting for transfers between devices, body(): got_b = lax.ppermute(to_b, 'lon', ring)  3.82 us
    ppermute x1, starting transfers between devices, body(): got_a = lax.ppermute(to_a, 'lon', swaps(lon_total, 0))  2.16 us
    pallas_call x1, Pallas kernels, body(): pl.pallas_call(own_kernel, in_specs=[pl.BlockSpec(memory_space=pl.ANY)] +...  2.06 us
    ppermute x1, starting transfers between devices, body(): got_q = lax.ppermute(to_q, 'lat', swaps(lat_total, 1))  1.91 us
    pallas_call x1, Pallas kernels, body(): pl.pallas_call(rows_kernel, in_specs=[hbm] * 7, out_specs=[vmem, vmem], o...  1.62 us
    ppermute x1, starting transfers between devices, body(): got_p = lax.ppermute(to_p, 'lat', swaps(lat_total, 0))  1.36 us
    ppermute x1, starting transfers between devices, body(): got_b = lax.ppermute(to_b, 'lon', ring)  1.17 us
  transfers between devices with their start and end apart: 4, of which 2 were waited for; matrix products, arithmetic and copies ran while one was open for 0% of the time, Pallas kernels for 9%

profile of v6, /device:TPU:19, one launch (start us, length us, event | category | flops | bytes accessed | tf_op | source)
XLA Modules:
  0.0 22.2 jit_solution(9746954536298124799)
XLA Ops:
  0.6 0.0 copy-start
  0.6 0.0 copy-start.1
  0.7 0.0 copy-start.2
  0.7 0.0 copy-start.3
  0.7 0.0 copy-start.4
  0.7 0.0 copy-start.5
  0.7 1.6 %rims.1 = (f32[56,128]{1,0:T(8,128)}, f32[56,128]{1,0:T(8,128)}) custom-call(s32[256]{0:T(256)} %bitcast.1, f32[256,128]{1,0:T(8,128)} %refs_0_.1, f32[256,128]{1,0:T(8,128)} %refs_1_.1, f32[256,128]{1,0:T(8,128)} %refs_2_.1, f32[256,128]{1,0:T(8,128)} %refs_3_.1, s32[256,128]{1,0:T(8,128)} %refs_4_.1, s32[256,128]{1,0:T(8,128)} %bank_ref.3), custom_call_target="tpu_custom_call" | custom-call | tf_op jit(solution)/shard_map/rims/pallas_call | solution.py:630
  2.3 0.0 copy-start.6
  2.3 1.4 %collective-permute-start = (f32[56,128]{1,0:T(8,128)}, f32[56,128]{1,0:T(8,128)S(1)}, u32[]{:S(2)}, u32[]{:S(2)}) collective-permute-start(f32[56,128]{1,0:T(8,128)} %get-tuple-element.14), channel_id=1, source_target_pairs={{0,1},{2,3},{1,0},{3,2},{4,5},{6,7},{5,4},{7,6},{8,9},{10,11},{9,8... | collective-permute-start | bytes 86024 | tf_op jit(solution)/shard_map/ppermute | solution.py:644
  3.7 1.9 %collective-permute-start.1 = (f32[56,128]{1,0:T(8,128)}, f32[56,128]{1,0:T(8,128)S(1)}, u32[]{:S(2)}, u32[]{:S(2)}) collective-permute-start(f32[56,128]{1,0:T(8,128)} %get-tuple-element.15), channel_id=1, source_target_pairs={{1,2},{2,1},{5,6},{6,5},{9,10},{10,9},{13,14},{14,13},{17,18},{18,... | collective-permute-start | bytes 86024 | tf_op jit(solution)/shard_map/ppermute | solution.py:645
  5.6 0.0 copy-done
  5.6 0.0 copy-done.1
  5.6 0.0 copy-done.2
  5.6 0.0 copy-done.3
  5.7 0.0 copy-done.4
  5.7 2.1 %own_reaches.1 = (f32[1216,128]{1,0:T(8,128)S(1)}, f32[264,128]{1,0:T(8,128)S(1)}, f32[8,128]{1,0:T(8,128)S(1)}) custom-call(s32[256]{0:T(256)S(1)} %bitcast.2, f32[256,128]{1,0:T(8,128)S(1)} %copy-done.1, f32[256,128]{1,0:T(8,128)S(1)} %copy-done.2, f32[256,128]{1,0:T(8,128)S(1)} %copy-done.3, f32[256,128]{1,0:T(8,128)S(1)} %copy-done.4, ...), custom_call_target="tpu_custom_call" | custom-call | tf_op jit(solution)/shard_map/own_reaches/pallas_call | solution.py:647
  7.7 0.0 collective-permute-done.p_ref
  7.8 0.8 %collective-permute-done.1.q_ref = f32[56,128]{1,0:T(8,128)S(1)} collective-permute-done((f32[56,128]{1,0:T(8,128)}, f32[56,128]{1,0:T(8,128)S(1)}, u32[]{:S(2)}, u32[]{:S(2)}) %collective-permute-start.1) | collective-permute-done | bytes 28704 | tf_op jit(solution)/shard_map/ppermute | solution.py:645
  8.5 0.7 %pack.1 = (f32[1216,128]{1,0:T(8,128)S(1)}, f32[152,128]{1,0:T(8,128)S(1)}, f32[152,128]{1,0:T(8,128)S(1)}) custom-call(f32[1216,128]{1,0:T(8,128)S(1)} %get-tuple-element.12.own_flat, f32[8,128]{1,0:T(8,128)S(1)} %get-tuple-element.13.listed_ref, f32[56,128]{1,0:T(8,128)S(1)} %collective-permute-done.p_ref, ...), custom_call_target="tpu_custom_call", output_to_operand_aliasing={{0}: (0, {})} | custom-call | tf_op jit(solution)/shard_map/pack/pallas_call | solution.py:667
  9.2 2.2 %collective-permute-start.2 = (f32[152,128]{1,0:T(8,128)S(1)}, f32[152,128]{1,0:T(8,128)S(1)}, u32[]{:S(2)}, u32[]{:S(2)}) collective-permute-start(f32[152,128]{1,0:T(8,128)S(1)} %get-tuple-element.18), channel_id=1, source_target_pairs={{0,4},{8,12},{16,20},{24,28},{4,0},{12,8},{20,16},{28,24},{1,5},{9... | collective-permute-start | bytes 233480 | tf_op jit(solution)/shard_map/ppermute | solution.py:677
  11.4 1.2 %collective-permute-start.3 = (f32[152,128]{1,0:T(8,128)S(1)}, f32[152,128]{1,0:T(8,128)S(1)}, u32[]{:S(2)}, u32[]{:S(2)}) collective-permute-start(f32[152,128]{1,0:T(8,128)S(1)} %get-tuple-element.19), channel_id=1, source_target_pairs={{4,8},{12,16},{20,24},{8,4},{16,12},{24,20},{28,0},{0,28},{5,9},{1... | collective-permute-start | bytes 233480 | tf_op jit(solution)/shard_map/ppermute | solution.py:678
  12.6 0.0 collective-permute-done.2.a_ref
  12.6 3.8 %collective-permute-done.3.b_ref = f32[152,128]{1,0:T(8,128)S(1)} collective-permute-done((f32[152,128]{1,0:T(8,128)S(1)}, f32[152,128]{1,0:T(8,128)S(1)}, u32[]{:S(2)}, u32[]{:S(2)}) %collective-permute-start.3) | collective-permute-done | bytes 77856 | tf_op jit(solution)/shard_map/ppermute | solution.py:678
  16.4 5.8 %steps.1 = (f32[256,128]{1,0:T(8,128)}, f32[256,128]{1,0:T(8,128)}, f32[256,128]{1,0:T(8,128)}, f32[256,128]{1,0:T(8,128)}) custom-call(f32[1216,128]{1,0:T(8,128)S(1)} %get-tuple-element.16.flat_ref, f32[264,128]{1,0:T(8,128)S(1)} %get-tuple-element.17.level_ref, s32[256,128]{1,0:T(8,128)S(1)} %copy-done, f32[8,128]{1,0:T(8,128)S(1)} %get-tuple-element.13.listed_ref, ...), custom_call_target="tpu_custom_call" | custom-call | tf_op jit(solution)/shard_map/steps/pallas_call | solution.py:681
  (2 shorter events, 0.0 us)
Async XLA Ops:
  0.6 5.0 %copy-start = (s32[256,128]{1,0:T(8,128)S(1)}, s32[256,128]{1,0:T(8,128)}, u32[]{:S(2)}) copy-start(s32[256,128]{1,0:T(8,128)} %bank_ref.3) | copy-start | bytes 393220
  0.6 5.0 %copy-start.1 = (f32[256,128]{1,0:T(8,128)S(1)}, f32[256,128]{1,0:T(8,128)}, u32[]{:S(2)}) copy-start(f32[256,128]{1,0:T(8,128)} %refs_0_.1) | copy-start | bytes 393220
  0.7 5.0 %copy-start.2 = (f32[256,128]{1,0:T(8,128)S(1)}, f32[256,128]{1,0:T(8,128)}, u32[]{:S(2)}) copy-start(f32[256,128]{1,0:T(8,128)} %refs_1_.1) | copy-start | bytes 393220
  0.7 5.0 %copy-start.3 = (f32[256,128]{1,0:T(8,128)S(1)}, f32[256,128]{1,0:T(8,128)}, u32[]{:S(2)}) copy-start(f32[256,128]{1,0:T(8,128)} %refs_2_.1) | copy-start | bytes 393220
  0.7 5.0 %copy-start.4 = (f32[256,128]{1,0:T(8,128)S(1)}, f32[256,128]{1,0:T(8,128)}, u32[]{:S(2)}) copy-start(f32[256,128]{1,0:T(8,128)} %refs_3_.1) | copy-start | bytes 393220
  0.7 5.0 %copy-start.5 = (s32[256,128]{1,0:T(8,128)S(1)}, s32[256,128]{1,0:T(8,128)}, u32[]{:S(2)}) copy-start(s32[256,128]{1,0:T(8,128)} %refs_4_.1) | copy-start | bytes 393220
  2.3 3.4 %copy-start.6 = (s32[256,1]{0,1:T(1,128)S(1)}, s32[256,1]{0,1:T(1,128)}, u32[]{:S(2)}) copy-start(s32[256,1]{0,1:T(1,128)} %param.11) | copy-start | bytes 3076
  2.3 5.4 %collective-permute-start = (f32[56,128]{1,0:T(8,128)}, f32[56,128]{1,0:T(8,128)S(1)}, u32[]{:S(2)}, u32[]{:S(2)}) collective-permute-start(f32[56,128]{1,0:T(8,128)} %get-tuple-element.14), channel_id=1, source_target_pairs={{0,1},{2,3},{1,0},{3,2},{4,5},{6,7},{5,4},{7,6},{8,9},{10,11},{9,8... | collective-permute-start | bytes 86024 | tf_op jit(solution)/shard_map/ppermute | solution.py:644
  3.7 4.8 %collective-permute-start.1 = (f32[56,128]{1,0:T(8,128)}, f32[56,128]{1,0:T(8,128)S(1)}, u32[]{:S(2)}, u32[]{:S(2)}) collective-permute-start(f32[56,128]{1,0:T(8,128)} %get-tuple-element.15), channel_id=1, source_target_pairs={{1,2},{2,1},{5,6},{6,5},{9,10},{10,9},{13,14},{14,13},{17,18},{18,... | collective-permute-start | bytes 86024 | tf_op jit(solution)/shard_map/ppermute | solution.py:645
  9.2 3.3 %collective-permute-start.2 = (f32[152,128]{1,0:T(8,128)S(1)}, f32[152,128]{1,0:T(8,128)S(1)}, u32[]{:S(2)}, u32[]{:S(2)}) collective-permute-start(f32[152,128]{1,0:T(8,128)S(1)} %get-tuple-element.18), channel_id=1, source_target_pairs={{0,4},{8,12},{16,20},{24,28},{4,0},{12,8},{20,16},{28,24},{1,5},{9... | collective-permute-start | bytes 233480 | tf_op jit(solution)/shard_map/ppermute | solution.py:677
  11.4 5.0 %collective-permute-start.3 = (f32[152,128]{1,0:T(8,128)S(1)}, f32[152,128]{1,0:T(8,128)S(1)}, u32[]{:S(2)}, u32[]{:S(2)}) collective-permute-start(f32[152,128]{1,0:T(8,128)S(1)} %get-tuple-element.19), channel_id=1, source_target_pairs={{4,8},{12,16},{20,24},{8,4},{16,12},{24,20},{28,0},{0,28},{5,9},{1... | collective-permute-start | bytes 233480 | tf_op jit(solution)/shard_map/ppermute | solution.py:678
